TPU v7x, 32 devices: a whole 2x2x4 slice. The times are simulated.
32 devices in a mesh: grp: 2 (over y), slab: 4 (over z), dom: 2 (over x), shot: 2 (over core).
Axes of the slice: x: 2, y: 2, z: 4, core: 2. Of those that a mesh axis runs over, the one named last changes fastest.
Arguments:
- particles: float32 [32, 16, 8, 128], P(('grp', 'dom'), 'slab'), parts along dimension 0, may hold values from -1.5 to 1.5
- background: float32 [32, 8, 128], P(('grp', 'slab')), parts along dimension 0, may hold values from 0.02 to 0.08
- wave_prev: bfloat16 [32, 2, 16, 8, 128], P(('grp', 'dom'), 'shot', 'slab'), parts along dimension 0, may hold values from -6 to 6
- wave_now: bfloat16 [32, 2, 16, 8, 128], P(('grp', 'dom'), 'shot', 'slab'), parts along dimension 0, may hold values from -6 to 6
- adjoint_near: bfloat16 [32, 2, 16, 8, 128], P(('grp', 'dom'), 'shot', 'slab'), parts along dimension 0, may hold values from -6 to 6
- adjoint_far: bfloat16 [32, 2, 16, 8, 128], P(('grp', 'dom'), 'shot', 'slab'), parts along dimension 0, may hold values from -6 to 6
- sources: int32 [4], P(('grp', 'shot')), parts along dimension 0, may hold values from 0 to 16383
- wavelet: float32 [4, 2], P(('grp', 'shot')), parts along dimension 0, may hold values from -16 to 16
- receivers: int32 [4, 128], P(('grp', 'shot')), parts along dimension 0, may hold values from 0 to 16383
- observed: float32 [4, 2, 128], P(('grp', 'shot')), parts along dimension 0, may hold values from -12 to 12
Outputs:
- update: float32 [32, 16, 8, 128], P(('grp', 'dom'), 'slab'), parts along dimension 0
There are 2 independent parts, one for each index of `grp`. A program takes and returns all parts, laid end to end along the dimension named above; each array names one. Nothing has to cross between parts.
Inputs may be any that keep to these rules, and one draw needn't show every extreme that they name: `sources`: the flat index (z * 8 + x) * 128 + y of each shot's source cell. `receivers`: flat indices of the receiver cells; cells may repeat.
All inputs are finite; a program needn't handle non-finite values.
Results may differ from a plain program's by a relative error of at most 0.0003.
Values sent between devices are 32-bit elements; how exact they have to be, the bound alone decides.
No kernel may reach another device: no remote copies, remote signals or barrier semaphores. Data moves between devices by JAX's collectives and lax.ppermute only.
A program may use at most 64 MiB of HBM per device.

v0:
```python
import math

import jax
import jax.numpy as jnp
from jax import lax
from jax.sharding import PartitionSpec as P

DATA_WEIGHT = 0.5
PRIOR_WEIGHT = 4.0
REPEL_WEIGHT = 4.0
STENCIL_WEIGHTS = (-205.0 / 72.0, 8.0 / 5.0, -1.0 / 5.0, 8.0 / 315.0, -1.0 / 560.0)


def extended_2(cells, sides, width):
    for axis, dim in sides:
        count = lax.axis_size(axis)
        ends = count - 1
        head = lax.slice_in_dim(cells, 0, width, axis=dim)
        tail = lax.slice_in_dim(cells, cells.shape[dim] - width, cells.shape[dim], axis=dim)
        cells = jnp.concatenate(
            [
                lax.ppermute(tail, axis, [(i, (i + 1) % count) for i in range(ends)]),
                cells,
                lax.ppermute(head, axis, [((i + 1) % count, i) for i in range(ends)]),
            ],
            axis=dim,
        )
    return cells


def laplace(padded, layers, row_count, column_count):

    def window(along_z, along_x, along_y):
        return padded[
            ...,
            4 + along_z : 4 + along_z + layers,
            4 + along_x : 4 + along_x + row_count,
            4 + along_y : 4 + along_y + column_count,
        ]

    result = 3.0 * STENCIL_WEIGHTS[0] * window(0, 0, 0)
    for offset in range(1, 5):
        beside = window(offset, 0, 0) + window(-offset, 0, 0) + window(0, offset, 0)
        beside = beside + window(0, -offset, 0) + window(0, 0, offset) + window(0, 0, -offset)
        result = result + STENCIL_WEIGHTS[offset] * beside
    return result


def rim_laplace(field):
    extended = extended_2(field, (("slab", 2),), 4)
    padded = jnp.pad(extended, [(0, 0), (0, 0), (0, 0), (4, 4), (4, 4)])
    return laplace(padded, field.shape[2], field.shape[3], field.shape[4])


def kernel_from_gram(gram_matrix):
    diagonal = jnp.diagonal(gram_matrix)
    distance = diagonal[:, None] + diagonal[None, :] - 2.0 * gram_matrix
    particle_count = gram_matrix.shape[0]
    kernel_width = jnp.sum(distance) / (
        particle_count * (particle_count - 1) * math.log(particle_count)
    )
    return jnp.exp(-distance / kernel_width)


def kernel_matrix(all_models):
    partial_gram = jnp.dot(
        all_models,
        all_models.T,
        precision=lax.Precision.HIGHEST,
        preferred_element_type=jnp.float32,
    )
    gram_matrix = lax.psum(partial_gram, "slab")
    return kernel_from_gram(gram_matrix)


def local(
    particles,
    background,
    wave_prev,
    wave_now,
    adjoint_near,
    adjoint_far,
    sources,
    wavelet,
    receivers,
    observed,
):
    group_size, shot_count, layers, row_count, column_count = wave_now.shape
    local_cells = layers * row_count * column_count
    first_cell = lax.axis_index("slab") * local_cells
    squared = background[None] * jnp.exp(particles)
    squared_wide = squared[:, None]
    cell_index = first_cell + jnp.arange(local_cells, dtype=jnp.int32).reshape(
        layers, row_count, column_count
    )
    source_mask = (cell_index[None] == sources[:, None, None, None]).astype(jnp.float32)
    local_index = receivers - first_cell
    inside = (local_index >= 0) & (local_index < local_cells)
    clipped = jnp.clip(local_index, 0, local_cells - 1)
    shot_rows = jnp.arange(shot_count, dtype=jnp.int32)[:, None]

    def record(field, column):
        picked = field.reshape(group_size, shot_count, local_cells)[:, shot_rows, clipped]
        return jnp.where(inside[None], picked - observed[None, :, column], 0.0)

    def inject(misfit):
        placed = (
            jnp.zeros((group_size, shot_count, local_cells), jnp.float32)
            .at[:, shot_rows, clipped]
            .add(misfit)
        )
        return placed.reshape(wave_now.shape)

    wave_zero = wave_prev.astype(jnp.float32)
    wave_one = wave_now.astype(jnp.float32)
    laplace_one = rim_laplace(wave_one)
    wave_two = (
        2.0 * wave_one
        - wave_zero
        + squared_wide * laplace_one
        + wavelet[:, 0, None, None, None] * source_mask
    )
    laplace_two = rim_laplace(wave_two)
    wave_three = (
        2.0 * wave_two
        - wave_one
        + squared_wide * laplace_two
        + wavelet[:, 1, None, None, None] * source_mask
    )
    misfit_two = record(wave_two, 0)
    misfit_three = record(wave_three, 1)
    adjoint_four = adjoint_near.astype(jnp.float32)
    adjoint_five = adjoint_far.astype(jnp.float32)
    adjoint_three = (
        2.0 * adjoint_four
        - adjoint_five
        + rim_laplace(squared_wide * adjoint_four)
        - inject(misfit_three)
    )
    adjoint_two = (
        2.0 * adjoint_three
        - adjoint_four
        + rim_laplace(squared_wide * adjoint_three)
        - inject(misfit_two)
    )
    correlation = jnp.sum(adjoint_two * laplace_one + adjoint_three * laplace_two, axis=1)
    summed = lax.psum(correlation, "shot")
    scores = DATA_WEIGHT * squared * summed - PRIOR_WEIGHT * particles
    flat_models = particles.reshape(group_size, -1)
    flat_scores = scores.reshape(group_size, -1)
    group_start = lax.axis_index("dom") * group_size
    all_models, all_scores = (
        lax.all_gather(flat_models, "dom", axis=0, tiled=True),
        lax.all_gather(flat_scores, "dom", axis=0, tiled=True),
    )
    kernel = kernel_matrix(all_models)
    kernel_rows = lax.dynamic_slice_in_dim(kernel, group_start, group_size, 0)
    pulled = jnp.dot(
        kernel_rows, all_scores, precision=lax.Precision.HIGHEST, preferred_element_type=jnp.float32
    )
    weight = jnp.sum(kernel_rows, axis=1)
    centred = jnp.dot(
        kernel_rows, all_models, precision=lax.Precision.HIGHEST, preferred_element_type=jnp.float32
    )
    update = (pulled + REPEL_WEIGHT * (flat_models * weight[:, None] - centred)) / weight[:, None]
    update = update.reshape(particles.shape)
    return update


def solution(mesh):
    placed = (
        P(("grp", "dom"), "slab", None, None),
        P(("grp", "slab"), None, None),
        P(("grp", "dom"), "shot", "slab", None, None),
        P(("grp", "dom"), "shot", "slab", None, None),
        P(("grp", "dom"), "shot", "slab", None, None),
        P(("grp", "dom"), "shot", "slab", None, None),
        P(("grp", "shot")),
        P(("grp", "shot"), None),
        P(("grp", "shot"), None),
        P(("grp", "shot"), None, None),
    )
    return jax.shard_map(
        local,
        mesh=mesh,
        in_specs=placed,
        out_specs=P(("grp", "dom"), "slab", None, None),
        check_vma=False,
    )
```

profile of v0, /device:TPU:0, one launch (start us, length us, event | category | flops | bytes accessed | tf_op | source)
XLA Modules:
  0.0 115.5 jit_solution(17733140582507449341)
XLA Ops:
  6.5 0.0 copy-start.1
  6.5 0.0 copy-start
  6.5 0.0 copy-start.3
  6.5 0.0 copy-start.4
  6.5 0.0 all-reduce.7.cloned.1.call-start
  6.6 0.9 bitcast_convert_fusion
  7.5 1.3 %collective-permute-start.2 = (f32[8,1,4,8,128]{4,3,2,0,1:T(8,128)S(1)}, f32[8,1,4,8,128]{4,3,2,0,1:T(8,128)S(1)}, u32[]{:S(2)}, u32[]{:S(2)}) collective-permute-start(f32[8,1,4,8,128]{4,3,2,0,1:T(8,128)S(1)} %bitcast_convert_fusion), channel_id=1, source_target_pairs={{4,0},{8,4},{12,8},{5,1},{9,5},{13,9},{6,2},{10,6},{14,10},{7,3},{... | collective-permute-start | bytes 393224 | tf_op jit(solution)/shard_map/ppermute | solution.py:24
  8.8 5.6 %collective-permute-start.3 = (f32[8,1,4,8,128]{4,3,2,0,1:T(8,128)S(1)}, f32[8,1,4,8,128]{4,3,2,0,1:T(8,128)S(1)}, u32[]{:S(2)}, u32[]{:S(2)}) collective-permute-start(f32[8,1,4,8,128]{4,3,2,0,1:T(8,128)S(1)} %bitcast_convert_fusion), channel_id=1, source_target_pairs={{0,4},{4,8},{8,12},{1,5},{5,9},{9,13},{2,6},{6,10},{10,14},{3,7},{... | collective-permute-start | bytes 393224 | tf_op jit(solution)/shard_map/ppermute | solution.py:22
  14.4 1.0 convert_multiply_fusion
  15.4 1.3 %collective-permute-start = (f32[8,1,4,8,128]{4,3,2,0,1:T(8,128)S(1)}, f32[8,1,4,8,128]{4,3,2,0,1:T(8,128)S(1)}, u32[]{:S(2)}, u32[]{:S(2)}) collective-permute-start(f32[8,1,4,8,128]{4,3,2,0,1:T(8,128)S(1)} %convert_multiply_fusion), channel_id=1, source_target_pairs={{4,0},{8,4},{12,8},{5,1},{9,5},{13,9},{6,2},{10,6},{14,10},{7,3},{... | collective-permute-start | bytes 393224 | tf_op jit(solution)/shard_map/ppermute | solution.py:24
  16.7 4.6 %collective-permute-start.1 = (f32[8,1,4,8,128]{4,3,2,0,1:T(8,128)S(1)}, f32[8,1,4,8,128]{4,3,2,0,1:T(8,128)S(1)}, u32[]{:S(2)}, u32[]{:S(2)}) collective-permute-start(f32[8,1,4,8,128]{4,3,2,0,1:T(8,128)S(1)} %convert_multiply_fusion), channel_id=1, source_target_pairs={{0,4},{4,8},{8,12},{1,5},{5,9},{9,13},{2,6},{6,10},{10,14},{3,7},{... | collective-permute-start | bytes 393224 | tf_op jit(solution)/shard_map/ppermute | solution.py:22
  21.2 0.7 fusion.132
  21.9 0.7 and_bitcast_fusion
  22.6 1.3 %fusion.143 = (f32[1,1]{1,0:T(1,128)}, f32[1,1]{1,0:T(1,128)}) fusion(f32[1,2]{1,0:T(1,128)} %param.17), kind=kLoop, calls=%fused_computation.254 | loop fusion | bytes 16 | tf_op jit(solution)/shard_map/slice | solution.py:128
  24.6 0.8 slice_bitcast_fusion.1
  25.3 1.0 copy.46
  26.3 0.7 broadcast_select_fusion.1
  27.0 5.6 %all_gather.6 = f32[16,4096]{1,0:T(8,128)S(1)} all-gather(f32[8,4096]{1,0:T(8,128)S(1)} %bitcast.135), channel_id=1, replica_groups=mesh['grp'=2,'slab'=4,'dom'=2,'shot'=2] {'dom'}, dimensions={0}, use_global_device_ids=true | all-gather | bytes 393216 | tf_op jit(solution)/shard_map/all_gather | solution.py:153
  32.7 0.7 broadcast_select_fusion
  33.3 0.0 collective-permute-done.2
  33.3 0.0 collective-permute-done.3
  33.3 0.5 select_maximum_fusion.4
  33.8 0.0 copy-done.1
  33.8 0.0 copy-done
  33.8 0.0 copy-done.3
  33.8 0.0 copy-done.4
  33.9 0.6 fusion.114
  34.5 1.3 %collective-permute-start.4 = (f32[8,1,4,8,128]{4,3,2,0,1:T(8,128)S(1)}, f32[8,1,4,8,128]{4,3,2,0,1:T(8,128)S(1)}, u32[]{:S(2)}, u32[]{:S(2)}) collective-permute-start(f32[8,1,4,8,128]{4,3,2,0,1:T(8,128)S(1)} %get-tuple-element.11), channel_id=1, source_target_pairs={{4,0},{8,4},{12,8},{5,1},{9,5},{13,9},{6,2},{10,6},{14,10},{7,3},{... | collective-permute-start | bytes 393224 | tf_op jit(solution)/shard_map/ppermute | solution.py:24
  35.8 4.6 %collective-permute-start.5 = (f32[8,1,4,8,128]{4,3,2,0,1:T(8,128)S(1)}, f32[8,1,4,8,128]{4,3,2,0,1:T(8,128)S(1)}, u32[]{:S(2)}, u32[]{:S(2)}) collective-permute-start(f32[8,1,4,8,128]{4,3,2,0,1:T(8,128)S(1)} %get-tuple-element.11), channel_id=1, source_target_pairs={{0,4},{4,8},{8,12},{1,5},{5,9},{9,13},{2,6},{6,10},{10,14},{3,7},{... | collective-permute-start | bytes 393224 | tf_op jit(solution)/shard_map/ppermute | solution.py:22
  40.3 0.0 collective-permute-done
  40.3 0.0 collective-permute-done.1
  40.3 0.5 select_maximum_fusion.6
  40.8 0.5 collective-permute-done.4
  41.3 1.5 %collective-permute-done.5 = f32[8,1,4,8,128]{4,3,2,0,1:T(8,128)S(1)} collective-permute-done((f32[8,1,4,8,128]{4,3,2,0,1:T(8,128)S(1)}, f32[8,1,4,8,128]{4,3,2,0,1:T(8,128)S(1)}, u32[]{:S(2)}, u32[]{:S(2)}) %collective-permute-start.5) | collective-permute-done | bytes 131104 | tf_op jit(solution)/shard_map/ppermute | solution.py:22
  42.8 0.5 select_maximum_fusion.2
  43.3 0.6 fusion.116
  43.9 2.0 %copy.30 = f32[8,1,4,8,128]{0,4,3,2,1:T(8,128)} copy(f32[8,1,4,8,128]{4,3,2,0,1:T(8,128)S(1)} %get-tuple-element.9) | data formatting | bytes 262144 | tf_op jit(solution)/shard_map/add | solution.py:125
  45.9 6.8 %scatter_custom_fusion = f32[8,4096]{0,1:T(8,128)} fusion(s32[128]{0:T(128)S(1)} %get-tuple-element.16, f32[]{:T(128)} %constant.21.clone.1, f32[128]{0:T(128)S(1)} %get-tuple-element.13, pred[128]{0:T(512)(128)(4,1)S(1)} %and_bitcast_fusion, f32[8,1,4096]{0,2,1:T(8,128)} %bitcast.131, s32[128]{0:T(128)S(1)} %get-tuple-element.15), kind=kCustom, calls=%fused_computation.26 | custom fusion | flops 3072 | bytes 2230784 | tf_op jit(solution)/shard_map/scatter-add | solution.py:110
  52.7 2.2 %copy.31 = f32[8,1,4,8,128]{4,3,2,1,0:T(8,128)S(1)} copy(f32[8,1,4,8,128]{0,4,3,2,1:T(8,128)} %bitcast.132) | data formatting | bytes 262144 | tf_op jit(solution)/shard_map/reshape | solution.py:112
  54.9 0.0 copy-done.2
  54.9 0.0 copy-done.5
  54.9 0.6 bitcast_multiply_fusion.1
  55.5 4.3 %collective-permute-start.7 = (f32[8,1,4,8,128]{4,3,2,0,1:T(8,128)S(1)}, f32[8,1,4,8,128]{4,3,2,0,1:T(8,128)S(1)}, u32[]{:S(2)}, u32[]{:S(2)}) collective-permute-start(f32[8,1,4,8,128]{4,3,2,0,1:T(8,128)S(1)} %get-tuple-element.7), channel_id=1, source_target_pairs={{0,4},{4,8},{8,12},{1,5},{5,9},{9,13},{2,6},{6,10},{10,14},{3,7},{... | collective-permute-start | bytes 393224 | tf_op jit(solution)/shard_map/ppermute | solution.py:22
  59.9 1.3 %collective-permute-start.6 = (f32[8,1,4,8,128]{4,3,2,0,1:T(8,128)S(1)}, f32[8,1,4,8,128]{4,3,2,0,1:T(8,128)S(1)}, u32[]{:S(2)}, u32[]{:S(2)}) collective-permute-start(f32[8,1,4,8,128]{4,3,2,0,1:T(8,128)S(1)} %get-tuple-element.7), channel_id=1, source_target_pairs={{4,0},{8,4},{12,8},{5,1},{9,5},{13,9},{6,2},{10,6},{14,10},{7,3},{... | collective-permute-start | bytes 393224 | tf_op jit(solution)/shard_map/ppermute | solution.py:24
  61.2 0.5 fusion.144
  61.6 14.0 %psum.14 = f32[16,16]{1,0:T(8,128)S(1)} all-reduce(f32[16,16]{1,0:T(8,128)S(1)} %fusion.144), channel_id=1, replica_groups=mesh['grp'=2,'slab'=4,'dom'=2,'shot'=2] {'slab'}, use_global_device_ids=true, to_apply=%region_0.1 | all-reduce | flops 256 | bytes 2048 | tf_op jit(solution)/shard_map/psum | solution.py:72
  75.7 0.7 gather_fusion
  76.3 0.6 copy.34
  76.9 3.0 %scatter_custom_fusion.1 = f32[8,4096]{0,1:T(8,128)} fusion(s32[128]{0:T(128)S(1)} %get-tuple-element.16, f32[]{:T(128)} %constant.21.clone.1, f32[128]{0:T(128)S(1)} %get-tuple-element.14, pred[128]{0:T(512)(128)(4,1)S(1)} %and_bitcast_fusion, f32[8,1,4096]{0,2,1:T(8,128)S(1)} %bitcast.129, s32[128]{0:T(128)S(1)} %get-tuple-element.15), kind=kCustom, calls=%fused_computation.24 | custom fusion | flops 3072 | bytes 2230784 | tf_op jit(solution)/shard_map/scatter-add | solution.py:110
  80.0 2.2 %copy.35 = f32[8,1,4,8,128]{4,3,2,0,1:T(8,128)S(1)} copy(f32[8,1,4,8,128]{0,4,3,2,1:T(8,128)} %bitcast.130) | data formatting | bytes 262144 | tf_op jit(solution)/shard_map/reshape | solution.py:112
  82.2 0.0 collective-permute-done.7
  82.2 0.0 collective-permute-done.6
  82.2 0.5 select_maximum_fusion
  82.7 1.3 %fusion.19 = f32[8,4,8,128]{3,2,1,0:T(8,128)} fusion(f32[8,1,4,8,128]{4,3,2,0,1:T(8,128)S(1)} %get-tuple-element.12, f32[8,1,4,8,128]{4,3,2,0,1:T(8,128)S(1)} %copy.35, f32[8,1,4,8,128]{4,3,2,0,1:T(8,128)S(1)} %collective-permute-done.7, f32[8,1,4,8,128]{4,3,2,0,1:T(8,128)S(1)} %get-tuple-element.7, f32[8,1,4,8,128]{4,3,2,0,1:T(8,128)S(1)} %collective-permute-done.6, ...), kind=kLoop, calls=%fused_computation.72 | loop fusion | flops 1409024 | bytes 3211264 | tf_op jit(solution)/shard_map/reduce_sum | solution.py:146
  83.9 0.0 all-reduce.7.cloned.1.call-update
  83.9 0.7 fusion.139
  85.3 0.1 fusion.135
  85.4 14.7 %all-reduce.7.cloned.1.call-done = f32[8,4,8,128]{3,2,1,0:T(8,128)} async-done(((f32[8,4,8,128]{3,2,1,0:T(8,128)}), f32[8,4,8,128]{3,2,1,0:T(8,128)}) %all-reduce.7.cloned.1.call-update) | async-done | bytes 131088 | tf_op jit(solution)/shard_map/psum | solution.py:147
  100.1 0.9 subtract_bitcast_fusion
  101.0 0.1 copy.45
  101.1 6.3 %all_gather.7 = f32[16,4096]{1,0:T(8,128)S(1)} all-gather(f32[8,4096]{1,0:T(8,128)S(1)} %bitcast.136), channel_id=1, replica_groups=mesh['grp'=2,'slab'=4,'dom'=2,'shot'=2] {'dom'}, dimensions={0}, use_global_device_ids=true | all-gather | bytes 393216 | tf_op jit(solution)/shard_map/all_gather | solution.py:154
  107.4 0.3 fusion.136
  107.7 0.3 fusion.2
  108.0 0.7 copy.38
  (5 shorter events, 0.0 us)
Async XLA Ops:
  6.5 27.3 %copy-start.1 = (bf16[8,1,4,8,128]{4,3,2,1,0:T(8,128)(2,1)S(1)}, bf16[8,1,4,8,128]{4,3,2,1,0:T(8,128)(2,1)}, u32[]{:S(2)}) copy-start(bf16[8,1,4,8,128]{4,3,2,1,0:T(8,128)(2,1)} %param.13) | copy-start | bytes 196612
  6.5 27.3 %copy-start = (f32[8,4,8,128]{3,2,1,0:T(8,128)S(1)}, f32[8,4,8,128]{3,2,1,0:T(8,128)}, u32[]{:S(2)}) copy-start(f32[8,4,8,128]{3,2,1,0:T(8,128)} %param.10) | copy-start | bytes 393220
  6.5 27.3 %copy-start.3 = (f32[4,8,128]{2,1,0:T(8,128)S(1)}, f32[4,8,128]{2,1,0:T(8,128)}, u32[]{:S(2)}) copy-start(f32[4,8,128]{2,1,0:T(8,128)} %param.11) | copy-start | bytes 49156
  6.5 27.3 %copy-start.4 = (bf16[8,1,4,8,128]{4,3,2,1,0:T(8,128)(2,1)S(1)}, bf16[8,1,4,8,128]{4,3,2,1,0:T(8,128)(2,1)}, u32[]{:S(2)}) copy-start(bf16[8,1,4,8,128]{4,3,2,1,0:T(8,128)(2,1)} %param.12) | copy-start | bytes 196612
  6.5 93.5 %all-reduce.7.cloned.1.call-start = ((), (), s32[]{:S(2)}) async-start(), calls=%async_computation | async-start | bytes 262144 | tf_op jit(solution)/shard_map/psum | solution.py:147
  7.5 25.8 %collective-permute-start.2 = (f32[8,1,4,8,128]{4,3,2,0,1:T(8,128)S(1)}, f32[8,1,4,8,128]{4,3,2,0,1:T(8,128)S(1)}, u32[]{:S(2)}, u32[]{:S(2)}) collective-permute-start(f32[8,1,4,8,128]{4,3,2,0,1:T(8,128)S(1)} %bitcast_convert_fusion), channel_id=1, source_target_pairs={{4,0},{8,4},{12,8},{5,1},{9,5},{13,9},{6,2},{10,6},{14,10},{7,3},{... | collective-permute-start | bytes 393224 | tf_op jit(solution)/shard_map/ppermute | solution.py:24
  8.8 24.5 %collective-permute-start.3 = (f32[8,1,4,8,128]{4,3,2,0,1:T(8,128)S(1)}, f32[8,1,4,8,128]{4,3,2,0,1:T(8,128)S(1)}, u32[]{:S(2)}, u32[]{:S(2)}) collective-permute-start(f32[8,1,4,8,128]{4,3,2,0,1:T(8,128)S(1)} %bitcast_convert_fusion), channel_id=1, source_target_pairs={{0,4},{4,8},{8,12},{1,5},{5,9},{9,13},{2,6},{6,10},{10,14},{3,7},{... | collective-permute-start | bytes 393224 | tf_op jit(solution)/shard_map/ppermute | solution.py:22
  15.4 25.0 %collective-permute-start = (f32[8,1,4,8,128]{4,3,2,0,1:T(8,128)S(1)}, f32[8,1,4,8,128]{4,3,2,0,1:T(8,128)S(1)}, u32[]{:S(2)}, u32[]{:S(2)}) collective-permute-start(f32[8,1,4,8,128]{4,3,2,0,1:T(8,128)S(1)} %convert_multiply_fusion), channel_id=1, source_target_pairs={{4,0},{8,4},{12,8},{5,1},{9,5},{13,9},{6,2},{10,6},{14,10},{7,3},{... | collective-permute-start | bytes 393224 | tf_op jit(solution)/shard_map/ppermute | solution.py:24
  16.7 23.7 %collective-permute-start.1 = (f32[8,1,4,8,128]{4,3,2,0,1:T(8,128)S(1)}, f32[8,1,4,8,128]{4,3,2,0,1:T(8,128)S(1)}, u32[]{:S(2)}, u32[]{:S(2)}) collective-permute-start(f32[8,1,4,8,128]{4,3,2,0,1:T(8,128)S(1)} %convert_multiply_fusion), channel_id=1, source_target_pairs={{0,4},{4,8},{8,12},{1,5},{5,9},{9,13},{2,6},{6,10},{10,14},{3,7},{... | collective-permute-start | bytes 393224 | tf_op jit(solution)/shard_map/ppermute | solution.py:22
  34.5 6.9 %collective-permute-start.4 = (f32[8,1,4,8,128]{4,3,2,0,1:T(8,128)S(1)}, f32[8,1,4,8,128]{4,3,2,0,1:T(8,128)S(1)}, u32[]{:S(2)}, u32[]{:S(2)}) collective-permute-start(f32[8,1,4,8,128]{4,3,2,0,1:T(8,128)S(1)} %get-tuple-element.11), channel_id=1, source_target_pairs={{4,0},{8,4},{12,8},{5,1},{9,5},{13,9},{6,2},{10,6},{14,10},{7,3},{... | collective-permute-start | bytes 393224 | tf_op jit(solution)/shard_map/ppermute | solution.py:24
  35.8 7.1 %collective-permute-start.5 = (f32[8,1,4,8,128]{4,3,2,0,1:T(8,128)S(1)}, f32[8,1,4,8,128]{4,3,2,0,1:T(8,128)S(1)}, u32[]{:S(2)}, u32[]{:S(2)}) collective-permute-start(f32[8,1,4,8,128]{4,3,2,0,1:T(8,128)S(1)} %get-tuple-element.11), channel_id=1, source_target_pairs={{0,4},{4,8},{8,12},{1,5},{5,9},{9,13},{2,6},{6,10},{10,14},{3,7},{... | collective-permute-start | bytes 393224 | tf_op jit(solution)/shard_map/ppermute | solution.py:22
  52.7 2.2 %copy-start.2 = (bf16[8,1,4,8,128]{4,3,2,1,0:T(8,128)(2,1)S(1)}, bf16[8,1,4,8,128]{4,3,2,1,0:T(8,128)(2,1)}, u32[]{:S(2)}) copy-start(bf16[8,1,4,8,128]{4,3,2,1,0:T(8,128)(2,1)} %param.14) | copy-start | bytes 196612
  52.7 2.2 %copy-start.5 = (bf16[8,1,4,8,128]{4,3,2,1,0:T(8,128)(2,1)S(1)}, bf16[8,1,4,8,128]{4,3,2,1,0:T(8,128)(2,1)}, u32[]{:S(2)}) copy-start(bf16[8,1,4,8,128]{4,3,2,1,0:T(8,128)(2,1)} %param.15) | copy-start | bytes 196612
  55.5 26.6 %collective-permute-start.7 = (f32[8,1,4,8,128]{4,3,2,0,1:T(8,128)S(1)}, f32[8,1,4,8,128]{4,3,2,0,1:T(8,128)S(1)}, u32[]{:S(2)}, u32[]{:S(2)}) collective-permute-start(f32[8,1,4,8,128]{4,3,2,0,1:T(8,128)S(1)} %get-tuple-element.7), channel_id=1, source_target_pairs={{0,4},{4,8},{8,12},{1,5},{5,9},{9,13},{2,6},{6,10},{10,14},{3,7},{... | collective-permute-start | bytes 393224 | tf_op jit(solution)/shard_map/ppermute | solution.py:22
  59.9 22.3 %collective-permute-start.6 = (f32[8,1,4,8,128]{4,3,2,0,1:T(8,128)S(1)}, f32[8,1,4,8,128]{4,3,2,0,1:T(8,128)S(1)}, u32[]{:S(2)}, u32[]{:S(2)}) collective-permute-start(f32[8,1,4,8,128]{4,3,2,0,1:T(8,128)S(1)} %get-tuple-element.7), channel_id=1, source_target_pairs={{4,0},{8,4},{12,8},{5,1},{9,5},{13,9},{6,2},{10,6},{14,10},{7,3},{... | collective-permute-start | bytes 393224 | tf_op jit(solution)/shard_map/ppermute | solution.py:24
Sparse Core Ops, SparseCore 0:
  84.1 15.9 all-reduce.6
where the time goes:
time: 116 us
  blocking collectives  26 us (22%)
  starting transfers between devices  24.2 us (21%)
  other arithmetic  21.2 us (18%)
  waiting for transfers between devices  16.7 us (14%)
  between operations  15 us (13%)
  local copies, waits for them, and re-layouts  11.5 us (10%)
    ppermute x4, starting transfers between devices, extended_2(): lax.ppermute(tail, axis, [(i, (i + 1) % count) for i in range(ends)])  19 us
    psum x1, waiting for transfers between devices, local(): summed = lax.psum(correlation, 'shot')  14.7 us
    psum x1, blocking collectives, kernel_matrix(): gram_matrix = lax.psum(partial_gram, 'slab')  14 us
    scatter-add x2, other arithmetic, inject(): placed = jnp.zeros((group_size, shot_count, local_cells), jnp.float32).at...  9.84 us
    all_gather x1, blocking collectives, local(): lax.all_gather(flat_scores, 'dom', axis=0, tiled=True)  6.34 us
    all_gather x1, blocking collectives, local(): lax.all_gather(flat_models, 'dom', axis=0, tiled=True)  5.64 us
    ppermute x4, starting transfers between devices, extended_2(): lax.ppermute(head, axis, [((i + 1) % count, i) for i in range(ends)])  5.17 us
    reshape x2, local copies, waits for them, and re-layouts, inject(): return placed.reshape(wave_now.shape)  4.37 us
  transfers between devices with their start and end apart: 9, of which 3 were waited for; matrix products, arithmetic and copies ran while one was open for 14% of the time, Pallas kernels for 0%

commit v1 on v0

v1 whole, which is shorter than its diff:
```python
import functools
import math

import jax
import jax.numpy as jnp
from jax import lax
from jax.experimental import pallas as pl
from jax.experimental.pallas import tpu as pltpu
from jax.sharding import PartitionSpec as P

DATA_WEIGHT = 0.5
PRIOR_WEIGHT = 4.0
REPEL_WEIGHT = 4.0
STENCIL = (-205.0 / 72.0, 8.0 / 5.0, -1.0 / 5.0, 8.0 / 315.0, -1.0 / 560.0)
RADIUS = 4
F32 = jnp.float32
HIGHEST = lax.Precision.HIGHEST


def call(body, outs, *operands, flops=1 << 20):
    moved = sum(x.size * x.dtype.itemsize for x in operands)
    return pl.pallas_call(
        body,
        out_shape=[jax.ShapeDtypeStruct(s, F32) for s in outs],
        in_specs=[pl.BlockSpec(memory_space=pltpu.VMEM)] * len(operands),
        out_specs=[pl.BlockSpec(memory_space=pltpu.VMEM)] * len(outs),
        compiler_params=pltpu.CompilerParams(vmem_limit_bytes=24 << 20),
        cost_estimate=pl.CostEstimate(flops=flops, bytes_accessed=moved, transcendentals=0),
    )(*operands)


def plane_weights(rows, columns):
    x = lax.broadcasted_iota(jnp.int32, (rows, columns), 0)
    y = lax.broadcasted_iota(jnp.int32, (rows, columns), 1)
    found = []
    for axis, at, size in ((0, x, rows), (1, y, columns)):
        for shift in range(-RADIUS, RADIUS + 1):
            if shift:
                inside = (at + shift >= 0) & (at + shift < size)
                found.append((axis, (-shift) % size, jnp.where(inside, STENCIL[abs(shift)], 0.0)))
    return found


def inner_laplace(planes, weights):
    result = []
    for z, here in enumerate(planes):
        total = (3.0 * STENCIL[0]) * here
        for other, plane in enumerate(planes):
            if other != z and abs(other - z) <= RADIUS:
                total = total + STENCIL[abs(other - z)] * plane
        for axis, shift, weight in weights:
            total = total + weight * pltpu.roll(here, shift, axis)
        result.append(total)
    return result


def outer_laplace(below, above, z, layers):
    total = None
    for j in range(RADIUS):
        for plane, distance in ((below[j], z + RADIUS - j), (above[j], layers + j - z)):
            if distance <= RADIUS:
                term = STENCIL[distance] * plane
                total = term if total is None else total + term
    return total


def planes_of(block, rows):
    return [block[z * rows : (z + 1) * rows] for z in range(block.shape[0] // rows)]


def sides(place_ref, first, second, rows, p):
    turned = place_ref[1:2, :] > 0
    low_on = place_ref[2:3, :] > 0
    high_on = place_ref[3:4, :] > 0
    a, b = planes_of(first[p], rows), planes_of(second[p], rows)
    below = [jnp.where(low_on, jnp.where(turned, v, u), 0.0) for u, v in zip(a, b)]
    above = [jnp.where(high_on, jnp.where(turned, u, v), 0.0) for u, v in zip(a, b)]
    return below, above


def loop(count, body):
    def step(p, carry):
        body(p)
        return carry

    lax.fori_loop(0, count, step, 0)


def solution(mesh):
    slabs, doms = mesh.shape["slab"], mesh.shape["dom"]
    up = [(2 * z, 2 * z + 2) for z in range(slabs - 1)] + [(2 * slabs - 2, 2 * slabs - 1)]
    up += [(2 * z + 1, 2 * z - 1) for z in range(1, slabs)] + [(1, 0)]
    down = [(b, a) for a, b in up]

    def exchange(block):
        return lax.ppermute(block, ("slab", "shot"), up), lax.ppermute(block, ("slab", "shot"), down)

    def from_dom(block, distance):
        return lax.ppermute(block, "dom", [((i + distance) % doms, i) for i in range(doms)])

    def other_shot(block):
        return lax.ppermute(block, "shot", [(0, 1), (1, 0)])

    def slab_sum(block):
        if slabs & (slabs - 1):
            return lax.psum(block, "slab")
        step = 1
        while step < slabs:
            block = block + lax.ppermute(block, "slab", [(i, i ^ step) for i in range(slabs)])
            step *= 2
        return block

    def local(
        particles,
        background,
        wave_prev,
        wave_now,
        adjoint_near,
        adjoint_far,
        sources,
        wavelet,
        receivers,
        observed,
    ):
        count, layers, rows, columns = particles.shape
        depth = layers * rows
        total = count * doms
        stack = (count, depth, columns)
        models = particles.reshape(stack)
        ground = background.reshape(depth, columns)
        zero, one, near, far = (
            field.reshape(stack) for field in (wave_prev, wave_now, adjoint_near, adjoint_far)
        )
        slab, shot = lax.axis_index("slab"), lax.axis_index("shot")
        place = jnp.stack([slab * depth, shot, slab > 0, slab < slabs - 1]).astype(jnp.int32)
        place = jnp.broadcast_to(jnp.pad(place, (0, 4))[:, None], (8, columns))

        def widen(one_ref, out_ref):
            out_ref[...] = one_ref[...].astype(F32)

        (wave_one,) = call(widen, [stack], one)
        one_first, one_second = exchange(wave_one)

        def medium(models_ref, ground_ref, near_ref, squared_ref, moved_ref):
            def particle(p):
                squared = ground_ref[...] * jnp.exp(models_ref[p])
                squared_ref[p] = squared
                moved_ref[p] = squared * near_ref[p].astype(F32)

            loop(count, particle)

        squared, near_moved = call(medium, [stack, stack], models, ground, near)
        near_first, near_second = exchange(near_moved)
        others = [from_dom(models, k) for k in range(1, doms)]

        def inner(one_ref, moved_ref, one_out, moved_out):
            weights = plane_weights(rows, columns)

            def particle(p):
                for source, out in ((one_ref, one_out), (moved_ref, moved_out)):
                    for z, plane in enumerate(inner_laplace(planes_of(source[p], rows), weights)):
                        out[p, z * rows : (z + 1) * rows] = plane

            loop(count, particle)

        one_inner, near_inner = call(inner, [stack, stack], wave_one, near_moved)

        def maps(place_ref, source_ref, wavelet_ref, receiver_ref, observed_ref, out_ref):
            first_row = place_ref[0:1, :]
            cells = receiver_ref[...]
            row = lax.shift_right_logical(cells, columns.bit_length() - 1) - first_row
            column = cells & (columns - 1)
            hit_row = lax.broadcasted_iota(jnp.int32, (depth, cells.shape[1]), 0) == row
            hit_column = lax.broadcasted_iota(jnp.int32, (columns, cells.shape[1]), 0) == column
            left = jnp.concatenate(
                [jnp.where(hit_row, value, 0.0) for value in (1.0, observed_ref[0:1], observed_ref[1:2])], axis=0
            )
            out_ref[0 : 3 * depth] = lax.dot_general(
                left,
                jnp.where(hit_column, 1.0, 0.0),
                (((1,), (1,)), ((), ())),
                precision=HIGHEST,
                preferred_element_type=F32,
            )
            cell = (lax.broadcasted_iota(jnp.int32, (depth, columns), 0) + first_row) * columns
            cell = cell + lax.broadcasted_iota(jnp.int32, (depth, columns), 1)
            at_source = cell == source_ref[...]
            out_ref[3 * depth : 4 * depth] = jnp.where(at_source, wavelet_ref[:, 0:1], 0.0)
            out_ref[4 * depth : 5 * depth] = jnp.where(at_source, wavelet_ref[:, 1:2], 0.0)

        (spots,) = call(
            maps,
            [(5 * depth, columns)],
            place,
            sources.reshape(1, 1),
            wavelet,
            receivers,
            observed.reshape(2, -1),
        )

        def second(place_ref, spots_ref, first, other, inner_ref, one_ref, zero_ref, squared_ref, lap_out, wave_out):
            def particle(p):
                below, above = sides(place_ref, first, other, rows, p)
                before = zero_ref[p].astype(F32)
                for z in range(layers):
                    at = slice(z * rows, (z + 1) * rows)
                    lap = inner_ref[p, at] + outer_laplace(below, above, z, layers)
                    lap_out[p, at] = lap
                    source = spots_ref[3 * depth + z * rows : 3 * depth + (z + 1) * rows]
                    wave_out[p, at] = 2.0 * one_ref[p, at] - before[at] + squared_ref[p, at] * lap + source

            loop(count, particle)

        lap_one, wave_two = call(
            second, [stack, stack], place, spots, one_first, one_second, one_inner, wave_one, zero, squared
        )
        two_first, two_second = exchange(wave_two)

        def gram(*refs):
            *parts, out_ref = refs
            height = total * rows
            same = None
            for z in range(layers):
                at = slice(z * rows, (z + 1) * rows)
                side = jnp.concatenate([part[:, at].reshape(count * rows, columns) for part in parts], axis=0)
                product = lax.dot_general(
                    side, side, (((1,), (1,)), ((), ())), precision=HIGHEST, preferred_element_type=F32
                )
                same = product if same is None else same + product
            r = lax.broadcasted_iota(jnp.int32, (height, height), 0)
            c = lax.broadcasted_iota(jnp.int32, (height, height), 1)
            same = jnp.where(r % rows == c % rows, same, 0.0)
            pick = jnp.where(
                lax.broadcasted_iota(jnp.int32, (total, height), 1) // rows
                == lax.broadcasted_iota(jnp.int32, (total, height), 0),
                1.0,
                0.0,
            )
            half = jnp.dot(pick, same, precision=HIGHEST, preferred_element_type=F32)
            out_ref[...] = lax.dot_general(
                half, pick, (((1,), (1,)), ((), ())), precision=HIGHEST, preferred_element_type=F32
            )

        (partial_gram,) = call(gram, [(total, total)], models, *others)
        full_gram = slab_sum(partial_gram)

        def third_base(place_ref, first, other, inner_ref, near_ref, far_ref, two_ref, base_out, inner_out):
            weights = plane_weights(rows, columns)

            def particle(p):
                below, above = sides(place_ref, first, other, rows, p)
                later = 2.0 * near_ref[p].astype(F32) - far_ref[p].astype(F32)
                for z in range(layers):
                    at = slice(z * rows, (z + 1) * rows)
                    base_out[p, at] = later[at] + inner_ref[p, at] + outer_laplace(below, above, z, layers)
                for z, plane in enumerate(inner_laplace(planes_of(two_ref[p], rows), weights)):
                    inner_out[p, z * rows : (z + 1) * rows] = plane

            loop(count, particle)

        base, two_inner = call(
            third_base, [stack, stack], place, near_first, near_second, near_inner, near, far, wave_two
        )

        def third(
            place_ref, spots_ref, first, other, inner_ref, one_ref, two_ref, squared_ref, base_ref, lap_out, three_out, moved_out
        ):
            def particle(p):
                below, above = sides(place_ref, first, other, rows, p)
                for z in range(layers):
                    at = slice(z * rows, (z + 1) * rows)
                    hits, _, seen, _, source = (
                        spots_ref[k * depth + z * rows : k * depth + (z + 1) * rows] for k in range(5)
                    )
                    lap = inner_ref[p, at] + outer_laplace(below, above, z, layers)
                    lap_out[p, at] = lap
                    wave_three = 2.0 * two_ref[p, at] - one_ref[p, at] + squared_ref[p, at] * lap + source
                    three = base_ref[p, at] - (hits * wave_three - seen)
                    three_out[p, at] = three
                    moved_out[p, at] = squared_ref[p, at] * three

            loop(count, particle)

        lap_two, three, three_moved = call(
            third,
            [stack, stack, stack],
            place,
            spots,
            two_first,
            two_second,
            two_inner,
            wave_one,
            wave_two,
            squared,
            base,
        )
        three_first, three_second = exchange(three_moved)

        def fourth_base(spots_ref, moved_ref, three_ref, near_ref, two_ref, lap_one_ref, lap_two_ref, out_ref):
            weights = plane_weights(rows, columns)

            def particle(p):
                before = near_ref[p].astype(F32)
                for z, lap in enumerate(inner_laplace(planes_of(moved_ref[p], rows), weights)):
                    at = slice(z * rows, (z + 1) * rows)
                    hits = spots_ref[at]
                    seen = spots_ref[depth + z * rows : depth + (z + 1) * rows]
                    three = three_ref[p, at]
                    two = 2.0 * three - before[at] + lap - (hits * two_ref[p, at] - seen)
                    out_ref[p, at] = two * lap_one_ref[p, at] + three * lap_two_ref[p, at]

            loop(count, particle)

        (inner_correlation,) = call(
            fourth_base, [stack], spots, three_moved, three, near, wave_two, lap_one, lap_two
        )

        def fourth(place_ref, first, other, inner_ref, lap_one_ref, squared_ref, out_ref):
            def particle(p):
                below, above = sides(place_ref, first, other, rows, p)
                for z in range(layers):
                    at = slice(z * rows, (z + 1) * rows)
                    full = inner_ref[p, at] + outer_laplace(below, above, z, layers) * lap_one_ref[p, at]
                    out_ref[p, at] = DATA_WEIGHT * squared_ref[p, at] * full

            loop(count, particle)

        (pull,) = call(fourth, [stack], place, three_first, three_second, inner_correlation, lap_one, squared)
        pulls = [pull] + [from_dom(pull, k) for k in range(1, doms)]
        pulls = pulls + [other_shot(block) for block in pulls]

        def spread(gram_ref, out_ref):
            r = lax.broadcasted_iota(jnp.int32, (total, total), 0)
            c = lax.broadcasted_iota(jnp.int32, (total, total), 1)
            value = gram_ref[...]
            diagonal = jnp.where(r == c, value, 0.0)
            distance = jnp.sum(diagonal, axis=1, keepdims=True) + jnp.sum(diagonal, axis=0, keepdims=True) - 2.0 * value
            width = jnp.sum(jnp.sum(distance, axis=1, keepdims=True), axis=0, keepdims=True) / (
                total * (total - 1) * math.log(total)
            )
            kernel = jnp.exp(-distance / width)
            kernel = kernel / jnp.sum(kernel, axis=1, keepdims=True)
            tall, wide = count * rows, total * rows
            pick_row = jnp.where(
                lax.broadcasted_iota(jnp.int32, (tall, total), 0) // rows
                == lax.broadcasted_iota(jnp.int32, (tall, total), 1),
                1.0,
                0.0,
            )
            pick_column = jnp.where(
                lax.broadcasted_iota(jnp.int32, (total, wide), 1) // rows
                == lax.broadcasted_iota(jnp.int32, (total, wide), 0),
                1.0,
                0.0,
            )
            half = jnp.dot(pick_row, kernel, precision=HIGHEST, preferred_element_type=F32)
            full = jnp.dot(half, pick_column, precision=HIGHEST, preferred_element_type=F32)
            same = (
                lax.broadcasted_iota(jnp.int32, (tall, wide), 0) % rows
                == lax.broadcasted_iota(jnp.int32, (tall, wide), 1) % rows
            )
            out_ref[...] = jnp.where(same, full, 0.0)

        (spread_kernel,) = call(spread, [(count * rows, total * rows)], full_gram)

        def finish(kernel_ref, *refs):
            model_refs, pull_refs, out_ref = refs[:doms], refs[doms : 3 * doms], refs[3 * doms]
            for z in range(layers):
                at = slice(z * rows, (z + 1) * rows)
                side = jnp.concatenate(
                    [
                        (
                            pull_refs[k][:, at]
                            + pull_refs[doms + k][:, at]
                            - (PRIOR_WEIGHT + REPEL_WEIGHT) * model_refs[k][:, at]
                        ).reshape(count * rows, columns)
                        for k in range(doms)
                    ],
                    axis=0,
                )
                pulled = jnp.dot(kernel_ref[...], side, precision=HIGHEST, preferred_element_type=F32)
                out_ref[:, at] = pulled.reshape(count, rows, columns) + REPEL_WEIGHT * model_refs[0][:, at]

        (update,) = call(finish, [stack], spread_kernel, models, *others, *pulls)
        return update.reshape(particles.shape)

    placed = (
        P(("grp", "dom"), "slab", None, None),
        P(("grp", "slab"), None, None),
        P(("grp", "dom"), "shot", "slab", None, None),
        P(("grp", "dom"), "shot", "slab", None, None),
        P(("grp", "dom"), "shot", "slab", None, None),
        P(("grp", "dom"), "shot", "slab", None, None),
        P(("grp", "shot")),
        P(("grp", "shot"), None),
        P(("grp", "shot"), None),
        P(("grp", "shot"), None, None),
    )
    return jax.shard_map(
        local,
        mesh=mesh,
        in_specs=placed,
        out_specs=P(("grp", "dom"), "slab", None, None),
        check_vma=False,
    )
```

time: 116 us -> 39.8 us (0.34)
  blocking collectives: 26 us -> 0 us
  other arithmetic: 21.2 us -> 0.08 us
  between operations: 15 us -> 0.81 us
  local copies, waits for them, and re-layouts: 11.5 us -> 1.7 us
  starting transfers between devices: 24.2 us -> 16.1 us
  Pallas kernels: 0 us -> 6.33 us
  waiting for transfers between devices: 16.7 us -> 14.6 us
    psum x1 -> x0, waiting for transfers between devices: 14.7 us -> none  [local(): summed = lax.psum(correlation, 'shot')]
    psum x1 -> x0, blocking collectives: 14 us -> none  [kernel_matrix(): gram_matrix = lax.psum(partial_gram, 'slab')]
    ppermute x8 -> x14, waiting for transfers between devices: 2.01 us -> 14.6 us  [the longest x4 5.67 us: exchange(): lax.ppermute(block, ('slab', 'shot'), down)]
    all_gather x2 -> x0, blocking collectives: 12 us -> none  [the longest x1 6.34 us: local(): lax.all_gather(flat_scores, 'dom', axis=0, tiled=True)]
    scatter-add x2 -> x0, other arithmetic: 9.84 us -> none  [inject(): placed = jnp.zeros((group_size, shot_count, local_cells), jnp.float32).at...]
    ppermute x8 -> x14, starting transfers between devices: 24.2 us -> 16.1 us  [the longest x4 8.89 us: exchange(): lax.ppermute(block, ('slab', 'shot'), up)]
    pallas_call x0 -> x12, Pallas kernels: none -> 6.33 us  [call(): pl.pallas_call(body, out_shape=[jax.ShapeDtypeStruct(s, F32) for s in out...]
    reshape x3 -> x0, local copies, waits for them, and re-layouts: 5.06 us -> none  [the longest x2 4.37 us: inject(): return placed.reshape(wave_now.shape)]
  transfers between devices with their start and end apart: 9 -> 14, of which waited for: 3 -> 9; matrix products, arithmetic and copies ran while one was open for 14% -> 0% of each run, Pallas kernels for 0% -> 13%
where the time goes in v1:
time: 39.8 us; the launch traced here: 39.6 us
  starting transfers between devices  16.1 us (40%)
  waiting for transfers between devices  14.6 us (37%)
  Pallas kernels  6.33 us (16%)
  local copies, waits for them, and re-layouts  1.7 us (4%)
  between operations  0.81 us (2%)
    ppermute x4, starting transfers between devices, exchange(): lax.ppermute(block, ('slab', 'shot'), up)  8.89 us
    pallas_call x12, Pallas kernels, call(): pl.pallas_call(body, out_shape=[jax.ShapeDtypeStruct(s, F32) for s in out...  6.33 us
    ppermute x4, waiting for transfers between devices, exchange(): lax.ppermute(block, ('slab', 'shot'), down)  5.67 us
    ppermute x2, starting transfers between devices, slab_sum(): lax.ppermute(block, 'slab', [(i, i ^ step) for i in range(slabs)])  5.08 us
    ppermute x2, waiting for transfers between devices, from_dom(): lax.ppermute(block, 'dom', [((i + distance) % doms, i) for i in range(dom...  4.43 us
    ppermute x2, waiting for transfers between devices, slab_sum(): lax.ppermute(block, 'slab', [(i, i ^ step) for i in range(slabs)])  3.26 us
    ppermute x2, starting transfers between devices, from_dom(): lax.ppermute(block, 'dom', [((i + distance) % doms, i) for i in range(dom...  2.09 us
    unnamed x18, local copies, waits for them, and re-layouts  1.62 us
  transfers between devices with their start and end apart: 14, of which 9 were waited for; matrix products, arithmetic and copies ran while one was open for 0% of the time, Pallas kernels for 13%

profile of v1, /device:TPU:0, one launch (start us, length us, event | category | flops | bytes accessed | tf_op | source)
XLA Modules:
  0.0 39.6 jit_solution(130303490397333037)
XLA Ops:
  0.0 0.0 copy-start
  0.0 0.0 copy-start.2
  0.0 0.9 %copy-done.2 = bf16[8,1,4,8,128]{4,3,2,1,0:T(8,128)(2,1)S(1)} copy-done((bf16[8,1,4,8,128]{4,3,2,1,0:T(8,128)(2,1)S(1)}, bf16[8,1,4,8,128]{4,3,2,1,0:T(8,128)(2,1)}, u32[]{:S(2)}) %copy-start.2) | copy-done | bytes 65560
  0.9 0.0 copy-start.1
  0.9 3.0 %collective-permute-start.3 = (f32[8,32,128]{2,1,0:T(8,128)S(1)}, f32[8,32,128]{2,1,0:T(8,128)S(1)}, u32[]{:S(2)}, u32[]{:S(2)}) collective-permute-start(f32[8,32,128]{2,1,0:T(8,128)S(1)} %shard_map.103.one_ref), channel_id=1, source_target_pairs={{0,4},{4,8},{8,12},{12,13},{5,1},{9,5},{13,9},{1,0},{2,6},{6,10},{... | collective-permute-start | bytes 393224 | tf_op jit(solution)/shard_map/ppermute | solution.py:96
  3.9 0.0 collective-permute-start.4
  3.9 0.0 copy-done
  3.9 0.0 copy-done.1
  3.9 0.0 copy-start.5
  4.0 0.7 %copy-done.5 = f32[4,8,128]{2,1,0:T(8,128)S(1)} copy-done((f32[4,8,128]{2,1,0:T(8,128)S(1)}, f32[4,8,128]{2,1,0:T(8,128)}, u32[]{:S(2)}) %copy-start.5) | copy-done | bytes 16408
  4.7 0.1 shard_map.104
  4.8 2.0 %collective-permute-start.7 = (f32[8,32,128]{2,1,0:T(8,128)S(1)}, f32[8,32,128]{2,1,0:T(8,128)S(1)}, u32[]{:S(2)}, u32[]{:S(2)}) collective-permute-start(f32[8,32,128]{2,1,0:T(8,128)S(1)} %get-tuple-element.16.moved_ref), channel_id=1, source_target_pairs={{0,4},{4,8},{8,12},{12,13},{5,1},{9,5},{13,9},{1,0},{2,6},{6,10},{... | collective-permute-start | bytes 393224 | tf_op jit(solution)/shard_map/ppermute | solution.py:96
  6.8 0.0 collective-permute-start.8
  6.8 0.1 pad_add_fusion
  7.5 0.0 copy-start.6
  7.6 0.0 copy-start.7
  7.6 0.0 copy-start.8
  7.6 1.1 %shard_map.105 = (f32[8,32,128]{2,1,0:T(8,128)S(1)}, f32[8,32,128]{2,1,0:T(8,128)S(1)}) custom-call(f32[8,32,128]{2,1,0:T(8,128)S(1)} %shard_map.103.one_ref, f32[8,32,128]{2,1,0:T(8,128)S(1)} %get-tuple-element.16.moved_ref), custom_call_target="tpu_custom_call" | custom-call | flops 1048576 | bytes 262144 | tf_op jit(solution)/shard_map/pallas_call | solution.py:22
  8.7 0.0 copy-start.3
  8.7 0.1 broadcast_in_dim.2.place_ref
  8.8 0.0 copy-done.6
  8.8 0.0 copy-done.7
  8.8 0.0 copy-done.8
  8.8 0.3 shard_map.102.spots_ref
  9.1 0.0 collective-permute-done.3.first
  9.1 0.7 %collective-permute-done.4.other = f32[8,32,128]{2,1,0:T(8,128)S(1)} collective-permute-done((f32[8,32,128]{2,1,0:T(8,128)S(1)}, f32[8,32,128]{2,1,0:T(8,128)S(1)}, u32[]{:S(2)}, u32[]{:S(2)}) %collective-permute-start.4) | collective-permute-done | bytes 131104 | tf_op jit(solution)/shard_map/ppermute | solution.py:96
  9.8 0.0 copy-done.3
  9.8 0.0 copy-start.4
  9.8 0.2 shard_map.106
  9.9 1.8 %collective-permute-start.5 = (f32[8,32,128]{2,1,0:T(8,128)S(1)}, f32[8,32,128]{2,1,0:T(8,128)S(1)}, u32[]{:S(2)}, u32[]{:S(2)}) collective-permute-start(f32[8,32,128]{2,1,0:T(8,128)S(1)} %get-tuple-element.19.two_ref), channel_id=1, source_target_pairs={{0,4},{4,8},{8,12},{12,13},{5,1},{9,5},{13,9},{1,0},{2,6},{6,10},{... | collective-permute-start | bytes 393224 | tf_op jit(solution)/shard_map/ppermute | solution.py:96
  11.8 0.0 collective-permute-start.6
  11.8 0.0 collective-permute-done.7.first
  11.8 0.4 %collective-permute-done.8.other = f32[8,32,128]{2,1,0:T(8,128)S(1)} collective-permute-done((f32[8,32,128]{2,1,0:T(8,128)S(1)}, f32[8,32,128]{2,1,0:T(8,128)S(1)}, u32[]{:S(2)}, u32[]{:S(2)}) %collective-permute-start.8) | collective-permute-done | bytes 131104 | tf_op jit(solution)/shard_map/ppermute | solution.py:96
  12.2 0.0 copy-done.4
  12.2 0.9 %shard_map.107 = (f32[8,32,128]{2,1,0:T(8,128)S(1)}, f32[8,32,128]{2,1,0:T(8,128)S(1)}) custom-call(s32[8,128]{1,0:T(8,128)S(1)} %broadcast_in_dim.2.place_ref, f32[8,32,128]{2,1,0:T(8,128)S(1)} %collective-permute-done.7.first, f32[8,32,128]{2,1,0:T(8,128)S(1)} %collective-permute-done.8.other, f32[8,32,128]{2,1,0:T(8,128)S(1)} %get-tuple-element.20.inner_ref, ...), custom_call_target="tpu_custom_call" | custom-call | flops 1048576 | bytes 659456 | tf_op jit(solution)/shard_map/pallas_call | solution.py:22
  13.1 1.2 %collective-permute-done.5.first = f32[8,32,128]{2,1,0:T(8,128)S(1)} collective-permute-done((f32[8,32,128]{2,1,0:T(8,128)S(1)}, f32[8,32,128]{2,1,0:T(8,128)S(1)}, u32[]{:S(2)}, u32[]{:S(2)}) %collective-permute-start.5) | collective-permute-done | bytes 131104 | tf_op jit(solution)/shard_map/ppermute | solution.py:96
  14.3 2.4 %collective-permute-done.6.other = f32[8,32,128]{2,1,0:T(8,128)S(1)} collective-permute-done((f32[8,32,128]{2,1,0:T(8,128)S(1)}, f32[8,32,128]{2,1,0:T(8,128)S(1)}, u32[]{:S(2)}, u32[]{:S(2)}) %collective-permute-start.6) | collective-permute-done | bytes 131104 | tf_op jit(solution)/shard_map/ppermute | solution.py:96
  16.7 0.2 shard_map.108
  16.9 0.0 collective-permute-start.10
  16.9 2.0 %collective-permute-start.9 = (f32[8,32,128]{2,1,0:T(8,128)S(1)}, f32[8,32,128]{2,1,0:T(8,128)S(1)}, u32[]{:S(2)}, u32[]{:S(2)}) collective-permute-start(f32[8,32,128]{2,1,0:T(8,128)S(1)} %get-tuple-element.23.moved_ref), channel_id=1, source_target_pairs={{0,4},{4,8},{8,12},{12,13},{5,1},{9,5},{13,9},{1,0},{2,6},{6,10},{... | collective-permute-start | bytes 393224 | tf_op jit(solution)/shard_map/ppermute | solution.py:96
  19.0 0.9 %shard_map.109.inner_ref = f32[8,32,128]{2,1,0:T(8,128)S(1)} custom-call(f32[160,128]{1,0:T(8,128)S(1)} %shard_map.102.spots_ref, f32[8,32,128]{2,1,0:T(8,128)S(1)} %get-tuple-element.23.moved_ref, f32[8,32,128]{2,1,0:T(8,128)S(1)} %get-tuple-element.24.three_ref, bf16[8,32,128]{2,1,0:T(8,128)(2,1)S(1)} %bitcast.20, ...), custom_call_target="tpu_custom_call" | custom-call | flops 1048576 | bytes 802816 | tf_op jit(solution)/shard_map/pallas_call | solution.py:22
  19.8 2.1 %collective-permute-done.10.other = f32[8,32,128]{2,1,0:T(8,128)S(1)} collective-permute-done((f32[8,32,128]{2,1,0:T(8,128)S(1)}, f32[8,32,128]{2,1,0:T(8,128)S(1)}, u32[]{:S(2)}, u32[]{:S(2)}) %collective-permute-start.10) | collective-permute-done | bytes 131104 | tf_op jit(solution)/shard_map/ppermute | solution.py:96
  21.9 0.0 collective-permute-done.9.first
  21.9 0.1 shard_map.110.refs_2_
  22.1 1.6 %collective-permute-start.11 = (f32[8,32,128]{2,1,0:T(8,128)S(1)}, f32[8,32,128]{2,1,0:T(8,128)S(1)}, u32[]{:S(2)}, u32[]{:S(2)}) collective-permute-start(f32[8,32,128]{2,1,0:T(8,128)S(1)} %shard_map.110.refs_2_), channel_id=1, source_target_pairs={{2,0},{0,2},{3,1},{1,3},{6,4},{4,6},{7,5},{5,7},{10,8},{8,10},{11,... | collective-permute-start | bytes 393224 | tf_op jit(solution)/shard_map/ppermute | solution.py:99
  23.6 0.5 %collective-permute-start = (f32[8,32,128]{2,1,0:T(8,128)S(1)}, f32[8,32,128]{2,1,0:T(8,128)S(1)}, u32[]{:S(2)}, u32[]{:S(2)}) collective-permute-start(f32[8,32,128]{2,1,0:T(8,128)S(1)} %bitcast.15), channel_id=1, source_target_pairs={{2,0},{0,2},{3,1},{1,3},{6,4},{4,6},{7,5},{5,7},{10,8},{8,10},{11,... | collective-permute-start | bytes 393224 | tf_op jit(solution)/shard_map/ppermute | solution.py:99
  24.1 0.0 collective-permute-start.12
  24.1 2.9 %collective-permute-done.11.refs_3_ = f32[8,32,128]{2,1,0:T(8,128)S(1)} collective-permute-done((f32[8,32,128]{2,1,0:T(8,128)S(1)}, f32[8,32,128]{2,1,0:T(8,128)S(1)}, u32[]{:S(2)}, u32[]{:S(2)}) %collective-permute-start.11) | collective-permute-done | bytes 131104 | tf_op jit(solution)/shard_map/ppermute | solution.py:99
  27.1 0.0 collective-permute-start.13
  27.1 1.5 %collective-permute-done.refs_1_ = f32[8,32,128]{2,1,0:T(8,128)S(1)} collective-permute-done((f32[8,32,128]{2,1,0:T(8,128)S(1)}, f32[8,32,128]{2,1,0:T(8,128)S(1)}, u32[]{:S(2)}, u32[]{:S(2)}) %collective-permute-start) | collective-permute-done | bytes 131104 | tf_op jit(solution)/shard_map/ppermute | solution.py:99
  28.6 1.0 %shard_map.100 = f32[16,16]{1,0:T(8,128)S(1)} custom-call(f32[8,32,128]{2,1,0:T(8,128)S(1)} %bitcast.16, f32[8,32,128]{2,1,0:T(8,128)S(1)} %collective-permute-done.refs_1_), custom_call_target="tpu_custom_call" | custom-call | flops 1048576 | bytes 262144 | tf_op jit(solution)/shard_map/pallas_call | solution.py:22
  29.6 2.0 %collective-permute-start.1 = (f32[16,16]{1,0:T(8,128)S(1)}, f32[16,16]{1,0:T(8,128)S(1)}, u32[]{:S(2)}, u32[]{:S(2)}) collective-permute-start(f32[16,16]{1,0:T(8,128)S(1)} %shard_map.100), channel_id=1, source_target_pairs={{0,4},{4,0},{8,12},{12,8},{1,5},{5,1},{9,13},{13,9},{2,6},{6,2},{1... | collective-permute-start | bytes 3080 | tf_op jit(solution)/shard_map/ppermute | solution.py:109
  31.7 1.6 %collective-permute-done.1 = f32[16,16]{1,0:T(8,128)S(1)} collective-permute-done((f32[16,16]{1,0:T(8,128)S(1)}, f32[16,16]{1,0:T(8,128)S(1)}, u32[]{:S(2)}, u32[]{:S(2)}) %collective-permute-start.1) | collective-permute-done | bytes 1056 | tf_op jit(solution)/shard_map/ppermute | solution.py:109
  33.3 3.0 %collective-permute-start.2 = (f32[16,16]{1,0:T(8,128)S(1)}, f32[16,16]{1,0:T(8,128)S(1)}, u32[]{:S(2)}, u32[]{:S(2)}) collective-permute-start(f32[16,16]{1,0:T(8,128)S(1)} %add.8), channel_id=1, source_target_pairs={{0,8},{4,12},{8,0},{12,4},{1,9},{5,13},{9,1},{13,5},{2,10},{6,14},... | collective-permute-start | bytes 3080 | tf_op jit(solution)/shard_map/ppermute | solution.py:109
  36.3 1.6 %collective-permute-done.2 = f32[16,16]{1,0:T(8,128)S(1)} collective-permute-done((f32[16,16]{1,0:T(8,128)S(1)}, f32[16,16]{1,0:T(8,128)S(1)}, u32[]{:S(2)}, u32[]{:S(2)}) %collective-permute-start.2) | collective-permute-done | bytes 1056 | tf_op jit(solution)/shard_map/ppermute | solution.py:109
  38.0 0.6 %shard_map.101.kernel_ref = f32[64,128]{1,0:T(8,128)S(1)} custom-call(f32[16,16]{1,0:T(8,128)S(1)} %add.9.gram_ref), custom_call_target="tpu_custom_call" | custom-call | flops 1048576 | bytes 1024 | tf_op jit(solution)/shard_map/pallas_call | solution.py:22
  38.5 0.0 collective-permute-done.12.refs_4_
  38.6 0.0 collective-permute-done.13.refs_5_
  38.6 1.0 %shard_map.111 = f32[8,32,128]{2,1,0:T(8,128)} custom-call(f32[64,128]{1,0:T(8,128)S(1)} %shard_map.101.kernel_ref, f32[8,32,128]{2,1,0:T(8,128)S(1)} %bitcast.17, f32[8,32,128]{2,1,0:T(8,128)S(1)} %collective-permute-done.refs_1_, f32[8,32,128]{2,1,0:T(8,128)S(1)} %shard_map.110.refs_2_, f32[8,32,128]{2,1,0:T(8,128)S(1)} %collective-permute-done.11.refs_3_, ...), custom_call_target="tpu_custom_call" | custom-call | flops 1048576 | bytes 819200 | tf_op jit(solution)/shard_map/pallas_call | solution.py:22
  (4 shorter events, 0.0 us)
Async XLA Ops:
  0.0 3.9 %copy-start = (f32[8,4,8,128]{3,2,1,0:T(8,128)S(1)}, f32[8,4,8,128]{3,2,1,0:T(8,128)}, u32[]{:S(2)}) copy-start(f32[8,4,8,128]{3,2,1,0:T(8,128)} %param.10) | copy-start | bytes 393220
  0.0 0.9 %copy-start.2 = (bf16[8,1,4,8,128]{4,3,2,1,0:T(8,128)(2,1)S(1)}, bf16[8,1,4,8,128]{4,3,2,1,0:T(8,128)(2,1)}, u32[]{:S(2)}) copy-start(bf16[8,1,4,8,128]{4,3,2,1,0:T(8,128)(2,1)} %param.13) | copy-start | bytes 196612
  0.9 3.1 %copy-start.1 = (bf16[8,1,4,8,128]{4,3,2,1,0:T(8,128)(2,1)S(1)}, bf16[8,1,4,8,128]{4,3,2,1,0:T(8,128)(2,1)}, u32[]{:S(2)}) copy-start(bf16[8,1,4,8,128]{4,3,2,1,0:T(8,128)(2,1)} %param.14) | copy-start | bytes 196612
  0.9 8.2 %collective-permute-start.3 = (f32[8,32,128]{2,1,0:T(8,128)S(1)}, f32[8,32,128]{2,1,0:T(8,128)S(1)}, u32[]{:S(2)}, u32[]{:S(2)}) collective-permute-start(f32[8,32,128]{2,1,0:T(8,128)S(1)} %shard_map.103.one_ref), channel_id=1, source_target_pairs={{0,4},{4,8},{8,12},{12,13},{5,1},{9,5},{13,9},{1,0},{2,6},{6,10},{... | collective-permute-start | bytes 393224 | tf_op jit(solution)/shard_map/ppermute | solution.py:96
  3.9 5.8 %collective-permute-start.4 = (f32[8,32,128]{2,1,0:T(8,128)S(1)}, f32[8,32,128]{2,1,0:T(8,128)S(1)}, u32[]{:S(2)}, u32[]{:S(2)}) collective-permute-start(f32[8,32,128]{2,1,0:T(8,128)S(1)} %shard_map.103.one_ref), channel_id=1, source_target_pairs={{4,0},{8,4},{12,8},{13,12},{1,5},{5,9},{9,13},{0,1},{6,2},{10,6},{... | collective-permute-start | bytes 393224 | tf_op jit(solution)/shard_map/ppermute | solution.py:96
  3.9 0.7 %copy-start.5 = (f32[4,8,128]{2,1,0:T(8,128)S(1)}, f32[4,8,128]{2,1,0:T(8,128)}, u32[]{:S(2)}) copy-start(f32[4,8,128]{2,1,0:T(8,128)} %param.11) | copy-start | bytes 49156
  4.8 7.0 %collective-permute-start.7 = (f32[8,32,128]{2,1,0:T(8,128)S(1)}, f32[8,32,128]{2,1,0:T(8,128)S(1)}, u32[]{:S(2)}, u32[]{:S(2)}) collective-permute-start(f32[8,32,128]{2,1,0:T(8,128)S(1)} %get-tuple-element.16.moved_ref), channel_id=1, source_target_pairs={{0,4},{4,8},{8,12},{12,13},{5,1},{9,5},{13,9},{1,0},{2,6},{6,10},{... | collective-permute-start | bytes 393224 | tf_op jit(solution)/shard_map/ppermute | solution.py:96
  6.8 5.4 %collective-permute-start.8 = (f32[8,32,128]{2,1,0:T(8,128)S(1)}, f32[8,32,128]{2,1,0:T(8,128)S(1)}, u32[]{:S(2)}, u32[]{:S(2)}) collective-permute-start(f32[8,32,128]{2,1,0:T(8,128)S(1)} %get-tuple-element.16.moved_ref), channel_id=1, source_target_pairs={{4,0},{8,4},{12,8},{13,12},{1,5},{5,9},{9,13},{0,1},{6,2},{10,6},{... | collective-permute-start | bytes 393224 | tf_op jit(solution)/shard_map/ppermute | solution.py:96
  7.5 1.2 %copy-start.6 = (f32[1,2,128]{2,1,0:T(2,128)S(1)}, f32[1,2,128]{2,1,0:T(2,128)}, u32[]{:S(2)}) copy-start(f32[1,2,128]{2,1,0:T(2,128)} %param.19) | copy-start | bytes 3076
  7.6 1.2 %copy-start.7 = (f32[1,2]{1,0:T(1,128)S(1)}, f32[1,2]{1,0:T(1,128)}, u32[]{:S(2)}) copy-start(f32[1,2]{1,0:T(1,128)} %wavelet_ref.1) | copy-start | bytes 28
  7.6 1.2 %copy-start.8 = (s32[1,128]{1,0:T(1,128)S(1)}, s32[1,128]{1,0:T(1,128)}, u32[]{:S(2)}) copy-start(s32[1,128]{1,0:T(1,128)} %receiver_ref.1) | copy-start | bytes 1540
  8.7 1.1 %copy-start.3 = (bf16[8,1,4,8,128]{4,3,2,1,0:T(8,128)(2,1)S(1)}, bf16[8,1,4,8,128]{4,3,2,1,0:T(8,128)(2,1)}, u32[]{:S(2)}) copy-start(bf16[8,1,4,8,128]{4,3,2,1,0:T(8,128)(2,1)} %param.12) | copy-start | bytes 196612
  9.8 2.4 %copy-start.4 = (bf16[8,1,4,8,128]{4,3,2,1,0:T(8,128)(2,1)S(1)}, bf16[8,1,4,8,128]{4,3,2,1,0:T(8,128)(2,1)}, u32[]{:S(2)}) copy-start(bf16[8,1,4,8,128]{4,3,2,1,0:T(8,128)(2,1)} %param.15) | copy-start | bytes 196612
  9.9 4.3 %collective-permute-start.5 = (f32[8,32,128]{2,1,0:T(8,128)S(1)}, f32[8,32,128]{2,1,0:T(8,128)S(1)}, u32[]{:S(2)}, u32[]{:S(2)}) collective-permute-start(f32[8,32,128]{2,1,0:T(8,128)S(1)} %get-tuple-element.19.two_ref), channel_id=1, source_target_pairs={{0,4},{4,8},{8,12},{12,13},{5,1},{9,5},{13,9},{1,0},{2,6},{6,10},{... | collective-permute-start | bytes 393224 | tf_op jit(solution)/shard_map/ppermute | solution.py:96
  11.8 5.0 %collective-permute-start.6 = (f32[8,32,128]{2,1,0:T(8,128)S(1)}, f32[8,32,128]{2,1,0:T(8,128)S(1)}, u32[]{:S(2)}, u32[]{:S(2)}) collective-permute-start(f32[8,32,128]{2,1,0:T(8,128)S(1)} %get-tuple-element.19.two_ref), channel_id=1, source_target_pairs={{4,0},{8,4},{12,8},{13,12},{1,5},{5,9},{9,13},{0,1},{6,2},{10,6},{... | collective-permute-start | bytes 393224 | tf_op jit(solution)/shard_map/ppermute | solution.py:96
  16.9 5.0 %collective-permute-start.10 = (f32[8,32,128]{2,1,0:T(8,128)S(1)}, f32[8,32,128]{2,1,0:T(8,128)S(1)}, u32[]{:S(2)}, u32[]{:S(2)}) collective-permute-start(f32[8,32,128]{2,1,0:T(8,128)S(1)} %get-tuple-element.23.moved_ref), channel_id=1, source_target_pairs={{4,0},{8,4},{12,8},{13,12},{1,5},{5,9},{9,13},{0,1},{6,2},{10,6},{... | collective-permute-start | bytes 393224 | tf_op jit(solution)/shard_map/ppermute | solution.py:96
  16.9 5.0 %collective-permute-start.9 = (f32[8,32,128]{2,1,0:T(8,128)S(1)}, f32[8,32,128]{2,1,0:T(8,128)S(1)}, u32[]{:S(2)}, u32[]{:S(2)}) collective-permute-start(f32[8,32,128]{2,1,0:T(8,128)S(1)} %get-tuple-element.23.moved_ref), channel_id=1, source_target_pairs={{0,4},{4,8},{8,12},{12,13},{5,1},{9,5},{13,9},{1,0},{2,6},{6,10},{... | collective-permute-start | bytes 393224 | tf_op jit(solution)/shard_map/ppermute | solution.py:96
  22.1 5.0 %collective-permute-start.11 = (f32[8,32,128]{2,1,0:T(8,128)S(1)}, f32[8,32,128]{2,1,0:T(8,128)S(1)}, u32[]{:S(2)}, u32[]{:S(2)}) collective-permute-start(f32[8,32,128]{2,1,0:T(8,128)S(1)} %shard_map.110.refs_2_), channel_id=1, source_target_pairs={{2,0},{0,2},{3,1},{1,3},{6,4},{4,6},{7,5},{5,7},{10,8},{8,10},{11,... | collective-permute-start | bytes 393224 | tf_op jit(solution)/shard_map/ppermute | solution.py:99
  23.6 5.0 %collective-permute-start = (f32[8,32,128]{2,1,0:T(8,128)S(1)}, f32[8,32,128]{2,1,0:T(8,128)S(1)}, u32[]{:S(2)}, u32[]{:S(2)}) collective-permute-start(f32[8,32,128]{2,1,0:T(8,128)S(1)} %bitcast.15), channel_id=1, source_target_pairs={{2,0},{0,2},{3,1},{1,3},{6,4},{4,6},{7,5},{5,7},{10,8},{8,10},{11,... | collective-permute-start | bytes 393224 | tf_op jit(solution)/shard_map/ppermute | solution.py:99
  24.1 14.4 %collective-permute-start.12 = (f32[8,32,128]{2,1,0:T(8,128)S(1)}, f32[8,32,128]{2,1,0:T(8,128)S(1)}, u32[]{:S(2)}, u32[]{:S(2)}) collective-permute-start(f32[8,32,128]{2,1,0:T(8,128)S(1)} %shard_map.110.refs_2_), channel_id=1, source_target_pairs={{0,1},{1,0},{2,3},{3,2},{4,5},{5,4},{6,7},{7,6},{8,9},{9,8},{10,11... | collective-permute-start | bytes 393224 | tf_op jit(solution)/shard_map/ppermute | solution.py:102
  27.1 11.5 %collective-permute-start.13 = (f32[8,32,128]{2,1,0:T(8,128)S(1)}, f32[8,32,128]{2,1,0:T(8,128)S(1)}, u32[]{:S(2)}, u32[]{:S(2)}) collective-permute-start(f32[8,32,128]{2,1,0:T(8,128)S(1)} %collective-permute-done.11.refs_3_), channel_id=1, source_target_pairs={{0,1},{1,0},{2,3},{3,2},{4,5},{5,4},{6,7},{7,6},{8,9},{9,8},{10,11... | collective-permute-start | bytes 393224 | tf_op jit(solution)/shard_map/ppermute | solution.py:102
  29.6 3.7 %collective-permute-start.1 = (f32[16,16]{1,0:T(8,128)S(1)}, f32[16,16]{1,0:T(8,128)S(1)}, u32[]{:S(2)}, u32[]{:S(2)}) collective-permute-start(f32[16,16]{1,0:T(8,128)S(1)} %shard_map.100), channel_id=1, source_target_pairs={{0,4},{4,0},{8,12},{12,8},{1,5},{5,1},{9,13},{13,9},{2,6},{6,2},{1... | collective-permute-start | bytes 3080 | tf_op jit(solution)/shard_map/ppermute | solution.py:109
  33.3 4.7 %collective-permute-start.2 = (f32[16,16]{1,0:T(8,128)S(1)}, f32[16,16]{1,0:T(8,128)S(1)}, u32[]{:S(2)}, u32[]{:S(2)}) collective-permute-start(f32[16,16]{1,0:T(8,128)S(1)} %add.8), channel_id=1, source_target_pairs={{0,8},{4,12},{8,0},{12,4},{1,9},{5,13},{9,1},{13,5},{2,10},{6,14},... | collective-permute-start | bytes 3080 | tf_op jit(solution)/shard_map/ppermute | solution.py:109

commit v2 on v1

v2 whole, which is shorter than its diff:
```python
import functools
import math

import jax
import jax.numpy as jnp
from jax import lax
from jax.experimental import pallas as pl
from jax.experimental.pallas import tpu as pltpu
from jax.sharding import PartitionSpec as P

DATA_WEIGHT = 0.5
PRIOR_WEIGHT = 4.0
REPEL_WEIGHT = 4.0
STENCIL = (-205.0 / 72.0, 8.0 / 5.0, -1.0 / 5.0, 8.0 / 315.0, -1.0 / 560.0)
RADIUS = 4
F32 = jnp.float32
HIGHEST = lax.Precision.HIGHEST


def call(body, outs, *operands, far=0, scratch=(), flops=1 << 20):
    moved = sum(x.size * x.dtype.itemsize for x in operands)
    outs = [x if isinstance(x, jax.ShapeDtypeStruct) else jax.ShapeDtypeStruct(x, F32) for x in outs]
    near = pl.BlockSpec(memory_space=pltpu.VMEM)
    operands = [pltpu.with_memory_space_constraint(x, pltpu.HBM) for x in operands[:far]] + list(operands[far:])
    return pl.pallas_call(
        body,
        out_shape=outs,
        in_specs=[pl.BlockSpec(memory_space=pltpu.HBM)] * far + [near] * (len(operands) - far),
        out_specs=[near] * len(outs),
        scratch_shapes=list(scratch),
        compiler_params=pltpu.CompilerParams(vmem_limit_bytes=24 << 20),
        cost_estimate=pl.CostEstimate(flops=flops, bytes_accessed=moved, transcendentals=0),
    )(*operands)


def fetch(sources, targets, semaphores):
    copies = [
        pltpu.make_async_copy(source, target, semaphores.at[k])
        for k, (source, target) in enumerate(zip(sources, targets))
    ]
    for copy in copies:
        copy.start()
    return copies


def plane_weights(rows, columns):
    x = lax.broadcasted_iota(jnp.int32, (rows, columns), 0)
    y = lax.broadcasted_iota(jnp.int32, (rows, columns), 1)
    found = []
    for axis, at, size in ((0, x, rows), (1, y, columns)):
        for shift in range(-RADIUS, RADIUS + 1):
            if shift:
                inside = (at + shift >= 0) & (at + shift < size)
                found.append((axis, (-shift) % size, jnp.where(inside, STENCIL[abs(shift)], 0.0)))
    return found


def inner_laplace(planes, weights):
    result = []
    for z, here in enumerate(planes):
        middle = (3.0 * STENCIL[0]) * here
        for other, plane in enumerate(planes):
            if other != z and abs(other - z) <= RADIUS:
                middle = middle + STENCIL[abs(other - z)] * plane
        parts = [middle]
        for low in range(0, len(weights), 4):
            some = None
            for axis, shift, weight in weights[low : low + 4]:
                term = weight * pltpu.roll(here, shift, axis)
                some = term if some is None else some + term
            parts.append(some)
        while len(parts) > 1:
            parts = [sum(parts[k : k + 2][1:], parts[k]) for k in range(0, len(parts), 2)]
        result.append(parts[0])
    return result


def outer_laplace(below, above, z, layers):
    total = None
    for j in range(RADIUS):
        for plane, distance in ((below[j], z + RADIUS - j), (above[j], layers + j - z)):
            if distance <= RADIUS:
                term = STENCIL[distance] * plane
                total = term if total is None else total + term
    return total


def planes_of(block, rows):
    return [block[z * rows : (z + 1) * rows] for z in range(block.shape[0] // rows)]


def side_masks(rows, columns):
    slab = jnp.full((rows, columns), lax.axis_index("slab"), jnp.int32)
    shot = jnp.full((rows, columns), lax.axis_index("shot"), jnp.int32)
    return shot > 0, slab > 0, slab < lax.axis_size("slab") - 1


def sides(masks, first, second, rows, p):
    turned, low_on, high_on = masks
    a, b = planes_of(first[p], rows), planes_of(second[p], rows)
    below = [jnp.where(low_on, jnp.where(turned, v, u), 0.0) for u, v in zip(a, b)]
    above = [jnp.where(high_on, jnp.where(turned, u, v), 0.0) for u, v in zip(a, b)]
    return below, above


def loop(count, body, together=2):
    if count % together:
        together = 1

    def step(group, carry):
        for p in range(together):
            body(group * together + p)
        return carry

    lax.fori_loop(0, count // together, step, 0)


def solution(mesh):
    slabs, doms = mesh.shape["slab"], mesh.shape["dom"]
    up = [(2 * z, 2 * z + 2) for z in range(slabs - 1)] + [(2 * slabs - 2, 2 * slabs - 1)]
    up += [(2 * z + 1, 2 * z - 1) for z in range(1, slabs)] + [(1, 0)]
    down = [(b, a) for a, b in up]

    def exchange(block):
        return lax.ppermute(block, ("slab", "shot"), up), lax.ppermute(block, ("slab", "shot"), down)

    def from_dom(block, distance):
        return lax.ppermute(block, "dom", [((i + distance) % doms, i) for i in range(doms)])

    def other_shot(block):
        return lax.ppermute(block, "shot", [(0, 1), (1, 0)])

    halving = slabs >= 4 and slabs & (slabs - 1) == 0

    def from_slab(block, step):
        if not halving:
            return jnp.zeros_like(block)
        return lax.ppermute(block, "slab", [(i, i ^ step) for i in range(slabs)])

    def local(
        particles,
        background,
        wave_prev,
        wave_now,
        adjoint_near,
        adjoint_far,
        sources,
        wavelet,
        receivers,
        observed,
    ):
        count, layers, rows, columns = particles.shape
        depth = layers * rows
        total = count * doms
        stack = (count, depth, columns)
        at_plane = [slice(z * rows, (z + 1) * rows) for z in range(layers)]
        models = particles.reshape(stack)
        ground = background.reshape(depth, columns)
        zero, one, near, far = (
            field.reshape(stack) for field in (wave_prev, wave_now, adjoint_near, adjoint_far)
        )

        halves = jax.ShapeDtypeStruct(stack, one.dtype)

        def prepare(one_hbm, models_hbm, ground_hbm, near_hbm, wave_ref, squared_ref, moved_ref, models_ref, near_ref, one_ref, ground_ref, arrived):
            copies = fetch(
                (one_hbm, models_hbm, ground_hbm, near_hbm), (one_ref, models_ref, ground_ref, near_ref), arrived
            )
            for copy in copies:
                copy.wait()

            def particle(p):
                wave_ref[p] = one_ref[p].astype(F32)
                squared = ground_ref[...] * jnp.exp(models_ref[p])
                squared_ref[p] = squared
                moved_ref[p] = squared * near_ref[p].astype(F32)

            loop(count, particle)

        wave_one, squared, near_moved, models, near = call(
            prepare,
            [stack] * 4 + [halves],
            one,
            models,
            ground,
            near,
            far=4,
            scratch=[
                pltpu.VMEM(stack, one.dtype),
                pltpu.VMEM((depth, columns), F32),
                pltpu.SemaphoreType.DMA((4,)),
            ],
        )
        one_first, one_second = exchange(wave_one)
        near_first, near_second = exchange(near_moved)
        others = [from_dom(models, k) for k in range(1, doms)]

        def first_base(*refs):
            far_away, (source_ref, one_ref, inner_out, spots_out), held = refs[:5], refs[5:9], refs[9:14]
            wavelet_ref, receiver_ref, observed_ref = held[2:]
            copies = fetch(far_away, held, refs[14])
            weights = plane_weights(rows, columns)

            def particle(p):
                for at, plane in zip(at_plane, inner_laplace(planes_of(one_ref[p], rows), weights)):
                    inner_out[p, at] = plane

            loop(count, particle)
            for copy in copies:
                copy.wait()
            first_row = lax.axis_index("slab") * depth
            cells = receiver_ref[...]
            row = lax.shift_right_logical(cells, columns.bit_length() - 1) - first_row
            column = cells & (columns - 1)
            hit_row = lax.broadcasted_iota(jnp.int32, (depth, cells.shape[1]), 0) == row
            hit_column = lax.broadcasted_iota(jnp.int32, (columns, cells.shape[1]), 0) == column
            left = jnp.concatenate(
                [jnp.where(hit_row, value, 0.0) for value in (1.0, observed_ref[0:1], observed_ref[1:2])], axis=0
            )
            spots_out[0 : 3 * depth] = lax.dot_general(
                left,
                jnp.where(hit_column, 1.0, 0.0),
                (((1,), (1,)), ((), ())),
                precision=HIGHEST,
                preferred_element_type=F32,
            )
            cell = (lax.broadcasted_iota(jnp.int32, (depth, columns), 0) + first_row) * columns
            cell = cell + lax.broadcasted_iota(jnp.int32, (depth, columns), 1)
            at_source = cell == source_ref[...]
            spots_out[3 * depth : 4 * depth] = jnp.where(at_source, wavelet_ref[:, 0:1], 0.0)
            spots_out[4 * depth : 5 * depth] = jnp.where(at_source, wavelet_ref[:, 1:2], 0.0)

        small = (wavelet, receivers, observed.reshape(2, -1))
        one_inner, spots, zero, far = call(
            first_base,
            [stack, (5 * depth, columns), halves, halves],
            zero,
            far,
            *small,
            sources.reshape(1, 1),
            wave_one,
            far=5,
            scratch=[pltpu.VMEM(x.shape, x.dtype) for x in small] + [pltpu.SemaphoreType.DMA((5,))],
        )

        def spot(spots_ref, kind, z):
            return spots_ref[kind * depth + z * rows : kind * depth + (z + 1) * rows]

        def first(spots_ref, first, second, inner_ref, one_ref, zero_ref, squared_ref, lap_out, wave_out):
            masks = side_masks(rows, columns)

            def particle(p):
                below, above = sides(masks, first, second, rows, p)
                before = zero_ref[p].astype(F32)
                for z, at in enumerate(at_plane):
                    lap = inner_ref[p, at] + outer_laplace(below, above, z, layers)
                    lap_out[p, at] = lap
                    moved = squared_ref[p, at] * lap + spot(spots_ref, 3, z)
                    wave_out[p, at] = 2.0 * one_ref[p, at] - before[at] + moved

            loop(count, particle)

        lap_one, wave_two = call(
            first, [stack] * 2, spots, one_first, one_second, one_inner, wave_one, zero, squared
        )
        two_first, two_second = exchange(wave_two)

        def gram(*refs):
            *parts, out_ref = refs
            height = total * rows
            same = None
            for at in at_plane:
                side = jnp.concatenate([part[:, at].reshape(count * rows, columns) for part in parts], axis=0)
                product = lax.dot_general(
                    side, side, (((1,), (1,)), ((), ())), precision=HIGHEST, preferred_element_type=F32
                )
                same = product if same is None else same + product
            r = lax.broadcasted_iota(jnp.int32, (height, height), 0)
            c = lax.broadcasted_iota(jnp.int32, (height, height), 1)
            same = jnp.where(r % rows == c % rows, same, 0.0)
            pick = jnp.where(
                lax.broadcasted_iota(jnp.int32, (total, height), 1) // rows
                == lax.broadcasted_iota(jnp.int32, (total, height), 0),
                1.0,
                0.0,
            )
            half = jnp.dot(pick, same, precision=HIGHEST, preferred_element_type=F32)
            out_ref[...] = lax.dot_general(
                half, pick, (((1,), (1,)), ((), ())), precision=HIGHEST, preferred_element_type=F32
            )

        (gram_one,) = call(gram, [(total, total)], models, *others)
        if not halving:
            gram_one = lax.psum(gram_one, "slab")
        gram_pair = from_slab(gram_one, 1)

        def second_base(first, second, moved_ref, near_ref, far_ref, two_ref, base_out, inner_out):
            weights = plane_weights(rows, columns)
            masks = side_masks(rows, columns)

            def waves(p):
                for at, plane in zip(at_plane, inner_laplace(planes_of(two_ref[p], rows), weights)):
                    inner_out[p, at] = plane

            def adjoints(p):
                below, above = sides(masks, first, second, rows, p)
                later = 2.0 * near_ref[p].astype(F32) - far_ref[p].astype(F32)
                for z, plane in enumerate(inner_laplace(planes_of(moved_ref[p], rows), weights)):
                    at = at_plane[z]
                    base_out[p, at] = later[at] + plane + outer_laplace(below, above, z, layers)

            loop(count, waves)
            loop(count, adjoints)

        base, two_inner = call(
            second_base, [stack] * 2, near_first, near_second, near_moved, near, far, wave_two
        )

        def second(
            spots_ref,
            first,
            second,
            inner_ref,
            one_ref,
            two_ref,
            squared_ref,
            base_ref,
            gram_ref,
            pair_ref,
            lap_out,
            three_out,
            moved_out,
            gram_out,
        ):
            gram_out[...] = gram_ref[...] + pair_ref[...]
            masks = side_masks(rows, columns)

            def particle(p):
                below, above = sides(masks, first, second, rows, p)
                for z, at in enumerate(at_plane):
                    lap = inner_ref[p, at] + outer_laplace(below, above, z, layers)
                    lap_out[p, at] = lap
                    moved = squared_ref[p, at] * lap + spot(spots_ref, 4, z)
                    wave_three = 2.0 * two_ref[p, at] - one_ref[p, at] + moved
                    three = base_ref[p, at] - (spot(spots_ref, 0, z) * wave_three - spot(spots_ref, 2, z))
                    three_out[p, at] = three
                    moved_out[p, at] = squared_ref[p, at] * three

            loop(count, particle)

        lap_two, three, three_moved, gram_two = call(
            second,
            [stack] * 3 + [(total, total)],
            spots,
            two_first,
            two_second,
            two_inner,
            wave_one,
            wave_two,
            squared,
            base,
            gram_one,
            gram_pair,
        )
        gram_pair = from_slab(gram_two, 2)
        three_first, three_second = exchange(three_moved)

        def third_base(spots_ref, moved_ref, three_ref, near_ref, two_ref, lap_one_ref, lap_two_ref, out_ref):
            weights = plane_weights(rows, columns)

            def particle(p):
                before = near_ref[p].astype(F32)
                for z, lap in enumerate(inner_laplace(planes_of(moved_ref[p], rows), weights)):
                    at = at_plane[z]
                    three = three_ref[p, at]
                    injected = spot(spots_ref, 0, z) * two_ref[p, at] - spot(spots_ref, 1, z)
                    two = 2.0 * three - before[at] + lap - injected
                    out_ref[p, at] = two * lap_one_ref[p, at] + three * lap_two_ref[p, at]

            loop(count, particle)

        (inner_correlation,) = call(
            third_base,
            [stack],
            spots,
            three_moved,
            three,
            near,
            wave_two,
            lap_one,
            lap_two,
        )

        def third(first, second, inner_ref, lap_one_ref, squared_ref, gram_ref, pair_ref, out_ref, gram_out):
            gram_out[...] = gram_ref[...] + pair_ref[...]
            masks = side_masks(rows, columns)

            def particle(p):
                below, above = sides(masks, first, second, rows, p)
                for z, at in enumerate(at_plane):
                    full = inner_ref[p, at] + outer_laplace(below, above, z, layers) * lap_one_ref[p, at]
                    out_ref[p, at] = DATA_WEIGHT * squared_ref[p, at] * full

            loop(count, particle)

        pull, gram_full = call(
            third,
            [stack, (total, total)],
            three_first,
            three_second,
            inner_correlation,
            lap_one,
            squared,
            gram_two,
            gram_pair,
        )
        step = 4
        while halving and step < slabs:
            gram_full = gram_full + from_slab(gram_full, step)
            step *= 2
        far_pulls = [from_dom(pull, k) for k in range(1, doms)]
        pull_pair = other_shot(pull)

        def spread(gram_ref, out_ref):
            value = gram_ref[...]
            r = lax.broadcasted_iota(jnp.int32, (total, total), 0)
            c = lax.broadcasted_iota(jnp.int32, (total, total), 1)
            diagonal = jnp.where(r == c, value, 0.0)
            distance = jnp.sum(diagonal, axis=1, keepdims=True) + jnp.sum(diagonal, axis=0, keepdims=True) - 2.0 * value
            width = jnp.sum(jnp.sum(distance, axis=1, keepdims=True), axis=0, keepdims=True) / (
                total * (total - 1) * math.log(total)
            )
            kernel = jnp.exp(-distance / width)
            kernel = kernel / jnp.sum(kernel, axis=1, keepdims=True)
            for j in range(total):
                for i in range(count):
                    out_ref[j, i] = jnp.broadcast_to(kernel[i : i + 1, j : j + 1], (rows, columns))

        (spread_kernel,) = call(spread, [(total, count, rows, columns)], gram_full)

        def weigh(kernel_ref, start, pulled, z, values):
            for j in range(len(values)):
                for i in range(count):
                    pulled[i] = pulled[i] + kernel_ref[start + j, i] * values[j]
            return pulled

        def last_base(kernel_ref, pull_ref, pair_ref, *refs):
            *model_refs, out_ref = refs
            both = PRIOR_WEIGHT + REPEL_WEIGHT
            for at in at_plane:
                pulled = [REPEL_WEIGHT * model_refs[0][i, at] for i in range(count)]
                own = [pull_ref[j, at] + pair_ref[j, at] - both * model_refs[0][j, at] for j in range(count)]
                pulled = weigh(kernel_ref, 0, pulled, at, own)
                for k in range(1, doms):
                    pulled = weigh(kernel_ref, k * count, pulled, at, [-both * model_refs[k][j, at] for j in range(count)])
                for i in range(count):
                    out_ref[i, at] = pulled[i]

        (update_base,) = call(last_base, [stack], spread_kernel, pull, pull_pair, models, *others)

        def others_pull(kernel_ref, *refs):
            *pulls, out_ref = refs
            for at in at_plane:
                pulled = [jnp.zeros((rows, columns), F32)] * count
                for k, block in enumerate(pulls):
                    pulled = weigh(kernel_ref, (k + 1) * count, pulled, at, [block[j, at] for j in range(count)])
                for i in range(count):
                    out_ref[i, at] = pulled[i]

        (far_pull,) = call(others_pull, [stack], spread_kernel, *far_pulls)

        def last(base_ref, pull_ref, pair_ref, out_ref):
            out_ref[...] = base_ref[...] + (pull_ref[...] + pair_ref[...])

        (update,) = call(last, [stack], update_base, far_pull, other_shot(far_pull))
        return update.reshape(particles.shape)

    placed = (
        P(("grp", "dom"), "slab", None, None),
        P(("grp", "slab"), None, None),
        P(("grp", "dom"), "shot", "slab", None, None),
        P(("grp", "dom"), "shot", "slab", None, None),
        P(("grp", "dom"), "shot", "slab", None, None),
        P(("grp", "dom"), "shot", "slab", None, None),
        P(("grp", "shot")),
        P(("grp", "shot"), None),
        P(("grp", "shot"), None),
        P(("grp", "shot"), None, None),
    )
    return jax.shard_map(
        local,
        mesh=mesh,
        in_specs=placed,
        out_specs=P(("grp", "dom"), "slab", None, None),
        check_vma=False,
    )
```

time: 39.8 us -> 31.1 us (0.78)
  waiting for transfers between devices: 14.6 us -> 7 us
  local copies, waits for them, and re-layouts: 1.7 us -> 0 us
  Pallas kernels: 6.33 us -> 6.88 us
    ppermute x4, waiting for transfers between devices: 5.67 us -> 0.01 us  [exchange(): lax.ppermute(block, ('slab', 'shot'), down)]
    unnamed x18 -> x0, local copies, waits for them, and re-layouts: 1.62 us -> none
    ppermute x4, waiting for transfers between devices: 1.22 us -> 0.01 us  [exchange(): lax.ppermute(block, ('slab', 'shot'), up)]
    ppermute x2, waiting for transfers between devices: 0.01 us -> 1.09 us  [other_shot(): return lax.ppermute(block, 'shot', [(0, 1), (1, 0)])]
    ppermute x2, waiting for transfers between devices: 3.26 us -> 2.31 us  [from_slab(): return lax.ppermute(block, 'slab', [(i, i ^ step) for i in range(slabs)])]
    ppermute x2, starting transfers between devices: 5.08 us -> 4.17 us  [from_slab(): return lax.ppermute(block, 'slab', [(i, i ^ step) for i in range(slabs)])]
    ppermute x2, waiting for transfers between devices: 4.43 us -> 3.58 us  [from_dom(): lax.ppermute(block, 'dom', [((i + distance) % doms, i) for i in range(dom...]
    ppermute x2, starting transfers between devices: 2.09 us -> 2.83 us  [from_dom(): lax.ppermute(block, 'dom', [((i + distance) % doms, i) for i in range(dom...]
  transfers between devices with their start and end apart: 14 -> 14, of which waited for: 9 -> 4; matrix products, arithmetic and copies ran while one was open for 0% -> 0% of each run, Pallas kernels for 13% -> 16%
where the time goes in v2:
time: 31.1 us; the launch traced here: 30.9 us
  starting transfers between devices  16.3 us (52%)
  waiting for transfers between devices  7 us (23%)
  Pallas kernels  6.88 us (22%)
  between operations  0.77 us (2%)
    ppermute x4, starting transfers between devices, exchange(): lax.ppermute(block, ('slab', 'shot'), up)  8.66 us
    pallas_call x12, Pallas kernels, call(): pl.pallas_call(body, out_shape=outs, in_specs=[pl.BlockSpec(memory_space=...  6.88 us
    ppermute x2, starting transfers between devices, from_slab(): return lax.ppermute(block, 'slab', [(i, i ^ step) for i in range(slabs)])  4.17 us
    ppermute x2, waiting for transfers between devices, from_dom(): lax.ppermute(block, 'dom', [((i + distance) % doms, i) for i in range(dom...  3.58 us
    ppermute x2, starting transfers between devices, from_dom(): lax.ppermute(block, 'dom', [((i + distance) % doms, i) for i in range(dom...  2.83 us
    ppermute x2, waiting for transfers between devices, from_slab(): return lax.ppermute(block, 'slab', [(i, i ^ step) for i in range(slabs)])  2.31 us
    ppermute x2, waiting for transfers between devices, other_shot(): return lax.ppermute(block, 'shot', [(0, 1), (1, 0)])  1.09 us
  transfers between devices with their start and end apart: 14, of which 4 were waited for; matrix products, arithmetic and copies ran while one was open for 0% of the time, Pallas kernels for 16%

profile of v2, /device:TPU:0, one launch (start us, length us, event | category | flops | bytes accessed | tf_op | source)
XLA Modules:
  0.0 30.9 jit_solution(10192445218006123868)
XLA Ops:
  0.0 1.0 %shard_map.100 = (f32[8,32,128]{2,1,0:T(8,128)S(1)}, f32[8,32,128]{2,1,0:T(8,128)S(1)}, f32[8,32,128]{2,1,0:T(8,128)S(1)}, f32[8,32,128]{2,1,0:T(8,128)S(1)}, bf16[8,32,128]{2,1,0:T(8,128)(2,1)S(1)}) custom-call(bf16[8,32,128]{2,1,0:T(8,128)(2,1)} %bitcast.11, f32[8,32,128]{2,1,0:T(8,128)} %bitcast.10, f32[32,128]{1,0:T(8,128)} %bitcast.15, ...), custom_call_target="tpu_custom_call" | custom-call | flops 1048576 | bytes 278528 | tf_op jit(solution)/shard_map/pallas_call | solution.py:25
  1.1 0.5 %collective-permute-start.1 = (f32[8,32,128]{2,1,0:T(8,128)S(1)}, f32[8,32,128]{2,1,0:T(8,128)S(1)}, u32[]{:S(2)}, u32[]{:S(2)}) collective-permute-start(f32[8,32,128]{2,1,0:T(8,128)S(1)} %get-tuple-element.24.refs_6_.one_ref), channel_id=1, source_target_pairs={{4,0},{8,4},{12,8},{13,12},{1,5},{5,9},{9,13},{0,1},{6,2},{10,6},{... | collective-permute-start | bytes 393224 | tf_op jit(solution)/shard_map/ppermute | solution.py:125
  1.5 2.6 %collective-permute-start = (f32[8,32,128]{2,1,0:T(8,128)S(1)}, f32[8,32,128]{2,1,0:T(8,128)S(1)}, u32[]{:S(2)}, u32[]{:S(2)}) collective-permute-start(f32[8,32,128]{2,1,0:T(8,128)S(1)} %get-tuple-element.24.refs_6_.one_ref), channel_id=1, source_target_pairs={{0,4},{4,8},{8,12},{12,13},{5,1},{9,5},{13,9},{1,0},{2,6},{6,10},{... | collective-permute-start | bytes 393224 | tf_op jit(solution)/shard_map/ppermute | solution.py:125
  4.1 1.9 %collective-permute-start.6 = (f32[8,32,128]{2,1,0:T(8,128)S(1)}, f32[8,32,128]{2,1,0:T(8,128)S(1)}, u32[]{:S(2)}, u32[]{:S(2)}) collective-permute-start(f32[8,32,128]{2,1,0:T(8,128)S(1)} %get-tuple-element.35.refs_0_), channel_id=1, source_target_pairs={{2,0},{0,2},{3,1},{1,3},{6,4},{4,6},{7,5},{5,7},{10,8},{8,10},{11,... | collective-permute-start | bytes 393224 | tf_op jit(solution)/shard_map/ppermute | solution.py:128
  6.0 0.0 collective-permute-start.5
  6.0 2.0 %collective-permute-start.4 = (f32[8,32,128]{2,1,0:T(8,128)S(1)}, f32[8,32,128]{2,1,0:T(8,128)S(1)}, u32[]{:S(2)}, u32[]{:S(2)}) collective-permute-start(f32[8,32,128]{2,1,0:T(8,128)S(1)} %get-tuple-element.30.moved_ref), channel_id=1, source_target_pairs={{0,4},{4,8},{8,12},{12,13},{5,1},{9,5},{13,9},{1,0},{2,6},{6,10},{... | collective-permute-start | bytes 393224 | tf_op jit(solution)/shard_map/ppermute | solution.py:125
  8.7 1.2 %shard_map.101 = (f32[8,32,128]{2,1,0:T(8,128)S(1)}, f32[160,128]{1,0:T(8,128)S(1)}, bf16[8,32,128]{2,1,0:T(8,128)(2,1)S(1)}, bf16[8,32,128]{2,1,0:T(8,128)(2,1)S(1)}) custom-call(bf16[8,32,128]{2,1,0:T(8,128)(2,1)} %bitcast.13, bf16[8,32,128]{2,1,0:T(8,128)(2,1)} %bitcast.14, f32[1,2]{1,0:T(1,128)} %refs_2_.1, s32[1,128]{1,0:T(1,128)} %refs_3_.1, ...), custom_call_target="tpu_custom_call" | custom-call | flops 1048576 | bytes 263692 | tf_op jit(solution)/shard_map/pallas_call | solution.py:25
  9.9 0.0 collective-permute-done.1.second
  9.9 0.0 collective-permute-done.first
  9.9 0.1 shard_map.102
  10.1 0.0 collective-permute-start.3
  10.1 2.0 %collective-permute-start.2 = (f32[8,32,128]{2,1,0:T(8,128)S(1)}, f32[8,32,128]{2,1,0:T(8,128)S(1)}, u32[]{:S(2)}, u32[]{:S(2)}) collective-permute-start(f32[8,32,128]{2,1,0:T(8,128)S(1)} %get-tuple-element.29.two_ref), channel_id=1, source_target_pairs={{0,4},{4,8},{8,12},{12,13},{5,1},{9,5},{13,9},{1,0},{2,6},{6,10},{... | collective-permute-start | bytes 393224 | tf_op jit(solution)/shard_map/ppermute | solution.py:125
  12.1 0.0 collective-permute-done.6.refs_1_
  12.1 1.0 %shard_map.104.gram_ref = f32[16,16]{1,0:T(8,128)S(1)} custom-call(f32[8,32,128]{2,1,0:T(8,128)S(1)} %get-tuple-element.35.refs_0_, f32[8,32,128]{2,1,0:T(8,128)S(1)} %collective-permute-done.6.refs_1_), custom_call_target="tpu_custom_call" | custom-call | flops 1048576 | bytes 262144 | tf_op jit(solution)/shard_map/pallas_call | solution.py:25
  13.2 1.6 %collective-permute-start.7 = (f32[16,16]{1,0:T(8,128)S(1)}, f32[16,16]{1,0:T(8,128)S(1)}, u32[]{:S(2)}, u32[]{:S(2)}) collective-permute-start(f32[16,16]{1,0:T(8,128)S(1)} %shard_map.104.gram_ref), channel_id=1, source_target_pairs={{0,4},{4,0},{8,12},{12,8},{1,5},{5,1},{9,13},{13,9},{2,6},{6,2},{1... | collective-permute-start | bytes 3080 | tf_op jit(solution)/shard_map/ppermute | solution.py:138
  14.8 0.0 collective-permute-done.5.second
  14.8 0.0 collective-permute-done.4.first
  14.8 1.1 %shard_map.103 = (f32[8,32,128]{2,1,0:T(8,128)S(1)}, f32[8,32,128]{2,1,0:T(8,128)S(1)}) custom-call(f32[8,32,128]{2,1,0:T(8,128)S(1)} %collective-permute-done.4.first, f32[8,32,128]{2,1,0:T(8,128)S(1)} %collective-permute-done.5.second, f32[8,32,128]{2,1,0:T(8,128)S(1)} %get-tuple-element.30.moved_ref, bf16[8,32,128]{2,1,0:T(8,128)(2,1)S(1)} %get-tuple-element.31.near_ref, ...), custom_call_target="tpu_custom_call" | custom-call | flops 1048576 | bytes 655360 | tf_op jit(solution)/shard_map/pallas_call | solution.py:25
  15.9 0.9 %collective-permute-done.7.pair_ref = f32[16,16]{1,0:T(8,128)S(1)} collective-permute-done((f32[16,16]{1,0:T(8,128)S(1)}, f32[16,16]{1,0:T(8,128)S(1)}, u32[]{:S(2)}, u32[]{:S(2)}) %collective-permute-start.7) | collective-permute-done | bytes 1056 | tf_op jit(solution)/shard_map/ppermute | solution.py:138
  16.8 0.0 collective-permute-done.3.second
  16.8 0.0 collective-permute-done.2.first
  16.8 0.1 shard_map.105
  17.0 0.0 collective-permute-start.9
  17.0 2.0 %collective-permute-start.8 = (f32[8,32,128]{2,1,0:T(8,128)S(1)}, f32[8,32,128]{2,1,0:T(8,128)S(1)}, u32[]{:S(2)}, u32[]{:S(2)}) collective-permute-start(f32[8,32,128]{2,1,0:T(8,128)S(1)} %get-tuple-element.36.moved_ref), channel_id=1, source_target_pairs={{0,4},{4,8},{8,12},{12,13},{5,1},{9,5},{13,9},{1,0},{2,6},{6,10},{... | collective-permute-start | bytes 393224 | tf_op jit(solution)/shard_map/ppermute | solution.py:125
  19.0 2.6 %collective-permute-start.10 = (f32[16,16]{1,0:T(8,128)S(1)}, f32[16,16]{1,0:T(8,128)S(1)}, u32[]{:S(2)}, u32[]{:S(2)}) collective-permute-start(f32[16,16]{1,0:T(8,128)S(1)} %get-tuple-element.40.gram_ref), channel_id=1, source_target_pairs={{0,8},{4,12},{8,0},{12,4},{1,9},{5,13},{9,1},{13,5},{2,10},{6,14},... | collective-permute-start | bytes 3080 | tf_op jit(solution)/shard_map/ppermute | solution.py:138
  21.6 0.6 %shard_map.106.inner_ref = f32[8,32,128]{2,1,0:T(8,128)S(1)} custom-call(f32[160,128]{1,0:T(8,128)S(1)} %get-tuple-element.25.spots_ref, f32[8,32,128]{2,1,0:T(8,128)S(1)} %get-tuple-element.36.moved_ref, f32[8,32,128]{2,1,0:T(8,128)S(1)} %get-tuple-element.37.three_ref, bf16[8,32,128]{2,1,0:T(8,128)(2,1)S(1)} %get-tuple-element.31.near_ref, ...), custom_call_target="tpu_custom_call" | custom-call | flops 1048576 | bytes 802816 | tf_op jit(solution)/shard_map/pallas_call | solution.py:25
  22.2 1.4 %collective-permute-done.10.pair_ref = f32[16,16]{1,0:T(8,128)S(1)} collective-permute-done((f32[16,16]{1,0:T(8,128)S(1)}, f32[16,16]{1,0:T(8,128)S(1)}, u32[]{:S(2)}, u32[]{:S(2)}) %collective-permute-start.10) | collective-permute-done | bytes 1056 | tf_op jit(solution)/shard_map/ppermute | solution.py:138
  23.6 0.0 collective-permute-done.9.second
  23.6 0.0 collective-permute-done.8.first
  23.6 0.1 shard_map.107
  23.7 0.9 %collective-permute-start.12 = (f32[8,32,128]{2,1,0:T(8,128)S(1)}, f32[8,32,128]{2,1,0:T(8,128)S(1)}, u32[]{:S(2)}, u32[]{:S(2)}) collective-permute-start(f32[8,32,128]{2,1,0:T(8,128)S(1)} %get-tuple-element.42.pull_ref), channel_id=1, source_target_pairs={{2,0},{0,2},{3,1},{1,3},{6,4},{4,6},{7,5},{5,7},{10,8},{8,10},{11,... | collective-permute-start | bytes 393224 | tf_op jit(solution)/shard_map/ppermute | solution.py:128
  24.6 0.0 collective-permute-start.11
  24.6 0.5 %shard_map.108.kernel_ref = f32[16,8,8,128]{3,2,1,0:T(8,128)S(1)} custom-call(f32[16,16]{1,0:T(8,128)S(1)} %get-tuple-element.41.gram_ref), custom_call_target="tpu_custom_call" | custom-call | flops 1048576 | bytes 1024 | tf_op jit(solution)/shard_map/pallas_call | solution.py:25
  25.2 3.6 %collective-permute-done.12.refs_0_ = f32[8,32,128]{2,1,0:T(8,128)S(1)} collective-permute-done((f32[8,32,128]{2,1,0:T(8,128)S(1)}, f32[8,32,128]{2,1,0:T(8,128)S(1)}, u32[]{:S(2)}, u32[]{:S(2)}) %collective-permute-start.12) | collective-permute-done | bytes 131104 | tf_op jit(solution)/shard_map/ppermute | solution.py:128
  28.7 0.1 shard_map.110.pull_ref
  28.8 0.1 collective-permute-start.13
  28.9 0.0 collective-permute-done.11.pair_ref
  28.9 0.2 shard_map.109.base_ref
  29.1 1.1 %collective-permute-done.13.pair_ref = f32[8,32,128]{2,1,0:T(8,128)S(1)} collective-permute-done((f32[8,32,128]{2,1,0:T(8,128)S(1)}, f32[8,32,128]{2,1,0:T(8,128)S(1)}, u32[]{:S(2)}, u32[]{:S(2)}) %collective-permute-start.13) | collective-permute-done | bytes 131104 | tf_op jit(solution)/shard_map/ppermute | solution.py:131
  30.2 0.7 %shard_map.111 = f32[8,32,128]{2,1,0:T(8,128)} custom-call(f32[8,32,128]{2,1,0:T(8,128)S(1)} %shard_map.109.base_ref, f32[8,32,128]{2,1,0:T(8,128)S(1)} %shard_map.110.pull_ref, f32[8,32,128]{2,1,0:T(8,128)S(1)} %collective-permute-done.13.pair_ref), custom_call_target="tpu_custom_call" | custom-call | flops 1048576 | bytes 393216 | tf_op jit(solution)/shard_map/pallas_call | solution.py:25
Async XLA Ops:
  1.1 8.8 %collective-permute-start.1 = (f32[8,32,128]{2,1,0:T(8,128)S(1)}, f32[8,32,128]{2,1,0:T(8,128)S(1)}, u32[]{:S(2)}, u32[]{:S(2)}) collective-permute-start(f32[8,32,128]{2,1,0:T(8,128)S(1)} %get-tuple-element.24.refs_6_.one_ref), channel_id=1, source_target_pairs={{4,0},{8,4},{12,8},{13,12},{1,5},{5,9},{9,13},{0,1},{6,2},{10,6},{... | collective-permute-start | bytes 393224 | tf_op jit(solution)/shard_map/ppermute | solution.py:125
  1.5 8.4 %collective-permute-start = (f32[8,32,128]{2,1,0:T(8,128)S(1)}, f32[8,32,128]{2,1,0:T(8,128)S(1)}, u32[]{:S(2)}, u32[]{:S(2)}) collective-permute-start(f32[8,32,128]{2,1,0:T(8,128)S(1)} %get-tuple-element.24.refs_6_.one_ref), channel_id=1, source_target_pairs={{0,4},{4,8},{8,12},{12,13},{5,1},{9,5},{13,9},{1,0},{2,6},{6,10},{... | collective-permute-start | bytes 393224 | tf_op jit(solution)/shard_map/ppermute | solution.py:125
  4.1 8.0 %collective-permute-start.6 = (f32[8,32,128]{2,1,0:T(8,128)S(1)}, f32[8,32,128]{2,1,0:T(8,128)S(1)}, u32[]{:S(2)}, u32[]{:S(2)}) collective-permute-start(f32[8,32,128]{2,1,0:T(8,128)S(1)} %get-tuple-element.35.refs_0_), channel_id=1, source_target_pairs={{2,0},{0,2},{3,1},{1,3},{6,4},{4,6},{7,5},{5,7},{10,8},{8,10},{11,... | collective-permute-start | bytes 393224 | tf_op jit(solution)/shard_map/ppermute | solution.py:128
  6.0 8.7 %collective-permute-start.5 = (f32[8,32,128]{2,1,0:T(8,128)S(1)}, f32[8,32,128]{2,1,0:T(8,128)S(1)}, u32[]{:S(2)}, u32[]{:S(2)}) collective-permute-start(f32[8,32,128]{2,1,0:T(8,128)S(1)} %get-tuple-element.30.moved_ref), channel_id=1, source_target_pairs={{4,0},{8,4},{12,8},{13,12},{1,5},{5,9},{9,13},{0,1},{6,2},{10,6},{... | collective-permute-start | bytes 393224 | tf_op jit(solution)/shard_map/ppermute | solution.py:125
  6.0 8.7 %collective-permute-start.4 = (f32[8,32,128]{2,1,0:T(8,128)S(1)}, f32[8,32,128]{2,1,0:T(8,128)S(1)}, u32[]{:S(2)}, u32[]{:S(2)}) collective-permute-start(f32[8,32,128]{2,1,0:T(8,128)S(1)} %get-tuple-element.30.moved_ref), channel_id=1, source_target_pairs={{0,4},{4,8},{8,12},{12,13},{5,1},{9,5},{13,9},{1,0},{2,6},{6,10},{... | collective-permute-start | bytes 393224 | tf_op jit(solution)/shard_map/ppermute | solution.py:125
  10.1 6.8 %collective-permute-start.3 = (f32[8,32,128]{2,1,0:T(8,128)S(1)}, f32[8,32,128]{2,1,0:T(8,128)S(1)}, u32[]{:S(2)}, u32[]{:S(2)}) collective-permute-start(f32[8,32,128]{2,1,0:T(8,128)S(1)} %get-tuple-element.29.two_ref), channel_id=1, source_target_pairs={{4,0},{8,4},{12,8},{13,12},{1,5},{5,9},{9,13},{0,1},{6,2},{10,6},{... | collective-permute-start | bytes 393224 | tf_op jit(solution)/shard_map/ppermute | solution.py:125
  10.1 6.8 %collective-permute-start.2 = (f32[8,32,128]{2,1,0:T(8,128)S(1)}, f32[8,32,128]{2,1,0:T(8,128)S(1)}, u32[]{:S(2)}, u32[]{:S(2)}) collective-permute-start(f32[8,32,128]{2,1,0:T(8,128)S(1)} %get-tuple-element.29.two_ref), channel_id=1, source_target_pairs={{0,4},{4,8},{8,12},{12,13},{5,1},{9,5},{13,9},{1,0},{2,6},{6,10},{... | collective-permute-start | bytes 393224 | tf_op jit(solution)/shard_map/ppermute | solution.py:125
  13.2 3.7 %collective-permute-start.7 = (f32[16,16]{1,0:T(8,128)S(1)}, f32[16,16]{1,0:T(8,128)S(1)}, u32[]{:S(2)}, u32[]{:S(2)}) collective-permute-start(f32[16,16]{1,0:T(8,128)S(1)} %shard_map.104.gram_ref), channel_id=1, source_target_pairs={{0,4},{4,0},{8,12},{12,8},{1,5},{5,1},{9,13},{13,9},{2,6},{6,2},{1... | collective-permute-start | bytes 3080 | tf_op jit(solution)/shard_map/ppermute | solution.py:138
  17.0 6.6 %collective-permute-start.9 = (f32[8,32,128]{2,1,0:T(8,128)S(1)}, f32[8,32,128]{2,1,0:T(8,128)S(1)}, u32[]{:S(2)}, u32[]{:S(2)}) collective-permute-start(f32[8,32,128]{2,1,0:T(8,128)S(1)} %get-tuple-element.36.moved_ref), channel_id=1, source_target_pairs={{4,0},{8,4},{12,8},{13,12},{1,5},{5,9},{9,13},{0,1},{6,2},{10,6},{... | collective-permute-start | bytes 393224 | tf_op jit(solution)/shard_map/ppermute | solution.py:125
  17.0 6.6 %collective-permute-start.8 = (f32[8,32,128]{2,1,0:T(8,128)S(1)}, f32[8,32,128]{2,1,0:T(8,128)S(1)}, u32[]{:S(2)}, u32[]{:S(2)}) collective-permute-start(f32[8,32,128]{2,1,0:T(8,128)S(1)} %get-tuple-element.36.moved_ref), channel_id=1, source_target_pairs={{0,4},{4,8},{8,12},{12,13},{5,1},{9,5},{13,9},{1,0},{2,6},{6,10},{... | collective-permute-start | bytes 393224 | tf_op jit(solution)/shard_map/ppermute | solution.py:125
  19.0 4.5 %collective-permute-start.10 = (f32[16,16]{1,0:T(8,128)S(1)}, f32[16,16]{1,0:T(8,128)S(1)}, u32[]{:S(2)}, u32[]{:S(2)}) collective-permute-start(f32[16,16]{1,0:T(8,128)S(1)} %get-tuple-element.40.gram_ref), channel_id=1, source_target_pairs={{0,8},{4,12},{8,0},{12,4},{1,9},{5,13},{9,1},{13,5},{2,10},{6,14},... | collective-permute-start | bytes 3080 | tf_op jit(solution)/shard_map/ppermute | solution.py:138
  23.7 5.0 %collective-permute-start.12 = (f32[8,32,128]{2,1,0:T(8,128)S(1)}, f32[8,32,128]{2,1,0:T(8,128)S(1)}, u32[]{:S(2)}, u32[]{:S(2)}) collective-permute-start(f32[8,32,128]{2,1,0:T(8,128)S(1)} %get-tuple-element.42.pull_ref), channel_id=1, source_target_pairs={{2,0},{0,2},{3,1},{1,3},{6,4},{4,6},{7,5},{5,7},{10,8},{8,10},{11,... | collective-permute-start | bytes 393224 | tf_op jit(solution)/shard_map/ppermute | solution.py:128
  24.6 4.3 %collective-permute-start.11 = (f32[8,32,128]{2,1,0:T(8,128)S(1)}, f32[8,32,128]{2,1,0:T(8,128)S(1)}, u32[]{:S(2)}, u32[]{:S(2)}) collective-permute-start(f32[8,32,128]{2,1,0:T(8,128)S(1)} %get-tuple-element.42.pull_ref), channel_id=1, source_target_pairs={{0,1},{1,0},{2,3},{3,2},{4,5},{5,4},{6,7},{7,6},{8,9},{9,8},{10,11... | collective-permute-start | bytes 393224 | tf_op jit(solution)/shard_map/ppermute | solution.py:131
  28.8 1.4 %collective-permute-start.13 = (f32[8,32,128]{2,1,0:T(8,128)S(1)}, f32[8,32,128]{2,1,0:T(8,128)S(1)}, u32[]{:S(2)}, u32[]{:S(2)}) collective-permute-start(f32[8,32,128]{2,1,0:T(8,128)S(1)} %shard_map.110.pull_ref), channel_id=1, source_target_pairs={{0,1},{1,0},{2,3},{3,2},{4,5},{5,4},{6,7},{7,6},{8,9},{9,8},{10,11... | collective-permute-start | bytes 393224 | tf_op jit(solution)/shard_map/ppermute | solution.py:131

commit v3 on v2

--- a/solution.py
+++ b/solution.py
@@ -15,6 +15,7 @@
 RADIUS = 4
 F32 = jnp.float32
 HIGHEST = lax.Precision.HIGHEST
+LONG = 1 << 33
 
 
 def call(body, outs, *operands, far=0, scratch=(), flops=1 << 20):
@@ -193,7 +194,6 @@
         )
         one_first, one_second = exchange(wave_one)
         near_first, near_second = exchange(near_moved)
-        others = [from_dom(models, k) for k in range(1, doms)]
 
         def first_base(*refs):
             far_away, (source_ref, one_ref, inner_out, spots_out), held = refs[:5], refs[5:9], refs[9:14]
@@ -226,7 +226,7 @@
             )
             cell = (lax.broadcasted_iota(jnp.int32, (depth, columns), 0) + first_row) * columns
             cell = cell + lax.broadcasted_iota(jnp.int32, (depth, columns), 1)
-            at_source = cell == source_ref[...]
+            at_source = cell == source_ref[0:1, :]
             spots_out[3 * depth : 4 * depth] = jnp.where(at_source, wavelet_ref[:, 0:1], 0.0)
             spots_out[4 * depth : 5 * depth] = jnp.where(at_source, wavelet_ref[:, 1:2], 0.0)
 
@@ -237,7 +237,7 @@
             zero,
             far,
             *small,
-            sources.reshape(1, 1),
+            jnp.broadcast_to(sources[:, None], (rows, columns)),
             wave_one,
             far=5,
             scratch=[pltpu.VMEM(x.shape, x.dtype) for x in small] + [pltpu.SemaphoreType.DMA((5,))],
@@ -246,7 +246,10 @@
         def spot(spots_ref, kind, z):
             return spots_ref[kind * depth + z * rows : kind * depth + (z + 1) * rows]
 
-        def first(spots_ref, first, second, inner_ref, one_ref, zero_ref, squared_ref, lap_out, wave_out):
+        def first(
+            spots_ref, first, second, inner_ref, one_ref, zero_ref, squared_ref, models_ref, lap_out, wave_out, models_out
+        ):
+            models_out[...] = models_ref[...]
             masks = side_masks(rows, columns)
 
             def particle(p):
@@ -260,39 +263,11 @@
 
             loop(count, particle)
 
-        lap_one, wave_two = call(
-            first, [stack] * 2, spots, one_first, one_second, one_inner, wave_one, zero, squared
+        lap_one, wave_two, models_sent = call(
+            first, [stack] * 3, spots, one_first, one_second, one_inner, wave_one, zero, squared, models
         )
         two_first, two_second = exchange(wave_two)
-
-        def gram(*refs):
-            *parts, out_ref = refs
-            height = total * rows
-            same = None
-            for at in at_plane:
-                side = jnp.concatenate([part[:, at].reshape(count * rows, columns) for part in parts], axis=0)
-                product = lax.dot_general(
-                    side, side, (((1,), (1,)), ((), ())), precision=HIGHEST, preferred_element_type=F32
-                )
-                same = product if same is None else same + product
-            r = lax.broadcasted_iota(jnp.int32, (height, height), 0)
-            c = lax.broadcasted_iota(jnp.int32, (height, height), 1)
-            same = jnp.where(r % rows == c % rows, same, 0.0)
-            pick = jnp.where(
-                lax.broadcasted_iota(jnp.int32, (total, height), 1) // rows
-                == lax.broadcasted_iota(jnp.int32, (total, height), 0),
-                1.0,
-                0.0,
-            )
-            half = jnp.dot(pick, same, precision=HIGHEST, preferred_element_type=F32)
-            out_ref[...] = lax.dot_general(
-                half, pick, (((1,), (1,)), ((), ())), precision=HIGHEST, preferred_element_type=F32
-            )
-
-        (gram_one,) = call(gram, [(total, total)], models, *others)
-        if not halving:
-            gram_one = lax.psum(gram_one, "slab")
-        gram_pair = from_slab(gram_one, 1)
+        others = [from_dom(models_sent, k) for k in range(1, doms)]
 
         def second_base(first, second, moved_ref, near_ref, far_ref, two_ref, base_out, inner_out):
             weights = plane_weights(rows, columns)
@@ -325,14 +300,10 @@
             two_ref,
             squared_ref,
             base_ref,
-            gram_ref,
-            pair_ref,
             lap_out,
             three_out,
             moved_out,
-            gram_out,
         ):
-            gram_out[...] = gram_ref[...] + pair_ref[...]
             masks = side_masks(rows, columns)
 
             def particle(p):
@@ -348,9 +319,9 @@
 
             loop(count, particle)
 
-        lap_two, three, three_moved, gram_two = call(
+        lap_two, three, three_moved = call(
             second,
-            [stack] * 3 + [(total, total)],
+            [stack] * 3,
             spots,
             two_first,
             two_second,
@@ -359,11 +330,38 @@
             wave_two,
             squared,
             base,
-            gram_one,
-            gram_pair,
-        )
-        gram_pair = from_slab(gram_two, 2)
+        )
         three_first, three_second = exchange(three_moved)
+
+        wide = total * rows
+
+        def gram(*refs):
+            *parts, out_ref = refs
+            side = jnp.concatenate(
+                [
+                    jnp.concatenate([part[:, at].reshape(count * rows, columns) for part in parts], axis=0)
+                    for at in at_plane
+                ],
+                axis=1,
+            )
+            same = lax.dot_general(
+                side, side, (((1,), (1,)), ((), ())), precision=HIGHEST, preferred_element_type=F32
+            )
+            r = lax.broadcasted_iota(jnp.int32, (wide, wide), 0)
+            c = lax.broadcasted_iota(jnp.int32, (wide, wide), 1)
+            same = jnp.where(r % rows == c % rows, same, 0.0)
+            same = jnp.sum(same.reshape(total, rows, wide), axis=1)
+            step = 1
+            while step < rows:
+                same = same + pltpu.roll(same, wide - step, 1)
+                step *= 2
+            first_of = lax.broadcasted_iota(jnp.int32, (total, wide), 1) % rows == 0
+            out_ref[...] = jnp.where(first_of, same, 0.0)
+
+        (gram_one,) = call(gram, [(total, wide)], models, *others)
+        if not halving:
+            gram_one = lax.psum(gram_one, "slab")
+        gram_pair = from_slab(gram_one, 1)
 
         def third_base(spots_ref, moved_ref, three_ref, near_ref, two_ref, lap_one_ref, lap_two_ref, out_ref):
             weights = plane_weights(rows, columns)
@@ -391,88 +389,86 @@
             lap_two,
         )
 
-        def third(first, second, inner_ref, lap_one_ref, squared_ref, gram_ref, pair_ref, out_ref, gram_out):
-            gram_out[...] = gram_ref[...] + pair_ref[...]
+        def third(first, second, inner_ref, lap_one_ref, squared_ref, models_ref, out_ref):
             masks = side_masks(rows, columns)
 
             def particle(p):
                 below, above = sides(masks, first, second, rows, p)
                 for z, at in enumerate(at_plane):
                     full = inner_ref[p, at] + outer_laplace(below, above, z, layers) * lap_one_ref[p, at]
-                    out_ref[p, at] = DATA_WEIGHT * squared_ref[p, at] * full
-
-            loop(count, particle)
-
-        pull, gram_full = call(
+                    score = DATA_WEIGHT * squared_ref[p, at] * full
+                    out_ref[p, at] = score - 0.5 * (PRIOR_WEIGHT + REPEL_WEIGHT) * models_ref[p, at]
+
+            loop(count, particle)
+
+        (pull,) = call(
             third,
-            [stack, (total, total)],
+            [stack],
             three_first,
             three_second,
             inner_correlation,
             lap_one,
             squared,
-            gram_two,
-            gram_pair,
-        )
-        step = 4
-        while halving and step < slabs:
-            gram_full = gram_full + from_slab(gram_full, step)
-            step *= 2
+            models,
+        )
         far_pulls = [from_dom(pull, k) for k in range(1, doms)]
         pull_pair = other_shot(pull)
 
-        def spread(gram_ref, out_ref):
-            value = gram_ref[...]
-            r = lax.broadcasted_iota(jnp.int32, (total, total), 0)
-            c = lax.broadcasted_iota(jnp.int32, (total, total), 1)
-            diagonal = jnp.where(r == c, value, 0.0)
+        far_pairs = [other_shot(block) for block in far_pulls]
+
+        def plus(first_ref, second_ref, out_ref):
+            out_ref[...] = first_ref[...] + second_ref[...]
+
+        step = 2
+        while halving and step < slabs:
+            (gram_one,) = call(plus, [(total, wide)], gram_one, gram_pair, flops=LONG)
+            gram_pair = from_slab(gram_one, step)
+            step *= 2
+
+        def spread(gram_ref, pair_ref, out_ref):
+            value = gram_ref[...] + pair_ref[...]
+            r = lax.broadcasted_iota(jnp.int32, (total, wide), 0)
+            c = lax.broadcasted_iota(jnp.int32, (total, wide), 1)
+            diagonal = jnp.where(r * rows == c, value, 0.0)
             distance = jnp.sum(diagonal, axis=1, keepdims=True) + jnp.sum(diagonal, axis=0, keepdims=True) - 2.0 * value
+            distance = jnp.where(c % rows == 0, distance, 0.0)
             width = jnp.sum(jnp.sum(distance, axis=1, keepdims=True), axis=0, keepdims=True) / (
                 total * (total - 1) * math.log(total)
             )
-            kernel = jnp.exp(-distance / width)
+            kernel = jnp.where(c % rows == 0, jnp.exp(-distance / width), 0.0)
             kernel = kernel / jnp.sum(kernel, axis=1, keepdims=True)
             for j in range(total):
                 for i in range(count):
-                    out_ref[j, i] = jnp.broadcast_to(kernel[i : i + 1, j : j + 1], (rows, columns))
-
-        (spread_kernel,) = call(spread, [(total, count, rows, columns)], gram_full)
-
-        def weigh(kernel_ref, start, pulled, z, values):
+                    out_ref[j, i] = jnp.broadcast_to(kernel[i : i + 1, j * rows : j * rows + 1], (rows, columns))
+
+        (spread_kernel,) = call(spread, [(total, count, rows, columns)], gram_one, gram_pair, flops=LONG)
+
+        def weigh(kernel_ref, start, pulled, values):
             for j in range(len(values)):
                 for i in range(count):
                     pulled[i] = pulled[i] + kernel_ref[start + j, i] * values[j]
             return pulled
 
-        def last_base(kernel_ref, pull_ref, pair_ref, *refs):
-            *model_refs, out_ref = refs
-            both = PRIOR_WEIGHT + REPEL_WEIGHT
+        def last_base(kernel_ref, pull_ref, pair_ref, models_ref, out_ref):
             for at in at_plane:
-                pulled = [REPEL_WEIGHT * model_refs[0][i, at] for i in range(count)]
-                own = [pull_ref[j, at] + pair_ref[j, at] - both * model_refs[0][j, at] for j in range(count)]
-                pulled = weigh(kernel_ref, 0, pulled, at, own)
-                for k in range(1, doms):
-                    pulled = weigh(kernel_ref, k * count, pulled, at, [-both * model_refs[k][j, at] for j in range(count)])
+                pulled = [REPEL_WEIGHT * models_ref[i, at] for i in range(count)]
+                pulled = weigh(kernel_ref, 0, pulled, [pull_ref[j, at] + pair_ref[j, at] for j in range(count)])
                 for i in range(count):
                     out_ref[i, at] = pulled[i]
 
-        (update_base,) = call(last_base, [stack], spread_kernel, pull, pull_pair, models, *others)
-
-        def others_pull(kernel_ref, *refs):
+        (update_base,) = call(last_base, [stack], spread_kernel, pull, pull_pair, models)
+
+        def last(kernel_ref, base_ref, *refs):
             *pulls, out_ref = refs
             for at in at_plane:
-                pulled = [jnp.zeros((rows, columns), F32)] * count
-                for k, block in enumerate(pulls):
-                    pulled = weigh(kernel_ref, (k + 1) * count, pulled, at, [block[j, at] for j in range(count)])
+                pulled = [base_ref[i, at] for i in range(count)]
+                for k in range(1, doms):
+                    here, there = pulls[k - 1], pulls[doms - 1 + k - 1]
+                    pulled = weigh(kernel_ref, k * count, pulled, [here[j, at] + there[j, at] for j in range(count)])
                 for i in range(count):
                     out_ref[i, at] = pulled[i]
 
-        (far_pull,) = call(others_pull, [stack], spread_kernel, *far_pulls)
-
-        def last(base_ref, pull_ref, pair_ref, out_ref):
-            out_ref[...] = base_ref[...] + (pull_ref[...] + pair_ref[...])
-
-        (update,) = call(last, [stack], update_base, far_pull, other_shot(far_pull))
+        (update,) = call(last, [stack], spread_kernel, update_base, *far_pulls, *far_pairs)
         return update.reshape(particles.shape)
 
     placed = (

time: 31.1 us -> 28.9 us (0.929)
  waiting for transfers between devices: 7 us -> 2.54 us
  starting transfers between devices: 16.3 us -> 19.2 us
  Pallas kernels: 6.88 us -> 6.29 us
    ppermute x2, waiting for transfers between devices: 2.31 us -> 0.01 us  [from_slab(): return lax.ppermute(block, 'slab', [(i, i ^ step) for i in range(slabs)])]
    ppermute x2, waiting for transfers between devices: 3.58 us -> 1.34 us  [from_dom(): lax.ppermute(block, 'dom', [((i + distance) % doms, i) for i in range(dom...]
    ppermute x4, starting transfers between devices: 0.52 us -> 2.68 us  [exchange(): lax.ppermute(block, ('slab', 'shot'), down)]
    ppermute x4, starting transfers between devices: 8.66 us -> 7.51 us  [exchange(): lax.ppermute(block, ('slab', 'shot'), up)]
    ppermute x2, starting transfers between devices: 4.17 us -> 5.04 us  [from_slab(): return lax.ppermute(block, 'slab', [(i, i ^ step) for i in range(slabs)])]
    ppermute x2, starting transfers between devices: 2.83 us -> 3.61 us  [from_dom(): lax.ppermute(block, 'dom', [((i + distance) % doms, i) for i in range(dom...]
    ppermute x2, waiting for transfers between devices: 1.09 us -> 0.37 us  [other_shot(): return lax.ppermute(block, 'shot', [(0, 1), (1, 0)])]
    pallas_call x12, Pallas kernels: 6.88 us -> 6.29 us  [call(): pl.pallas_call(body, out_shape=outs, in_specs=[pl.BlockSpec(memory_space=...]
where the time goes in v3:
time: 28.9 us; the launch traced here: 28.8 us
  starting transfers between devices  19.2 us (66%)
  Pallas kernels  6.29 us (22%)
  waiting for transfers between devices  2.54 us (9%)
  between operations  0.76 us (3%)
    ppermute x4, starting transfers between devices, exchange(): lax.ppermute(block, ('slab', 'shot'), up)  7.51 us
    pallas_call x12, Pallas kernels, call(): pl.pallas_call(body, out_shape=outs, in_specs=[pl.BlockSpec(memory_space=...  6.29 us
    ppermute x2, starting transfers between devices, from_slab(): return lax.ppermute(block, 'slab', [(i, i ^ step) for i in range(slabs)])  5.04 us
    ppermute x2, starting transfers between devices, from_dom(): lax.ppermute(block, 'dom', [((i + distance) % doms, i) for i in range(dom...  3.61 us
    ppermute x4, starting transfers between devices, exchange(): lax.ppermute(block, ('slab', 'shot'), down)  2.68 us
    ppermute x2, waiting for transfers between devices, from_dom(): lax.ppermute(block, 'dom', [((i + distance) % doms, i) for i in range(dom...  1.34 us
  transfers between devices with their start and end apart: 14, of which 4 were waited for; matrix products, arithmetic and copies ran while one was open for 0% of the time, Pallas kernels for 16%

profile of v3, /device:TPU:0, one launch (start us, length us, event | category | flops | bytes accessed | tf_op | source)
XLA Modules:
  0.0 28.8 jit_solution(2207972527878934888)
XLA Ops:
  0.0 1.0 %shard_map.100 = (f32[8,32,128]{2,1,0:T(8,128)S(1)}, f32[8,32,128]{2,1,0:T(8,128)S(1)}, f32[8,32,128]{2,1,0:T(8,128)S(1)}, f32[8,32,128]{2,1,0:T(8,128)S(1)}, bf16[8,32,128]{2,1,0:T(8,128)(2,1)S(1)}) custom-call(bf16[8,32,128]{2,1,0:T(8,128)(2,1)} %bitcast.11, f32[8,32,128]{2,1,0:T(8,128)} %bitcast.10, f32[32,128]{1,0:T(8,128)} %bitcast.15, ...), custom_call_target="tpu_custom_call" | custom-call | flops 1048576 | bytes 278528 | tf_op jit(solution)/shard_map/pallas_call | solution.py:26
  1.1 0.5 %collective-permute-start.1 = (f32[8,32,128]{2,1,0:T(8,128)S(1)}, f32[8,32,128]{2,1,0:T(8,128)S(1)}, u32[]{:S(2)}, u32[]{:S(2)}) collective-permute-start(f32[8,32,128]{2,1,0:T(8,128)S(1)} %get-tuple-element.23.refs_6_.one_ref), channel_id=1, source_target_pairs={{4,0},{8,4},{12,8},{13,12},{1,5},{5,9},{9,13},{0,1},{6,2},{10,6},{... | collective-permute-start | bytes 393224 | tf_op jit(solution)/shard_map/ppermute | solution.py:126
  1.5 2.6 %collective-permute-start = (f32[8,32,128]{2,1,0:T(8,128)S(1)}, f32[8,32,128]{2,1,0:T(8,128)S(1)}, u32[]{:S(2)}, u32[]{:S(2)}) collective-permute-start(f32[8,32,128]{2,1,0:T(8,128)S(1)} %get-tuple-element.23.refs_6_.one_ref), channel_id=1, source_target_pairs={{0,4},{4,8},{8,12},{12,13},{5,1},{9,5},{13,9},{1,0},{2,6},{6,10},{... | collective-permute-start | bytes 393224 | tf_op jit(solution)/shard_map/ppermute | solution.py:126
  4.1 0.0 collective-permute-start.8
  4.1 2.0 %collective-permute-start.7 = (f32[8,32,128]{2,1,0:T(8,128)S(1)}, f32[8,32,128]{2,1,0:T(8,128)S(1)}, u32[]{:S(2)}, u32[]{:S(2)}) collective-permute-start(f32[8,32,128]{2,1,0:T(8,128)S(1)} %get-tuple-element.30.moved_ref), channel_id=1, source_target_pairs={{0,4},{4,8},{8,12},{12,13},{5,1},{9,5},{13,9},{1,0},{2,6},{6,10},{... | collective-permute-start | bytes 393224 | tf_op jit(solution)/shard_map/ppermute | solution.py:126
  6.8 1.2 %shard_map.101 = (f32[8,32,128]{2,1,0:T(8,128)S(1)}, f32[160,128]{1,0:T(8,128)S(1)}, bf16[8,32,128]{2,1,0:T(8,128)(2,1)S(1)}, bf16[8,32,128]{2,1,0:T(8,128)(2,1)S(1)}) custom-call(bf16[8,32,128]{2,1,0:T(8,128)(2,1)} %bitcast.13, bf16[8,32,128]{2,1,0:T(8,128)(2,1)} %bitcast.14, f32[1,2]{1,0:T(1,128)} %refs_2_.1, s32[1,128]{1,0:T(1,128)} %refs_3_.1, ...), custom_call_target="tpu_custom_call" | custom-call | flops 1048576 | bytes 267784 | tf_op jit(solution)/shard_map/pallas_call | solution.py:26
  8.0 0.0 collective-permute-done.1.second
  8.0 0.0 collective-permute-done.first
  8.0 0.1 shard_map.102
  8.2 1.1 %collective-permute-start.6 = (f32[8,32,128]{2,1,0:T(8,128)S(1)}, f32[8,32,128]{2,1,0:T(8,128)S(1)}, u32[]{:S(2)}, u32[]{:S(2)}) collective-permute-start(f32[8,32,128]{2,1,0:T(8,128)S(1)} %get-tuple-element.29.two_ref), channel_id=1, source_target_pairs={{4,0},{8,4},{12,8},{13,12},{1,5},{5,9},{9,13},{0,1},{6,2},{10,6},{... | collective-permute-start | bytes 393224 | tf_op jit(solution)/shard_map/ppermute | solution.py:126
  9.3 1.4 %collective-permute-start.5 = (f32[8,32,128]{2,1,0:T(8,128)S(1)}, f32[8,32,128]{2,1,0:T(8,128)S(1)}, u32[]{:S(2)}, u32[]{:S(2)}) collective-permute-start(f32[8,32,128]{2,1,0:T(8,128)S(1)} %get-tuple-element.29.two_ref), channel_id=1, source_target_pairs={{0,4},{4,8},{8,12},{12,13},{5,1},{9,5},{13,9},{1,0},{2,6},{6,10},{... | collective-permute-start | bytes 393224 | tf_op jit(solution)/shard_map/ppermute | solution.py:126
  10.7 1.8 %collective-permute-start.2 = (f32[8,32,128]{2,1,0:T(8,128)S(1)}, f32[8,32,128]{2,1,0:T(8,128)S(1)}, u32[]{:S(2)}, u32[]{:S(2)}) collective-permute-start(f32[8,32,128]{2,1,0:T(8,128)S(1)} %get-tuple-element.28), channel_id=1, source_target_pairs={{2,0},{0,2},{3,1},{1,3},{6,4},{4,6},{7,5},{5,7},{10,8},{8,10},{11,... | collective-permute-start | bytes 393224 | tf_op jit(solution)/shard_map/ppermute | solution.py:129
  12.5 0.0 collective-permute-done.8.second
  12.5 0.0 collective-permute-done.7.first
  12.5 1.1 %shard_map.106 = (f32[8,32,128]{2,1,0:T(8,128)S(1)}, f32[8,32,128]{2,1,0:T(8,128)S(1)}) custom-call(f32[8,32,128]{2,1,0:T(8,128)S(1)} %collective-permute-done.7.first, f32[8,32,128]{2,1,0:T(8,128)S(1)} %collective-permute-done.8.second, f32[8,32,128]{2,1,0:T(8,128)S(1)} %get-tuple-element.30.moved_ref, bf16[8,32,128]{2,1,0:T(8,128)(2,1)S(1)} %get-tuple-element.31.near_ref, ...), custom_call_target="tpu_custom_call" | custom-call | flops 1048576 | bytes 655360 | tf_op jit(solution)/shard_map/pallas_call | solution.py:26
  13.6 0.4 %collective-permute-done.6.second = f32[8,32,128]{2,1,0:T(8,128)S(1)} collective-permute-done((f32[8,32,128]{2,1,0:T(8,128)S(1)}, f32[8,32,128]{2,1,0:T(8,128)S(1)}, u32[]{:S(2)}, u32[]{:S(2)}) %collective-permute-start.6) | collective-permute-done | bytes 131104 | tf_op jit(solution)/shard_map/ppermute | solution.py:126
  14.0 0.0 collective-permute-done.5.first
  14.0 0.1 shard_map.107
  14.2 1.1 %collective-permute-start.10 = (f32[8,32,128]{2,1,0:T(8,128)S(1)}, f32[8,32,128]{2,1,0:T(8,128)S(1)}, u32[]{:S(2)}, u32[]{:S(2)}) collective-permute-start(f32[8,32,128]{2,1,0:T(8,128)S(1)} %get-tuple-element.35.moved_ref), channel_id=1, source_target_pairs={{4,0},{8,4},{12,8},{13,12},{1,5},{5,9},{9,13},{0,1},{6,2},{10,6},{... | collective-permute-start | bytes 393224 | tf_op jit(solution)/shard_map/ppermute | solution.py:126
  15.3 1.5 %collective-permute-start.9 = (f32[8,32,128]{2,1,0:T(8,128)S(1)}, f32[8,32,128]{2,1,0:T(8,128)S(1)}, u32[]{:S(2)}, u32[]{:S(2)}) collective-permute-start(f32[8,32,128]{2,1,0:T(8,128)S(1)} %get-tuple-element.35.moved_ref), channel_id=1, source_target_pairs={{0,4},{4,8},{8,12},{12,13},{5,1},{9,5},{13,9},{1,0},{2,6},{6,10},{... | collective-permute-start | bytes 393224 | tf_op jit(solution)/shard_map/ppermute | solution.py:126
  16.7 0.0 collective-permute-done.2.refs_1_
  16.7 0.6 %shard_map.103.first_ref = f32[16,128]{1,0:T(8,128)S(1)} custom-call(f32[8,32,128]{2,1,0:T(8,128)S(1)} %get-tuple-element.22.models_ref.refs_0_, f32[8,32,128]{2,1,0:T(8,128)S(1)} %collective-permute-done.2.refs_1_), custom_call_target="tpu_custom_call" | custom-call | flops 1048576 | bytes 262144 | tf_op jit(solution)/shard_map/pallas_call | solution.py:26
  17.3 2.0 %collective-permute-start.3 = (f32[16,128]{1,0:T(8,128)S(1)}, f32[16,128]{1,0:T(8,128)S(1)}, u32[]{:S(2)}, u32[]{:S(2)}) collective-permute-start(f32[16,128]{1,0:T(8,128)S(1)} %shard_map.103.first_ref), channel_id=1, source_target_pairs={{0,4},{4,0},{8,12},{12,8},{1,5},{5,1},{9,13},{13,9},{2,6},{6,2},{1... | collective-permute-start | bytes 24584 | tf_op jit(solution)/shard_map/ppermute | solution.py:139
  19.3 0.6 %shard_map.108.inner_ref = f32[8,32,128]{2,1,0:T(8,128)S(1)} custom-call(f32[160,128]{1,0:T(8,128)S(1)} %get-tuple-element.24.spots_ref, f32[8,32,128]{2,1,0:T(8,128)S(1)} %get-tuple-element.35.moved_ref, f32[8,32,128]{2,1,0:T(8,128)S(1)} %get-tuple-element.36.three_ref, bf16[8,32,128]{2,1,0:T(8,128)(2,1)S(1)} %get-tuple-element.31.near_ref, ...), custom_call_target="tpu_custom_call" | custom-call | flops 1048576 | bytes 802816 | tf_op jit(solution)/shard_map/pallas_call | solution.py:26
  19.9 0.0 collective-permute-done.10.second
  19.9 0.4 %collective-permute-done.9.first = f32[8,32,128]{2,1,0:T(8,128)S(1)} collective-permute-done((f32[8,32,128]{2,1,0:T(8,128)S(1)}, f32[8,32,128]{2,1,0:T(8,128)S(1)}, u32[]{:S(2)}, u32[]{:S(2)}) %collective-permute-start.9) | collective-permute-done | bytes 131104 | tf_op jit(solution)/shard_map/ppermute | solution.py:126
  20.3 0.1 shard_map.109.pull_ref
  20.4 1.8 %collective-permute-start.12 = (f32[8,32,128]{2,1,0:T(8,128)S(1)}, f32[8,32,128]{2,1,0:T(8,128)S(1)}, u32[]{:S(2)}, u32[]{:S(2)}) collective-permute-start(f32[8,32,128]{2,1,0:T(8,128)S(1)} %shard_map.109.pull_ref), channel_id=1, source_target_pairs={{2,0},{0,2},{3,1},{1,3},{6,4},{4,6},{7,5},{5,7},{10,8},{8,10},{11,... | collective-permute-start | bytes 393224 | tf_op jit(solution)/shard_map/ppermute | solution.py:129
  22.3 0.0 collective-permute-done.3.second_ref
  22.3 3.0 %collective-permute-start.4 = (f32[16,128]{1,0:T(8,128)S(1)}, f32[16,128]{1,0:T(8,128)S(1)}, u32[]{:S(2)}, u32[]{:S(2)}) collective-permute-start(f32[16,128]{1,0:T(8,128)S(1)} %shard_map.104.gram_ref), channel_id=1, source_target_pairs={{0,8},{4,12},{8,0},{12,4},{1,9},{5,13},{9,1},{13,5},{2,10},{6,14},... | collective-permute-start | bytes 24584 | tf_op jit(solution)/shard_map/ppermute | solution.py:139
  25.3 0.0 collective-permute-start.11
  25.3 1.3 %collective-permute-done.12.refs_0_ = f32[8,32,128]{2,1,0:T(8,128)S(1)} collective-permute-done((f32[8,32,128]{2,1,0:T(8,128)S(1)}, f32[8,32,128]{2,1,0:T(8,128)S(1)}, u32[]{:S(2)}, u32[]{:S(2)}) %collective-permute-start.12) | collective-permute-done | bytes 131104 | tf_op jit(solution)/shard_map/ppermute | solution.py:129
  26.7 0.3 %collective-permute-start.13 = (f32[8,32,128]{2,1,0:T(8,128)S(1)}, f32[8,32,128]{2,1,0:T(8,128)S(1)}, u32[]{:S(2)}, u32[]{:S(2)}) collective-permute-start(f32[8,32,128]{2,1,0:T(8,128)S(1)} %collective-permute-done.12.refs_0_), channel_id=1, source_target_pairs={{0,1},{1,0},{2,3},{3,2},{4,5},{5,4},{6,7},{7,6},{8,9},{9,8},{10,11... | collective-permute-start | bytes 393224 | tf_op jit(solution)/shard_map/ppermute | solution.py:132
  27.0 0.0 collective-permute-done.4.pair_ref
  27.0 0.5 %shard_map.105.kernel_ref = f32[16,8,8,128]{3,2,1,0:T(8,128)S(1)} custom-call(f32[16,128]{1,0:T(8,128)S(1)} %shard_map.104.gram_ref, f32[16,128]{1,0:T(8,128)S(1)} %collective-permute-done.4.pair_ref), custom_call_target="tpu_custom_call" | custom-call | flops 8589934592 | bytes 16384 | tf_op jit(solution)/shard_map/pallas_call | solution.py:26
  27.5 0.0 collective-permute-done.11.pair_ref
  27.5 0.1 shard_map.110.base_ref
  27.6 0.4 %collective-permute-done.13.refs_1_ = f32[8,32,128]{2,1,0:T(8,128)S(1)} collective-permute-done((f32[8,32,128]{2,1,0:T(8,128)S(1)}, f32[8,32,128]{2,1,0:T(8,128)S(1)}, u32[]{:S(2)}, u32[]{:S(2)}) %collective-permute-start.13) | collective-permute-done | bytes 131104 | tf_op jit(solution)/shard_map/ppermute | solution.py:132
  28.0 0.8 %shard_map.111 = f32[8,32,128]{2,1,0:T(8,128)} custom-call(f32[16,8,8,128]{3,2,1,0:T(8,128)S(1)} %shard_map.105.kernel_ref, f32[8,32,128]{2,1,0:T(8,128)S(1)} %shard_map.110.base_ref, f32[8,32,128]{2,1,0:T(8,128)S(1)} %collective-permute-done.12.refs_0_, f32[8,32,128]{2,1,0:T(8,128)S(1)} %collective-permute-done.13.refs_1_), custom_call_target="tpu_custom_call" | custom-call | flops 1048576 | bytes 917504 | tf_op jit(solution)/shard_map/pallas_call | solution.py:26
  (2 shorter events, 0.0 us)
Async XLA Ops:
  1.1 6.9 %collective-permute-start.1 = (f32[8,32,128]{2,1,0:T(8,128)S(1)}, f32[8,32,128]{2,1,0:T(8,128)S(1)}, u32[]{:S(2)}, u32[]{:S(2)}) collective-permute-start(f32[8,32,128]{2,1,0:T(8,128)S(1)} %get-tuple-element.23.refs_6_.one_ref), channel_id=1, source_target_pairs={{4,0},{8,4},{12,8},{13,12},{1,5},{5,9},{9,13},{0,1},{6,2},{10,6},{... | collective-permute-start | bytes 393224 | tf_op jit(solution)/shard_map/ppermute | solution.py:126
  1.5 6.5 %collective-permute-start = (f32[8,32,128]{2,1,0:T(8,128)S(1)}, f32[8,32,128]{2,1,0:T(8,128)S(1)}, u32[]{:S(2)}, u32[]{:S(2)}) collective-permute-start(f32[8,32,128]{2,1,0:T(8,128)S(1)} %get-tuple-element.23.refs_6_.one_ref), channel_id=1, source_target_pairs={{0,4},{4,8},{8,12},{12,13},{5,1},{9,5},{13,9},{1,0},{2,6},{6,10},{... | collective-permute-start | bytes 393224 | tf_op jit(solution)/shard_map/ppermute | solution.py:126
  4.1 8.3 %collective-permute-start.8 = (f32[8,32,128]{2,1,0:T(8,128)S(1)}, f32[8,32,128]{2,1,0:T(8,128)S(1)}, u32[]{:S(2)}, u32[]{:S(2)}) collective-permute-start(f32[8,32,128]{2,1,0:T(8,128)S(1)} %get-tuple-element.30.moved_ref), channel_id=1, source_target_pairs={{4,0},{8,4},{12,8},{13,12},{1,5},{5,9},{9,13},{0,1},{6,2},{10,6},{... | collective-permute-start | bytes 393224 | tf_op jit(solution)/shard_map/ppermute | solution.py:126
  4.1 8.3 %collective-permute-start.7 = (f32[8,32,128]{2,1,0:T(8,128)S(1)}, f32[8,32,128]{2,1,0:T(8,128)S(1)}, u32[]{:S(2)}, u32[]{:S(2)}) collective-permute-start(f32[8,32,128]{2,1,0:T(8,128)S(1)} %get-tuple-element.30.moved_ref), channel_id=1, source_target_pairs={{0,4},{4,8},{8,12},{12,13},{5,1},{9,5},{13,9},{1,0},{2,6},{6,10},{... | collective-permute-start | bytes 393224 | tf_op jit(solution)/shard_map/ppermute | solution.py:126
  8.2 5.9 %collective-permute-start.6 = (f32[8,32,128]{2,1,0:T(8,128)S(1)}, f32[8,32,128]{2,1,0:T(8,128)S(1)}, u32[]{:S(2)}, u32[]{:S(2)}) collective-permute-start(f32[8,32,128]{2,1,0:T(8,128)S(1)} %get-tuple-element.29.two_ref), channel_id=1, source_target_pairs={{4,0},{8,4},{12,8},{13,12},{1,5},{5,9},{9,13},{0,1},{6,2},{10,6},{... | collective-permute-start | bytes 393224 | tf_op jit(solution)/shard_map/ppermute | solution.py:126
  9.3 4.8 %collective-permute-start.5 = (f32[8,32,128]{2,1,0:T(8,128)S(1)}, f32[8,32,128]{2,1,0:T(8,128)S(1)}, u32[]{:S(2)}, u32[]{:S(2)}) collective-permute-start(f32[8,32,128]{2,1,0:T(8,128)S(1)} %get-tuple-element.29.two_ref), channel_id=1, source_target_pairs={{0,4},{4,8},{8,12},{12,13},{5,1},{9,5},{13,9},{1,0},{2,6},{6,10},{... | collective-permute-start | bytes 393224 | tf_op jit(solution)/shard_map/ppermute | solution.py:126
  10.7 6.0 %collective-permute-start.2 = (f32[8,32,128]{2,1,0:T(8,128)S(1)}, f32[8,32,128]{2,1,0:T(8,128)S(1)}, u32[]{:S(2)}, u32[]{:S(2)}) collective-permute-start(f32[8,32,128]{2,1,0:T(8,128)S(1)} %get-tuple-element.28), channel_id=1, source_target_pairs={{2,0},{0,2},{3,1},{1,3},{6,4},{4,6},{7,5},{5,7},{10,8},{8,10},{11,... | collective-permute-start | bytes 393224 | tf_op jit(solution)/shard_map/ppermute | solution.py:129
  14.2 5.8 %collective-permute-start.10 = (f32[8,32,128]{2,1,0:T(8,128)S(1)}, f32[8,32,128]{2,1,0:T(8,128)S(1)}, u32[]{:S(2)}, u32[]{:S(2)}) collective-permute-start(f32[8,32,128]{2,1,0:T(8,128)S(1)} %get-tuple-element.35.moved_ref), channel_id=1, source_target_pairs={{4,0},{8,4},{12,8},{13,12},{1,5},{5,9},{9,13},{0,1},{6,2},{10,6},{... | collective-permute-start | bytes 393224 | tf_op jit(solution)/shard_map/ppermute | solution.py:126
  15.3 5.0 %collective-permute-start.9 = (f32[8,32,128]{2,1,0:T(8,128)S(1)}, f32[8,32,128]{2,1,0:T(8,128)S(1)}, u32[]{:S(2)}, u32[]{:S(2)}) collective-permute-start(f32[8,32,128]{2,1,0:T(8,128)S(1)} %get-tuple-element.35.moved_ref), channel_id=1, source_target_pairs={{0,4},{4,8},{8,12},{12,13},{5,1},{9,5},{13,9},{1,0},{2,6},{6,10},{... | collective-permute-start | bytes 393224 | tf_op jit(solution)/shard_map/ppermute | solution.py:126
  17.3 4.9 %collective-permute-start.3 = (f32[16,128]{1,0:T(8,128)S(1)}, f32[16,128]{1,0:T(8,128)S(1)}, u32[]{:S(2)}, u32[]{:S(2)}) collective-permute-start(f32[16,128]{1,0:T(8,128)S(1)} %shard_map.103.first_ref), channel_id=1, source_target_pairs={{0,4},{4,0},{8,12},{12,8},{1,5},{5,1},{9,13},{13,9},{2,6},{6,2},{1... | collective-permute-start | bytes 24584 | tf_op jit(solution)/shard_map/ppermute | solution.py:139
  20.4 6.2 %collective-permute-start.12 = (f32[8,32,128]{2,1,0:T(8,128)S(1)}, f32[8,32,128]{2,1,0:T(8,128)S(1)}, u32[]{:S(2)}, u32[]{:S(2)}) collective-permute-start(f32[8,32,128]{2,1,0:T(8,128)S(1)} %shard_map.109.pull_ref), channel_id=1, source_target_pairs={{2,0},{0,2},{3,1},{1,3},{6,4},{4,6},{7,5},{5,7},{10,8},{8,10},{11,... | collective-permute-start | bytes 393224 | tf_op jit(solution)/shard_map/ppermute | solution.py:129
  22.3 4.7 %collective-permute-start.4 = (f32[16,128]{1,0:T(8,128)S(1)}, f32[16,128]{1,0:T(8,128)S(1)}, u32[]{:S(2)}, u32[]{:S(2)}) collective-permute-start(f32[16,128]{1,0:T(8,128)S(1)} %shard_map.104.gram_ref), channel_id=1, source_target_pairs={{0,8},{4,12},{8,0},{12,4},{1,9},{5,13},{9,1},{13,5},{2,10},{6,14},... | collective-permute-start | bytes 24584 | tf_op jit(solution)/shard_map/ppermute | solution.py:139
  25.3 2.2 %collective-permute-start.11 = (f32[8,32,128]{2,1,0:T(8,128)S(1)}, f32[8,32,128]{2,1,0:T(8,128)S(1)}, u32[]{:S(2)}, u32[]{:S(2)}) collective-permute-start(f32[8,32,128]{2,1,0:T(8,128)S(1)} %shard_map.109.pull_ref), channel_id=1, source_target_pairs={{0,1},{1,0},{2,3},{3,2},{4,5},{5,4},{6,7},{7,6},{8,9},{9,8},{10,11... | collective-permute-start | bytes 393224 | tf_op jit(solution)/shard_map/ppermute | solution.py:132
  26.7 1.3 %collective-permute-start.13 = (f32[8,32,128]{2,1,0:T(8,128)S(1)}, f32[8,32,128]{2,1,0:T(8,128)S(1)}, u32[]{:S(2)}, u32[]{:S(2)}) collective-permute-start(f32[8,32,128]{2,1,0:T(8,128)S(1)} %collective-permute-done.12.refs_0_), channel_id=1, source_target_pairs={{0,1},{1,0},{2,3},{3,2},{4,5},{5,4},{6,7},{7,6},{8,9},{9,8},{10,11... | collective-permute-start | bytes 393224 | tf_op jit(solution)/shard_map/ppermute | solution.py:132

commit v4 on v3

--- a/solution.py
+++ b/solution.py
@@ -90,10 +90,10 @@
     return [block[z * rows : (z + 1) * rows] for z in range(block.shape[0] // rows)]
 
 
-def side_masks(rows, columns):
+def side_masks(rows, columns, flip=False):
     slab = jnp.full((rows, columns), lax.axis_index("slab"), jnp.int32)
     shot = jnp.full((rows, columns), lax.axis_index("shot"), jnp.int32)
-    return shot > 0, slab > 0, slab < lax.axis_size("slab") - 1
+    return (shot == 0 if flip else shot > 0), slab > 0, slab < lax.axis_size("slab") - 1
 
 
 def sides(masks, first, second, rows, p):
@@ -122,8 +122,9 @@
     up += [(2 * z + 1, 2 * z - 1) for z in range(1, slabs)] + [(1, 0)]
     down = [(b, a) for a, b in up]
 
-    def exchange(block):
-        return lax.ppermute(block, ("slab", "shot"), up), lax.ppermute(block, ("slab", "shot"), down)
+    def exchange(block, flip=False):
+        ways = (down, up) if flip else (up, down)
+        return [lax.ppermute(block, ("slab", "shot"), way) for way in ways]
 
     def from_dom(block, distance):
         return lax.ppermute(block, "dom", [((i + distance) % doms, i) for i in range(doms)])
@@ -163,11 +164,17 @@
 
         halves = jax.ShapeDtypeStruct(stack, one.dtype)
 
-        def prepare(one_hbm, models_hbm, ground_hbm, near_hbm, wave_ref, squared_ref, moved_ref, models_ref, near_ref, one_ref, ground_ref, arrived):
-            copies = fetch(
-                (one_hbm, models_hbm, ground_hbm, near_hbm), (one_ref, models_ref, ground_ref, near_ref), arrived
-            )
-            for copy in copies:
+        small = (wavelet, receivers, observed.reshape(2, -1))
+
+        def prepare(*refs):
+            sources_hbm, (wave_ref, squared_ref, moved_ref, models_ref, *kept), (one_ref, ground_ref, arrived) = (
+                refs[:9],
+                refs[9:19],
+                refs[19:],
+            )
+            near_ref = kept[0]
+            copies = fetch(sources_hbm, (one_ref, models_ref, ground_ref, *kept), arrived)
+            for copy in copies[:4]:
                 copy.wait()
 
             def particle(p):
@@ -177,28 +184,30 @@
                 moved_ref[p] = squared * near_ref[p].astype(F32)
 
             loop(count, particle)
-
-        wave_one, squared, near_moved, models, near = call(
+            for copy in copies[4:]:
+                copy.wait()
+
+        wave_one, squared, near_moved, models, near, zero, far, *small = call(
             prepare,
-            [stack] * 4 + [halves],
+            [stack] * 4 + [halves] * 3 + [jax.ShapeDtypeStruct(x.shape, x.dtype) for x in small],
             one,
             models,
             ground,
             near,
-            far=4,
+            zero,
+            far,
+            *small,
+            far=9,
             scratch=[
                 pltpu.VMEM(stack, one.dtype),
                 pltpu.VMEM((depth, columns), F32),
-                pltpu.SemaphoreType.DMA((4,)),
+                pltpu.SemaphoreType.DMA((9,)),
             ],
         )
-        one_first, one_second = exchange(wave_one)
-        near_first, near_second = exchange(near_moved)
-
-        def first_base(*refs):
-            far_away, (source_ref, one_ref, inner_out, spots_out), held = refs[:5], refs[5:9], refs[9:14]
-            wavelet_ref, receiver_ref, observed_ref = held[2:]
-            copies = fetch(far_away, held, refs[14])
+        one_first, one_second = exchange(wave_one, flip=True)
+        near_first, near_second = exchange(near_moved, flip=True)
+
+        def first_base(source_ref, wavelet_ref, receiver_ref, observed_ref, one_ref, inner_out, spots_out):
             weights = plane_weights(rows, columns)
 
             def particle(p):
@@ -206,8 +215,6 @@
                     inner_out[p, at] = plane
 
             loop(count, particle)
-            for copy in copies:
-                copy.wait()
             first_row = lax.axis_index("slab") * depth
             cells = receiver_ref[...]
             row = lax.shift_right_logical(cells, columns.bit_length() - 1) - first_row
@@ -230,17 +237,12 @@
             spots_out[3 * depth : 4 * depth] = jnp.where(at_source, wavelet_ref[:, 0:1], 0.0)
             spots_out[4 * depth : 5 * depth] = jnp.where(at_source, wavelet_ref[:, 1:2], 0.0)
 
-        small = (wavelet, receivers, observed.reshape(2, -1))
-        one_inner, spots, zero, far = call(
+        one_inner, spots = call(
             first_base,
-            [stack, (5 * depth, columns), halves, halves],
-            zero,
-            far,
+            [stack, (5 * depth, columns)],
+            jnp.broadcast_to(sources[:, None], (rows, columns)),
             *small,
-            jnp.broadcast_to(sources[:, None], (rows, columns)),
             wave_one,
-            far=5,
-            scratch=[pltpu.VMEM(x.shape, x.dtype) for x in small] + [pltpu.SemaphoreType.DMA((5,))],
         )
 
         def spot(spots_ref, kind, z):
@@ -250,7 +252,7 @@
             spots_ref, first, second, inner_ref, one_ref, zero_ref, squared_ref, models_ref, lap_out, wave_out, models_out
         ):
             models_out[...] = models_ref[...]
-            masks = side_masks(rows, columns)
+            masks = side_masks(rows, columns, flip=True)
 
             def particle(p):
                 below, above = sides(masks, first, second, rows, p)
@@ -271,7 +273,7 @@
 
         def second_base(first, second, moved_ref, near_ref, far_ref, two_ref, base_out, inner_out):
             weights = plane_weights(rows, columns)
-            masks = side_masks(rows, columns)
+            masks = side_masks(rows, columns, flip=True)
 
             def waves(p):
                 for at, plane in zip(at_plane, inner_laplace(planes_of(two_ref[p], rows), weights)):

time: 28.9 us -> 28.6 us (0.990)
  starting transfers between devices: 19.2 us -> 17 us
  waiting for transfers between devices: 2.54 us -> 4.66 us
  Pallas kernels: 6.29 us -> 5.97 us
    ppermute x8, waiting for transfers between devices: 0.83 us -> 2.77 us  [exchange(): return [lax.ppermute(block, ('slab', 'shot'), way) for way in ways]]
    ppermute x8, starting transfers between devices: 10.2 us -> 9.16 us  [exchange(): return [lax.ppermute(block, ('slab', 'shot'), way) for way in ways]]
    ppermute x2, waiting for transfers between devices: 0.01 us -> 0.74 us  [from_slab(): return lax.ppermute(block, 'slab', [(i, i ^ step) for i in range(slabs)])]
    ppermute x2, starting transfers between devices: 3.61 us -> 3.19 us  [from_dom(): lax.ppermute(block, 'dom', [((i + distance) % doms, i) for i in range(dom...]
    ppermute x2, starting transfers between devices: 5.04 us -> 4.66 us  [from_slab(): return lax.ppermute(block, 'slab', [(i, i ^ step) for i in range(slabs)])]
    ppermute x2, waiting for transfers between devices: 0.37 us -> 0.01 us  [other_shot(): return lax.ppermute(block, 'shot', [(0, 1), (1, 0)])]
    ppermute x2, starting transfers between devices: 0.33 us -> 0.01 us  [other_shot(): return lax.ppermute(block, 'shot', [(0, 1), (1, 0)])]
    pallas_call x12, Pallas kernels: 6.29 us -> 5.97 us  [call(): pl.pallas_call(body, out_shape=outs, in_specs=[pl.BlockSpec(memory_space=...]
  transfers between devices with their start and end apart: 14 -> 14, of which waited for: 4 -> 6; matrix products, arithmetic and copies ran while one was open for 0% -> 0% of each run, Pallas kernels for 16% -> 14%
where the time goes in v4:
time: 28.6 us; the launch traced here: 28.4 us
  starting transfers between devices  17 us (59%)
  Pallas kernels  5.97 us (21%)
  waiting for transfers between devices  4.66 us (16%)
  between operations  0.77 us (3%)
    ppermute x8, starting transfers between devices, exchange(): return [lax.ppermute(block, ('slab', 'shot'), way) for way in ways]  9.16 us
    pallas_call x12, Pallas kernels, call(): pl.pallas_call(body, out_shape=outs, in_specs=[pl.BlockSpec(memory_space=...  5.97 us
    ppermute x2, starting transfers between devices, from_slab(): return lax.ppermute(block, 'slab', [(i, i ^ step) for i in range(slabs)])  4.66 us
    ppermute x2, starting transfers between devices, from_dom(): lax.ppermute(block, 'dom', [((i + distance) % doms, i) for i in range(dom...  3.19 us
    ppermute x8, waiting for transfers between devices, exchange(): return [lax.ppermute(block, ('slab', 'shot'), way) for way in ways]  2.77 us
    ppermute x2, waiting for transfers between devices, from_dom(): lax.ppermute(block, 'dom', [((i + distance) % doms, i) for i in range(dom...  1.15 us
    ppermute x2, waiting for transfers between devices, from_slab(): return lax.ppermute(block, 'slab', [(i, i ^ step) for i in range(slabs)])  0.74 us
  transfers between devices with their start and end apart: 14, of which 6 were waited for; matrix products, arithmetic and copies ran while one was open for 0% of the time, Pallas kernels for 14%

profile of v4, /device:TPU:0, one launch (start us, length us, event | category | flops | bytes accessed | tf_op | source)
XLA Modules:
  0.0 28.4 jit_solution(8708232191278613726)
XLA Ops:
  0.0 1.1 %shard_map.100 = (f32[8,32,128]{2,1,0:T(8,128)S(1)}, f32[8,32,128]{2,1,0:T(8,128)S(1)}, f32[8,32,128]{2,1,0:T(8,128)S(1)}, f32[8,32,128]{2,1,0:T(8,128)S(1)}, bf...) custom-call(bf16[8,32,128]{2,1,0:T(8,128)(2,1)} %bitcast.11, ...), custom_call_target="tpu_custom_call" | custom-call | flops 1048576 | bytes 411144 | tf_op jit(solution)/shard_map/pallas_call | solution.py:26
  1.1 3.0 %collective-permute-start.1 = (f32[8,32,128]{2,1,0:T(8,128)S(1)}, f32[8,32,128]{2,1,0:T(8,128)S(1)}, u32[]{:S(2)}, u32[]{:S(2)}) collective-permute-start(f32[8,32,128]{2,1,0:T(8,128)S(1)} %get-tuple-element.29.one_ref), channel_id=1, source_target_pairs={{0,4},{4,8},{8,12},{12,13},{5,1},{9,5},{13,9},{1,0},{2,6},{6,10},{... | collective-permute-start | bytes 393224 | tf_op jit(solution)/shard_map/ppermute | solution.py:127
  4.1 0.0 collective-permute-start
  4.2 2.0 %collective-permute-start.8 = (f32[8,32,128]{2,1,0:T(8,128)S(1)}, f32[8,32,128]{2,1,0:T(8,128)S(1)}, u32[]{:S(2)}, u32[]{:S(2)}) collective-permute-start(f32[8,32,128]{2,1,0:T(8,128)S(1)} %get-tuple-element.36.moved_ref), channel_id=1, source_target_pairs={{0,4},{4,8},{8,12},{12,13},{5,1},{9,5},{13,9},{1,0},{2,6},{6,10},{... | collective-permute-start | bytes 393224 | tf_op jit(solution)/shard_map/ppermute | solution.py:127
  6.2 0.0 collective-permute-start.7
  6.8 0.8 %shard_map.101 = (f32[8,32,128]{2,1,0:T(8,128)S(1)}, f32[160,128]{1,0:T(8,128)S(1)}) custom-call(s32[8,128]{1,0:T(8,128)S(1)} %broadcast_in_dim.9.source_ref, f32[1,2]{1,0:T(1,128)S(1)} %get-tuple-element.26.wavelet_ref, s32[1,128]{1,0:T(1,128)S(1)} %get-tuple-element.27.receiver_ref, f32[2,128]{1,0:T(2,128)S(1)} %get-tuple-element.28.observed_ref, ...), custom_call_target="tpu_custom_call" | custom-call | flops 1048576 | bytes 136712 | tf_op jit(solution)/shard_map/pallas_call | solution.py:26
  7.7 0.4 %collective-permute-done.1.second = f32[8,32,128]{2,1,0:T(8,128)S(1)} collective-permute-done((f32[8,32,128]{2,1,0:T(8,128)S(1)}, f32[8,32,128]{2,1,0:T(8,128)S(1)}, u32[]{:S(2)}, u32[]{:S(2)}) %collective-permute-start.1) | collective-permute-done | bytes 131104 | tf_op jit(solution)/shard_map/ppermute | solution.py:127
  8.0 1.1 %collective-permute-done.first = f32[8,32,128]{2,1,0:T(8,128)S(1)} collective-permute-done((f32[8,32,128]{2,1,0:T(8,128)S(1)}, f32[8,32,128]{2,1,0:T(8,128)S(1)}, u32[]{:S(2)}, u32[]{:S(2)}) %collective-permute-start) | collective-permute-done | bytes 131104 | tf_op jit(solution)/shard_map/ppermute | solution.py:127
  9.1 0.1 shard_map.102
  9.3 0.0 collective-permute-start.6
  9.3 2.0 %collective-permute-start.5 = (f32[8,32,128]{2,1,0:T(8,128)S(1)}, f32[8,32,128]{2,1,0:T(8,128)S(1)}, u32[]{:S(2)}, u32[]{:S(2)}) collective-permute-start(f32[8,32,128]{2,1,0:T(8,128)S(1)} %get-tuple-element.35.two_ref), channel_id=1, source_target_pairs={{0,4},{4,8},{8,12},{12,13},{5,1},{9,5},{13,9},{1,0},{2,6},{6,10},{... | collective-permute-start | bytes 393224 | tf_op jit(solution)/shard_map/ppermute | solution.py:127
  11.3 1.6 %collective-permute-start.2 = (f32[8,32,128]{2,1,0:T(8,128)S(1)}, f32[8,32,128]{2,1,0:T(8,128)S(1)}, u32[]{:S(2)}, u32[]{:S(2)}) collective-permute-start(f32[8,32,128]{2,1,0:T(8,128)S(1)} %get-tuple-element.34), channel_id=1, source_target_pairs={{2,0},{0,2},{3,1},{1,3},{6,4},{4,6},{7,5},{5,7},{10,8},{8,10},{11,... | collective-permute-start | bytes 393224 | tf_op jit(solution)/shard_map/ppermute | solution.py:130
  12.9 0.0 collective-permute-done.8.second
  12.9 0.0 collective-permute-done.7.first
  12.9 1.1 %shard_map.106 = (f32[8,32,128]{2,1,0:T(8,128)S(1)}, f32[8,32,128]{2,1,0:T(8,128)S(1)}) custom-call(f32[8,32,128]{2,1,0:T(8,128)S(1)} %collective-permute-done.7.first, f32[8,32,128]{2,1,0:T(8,128)S(1)} %collective-permute-done.8.second, f32[8,32,128]{2,1,0:T(8,128)S(1)} %get-tuple-element.36.moved_ref, bf16[8,32,128]{2,1,0:T(8,128)(2,1)S(1)} %get-tuple-element.37.near_ref, ...), custom_call_target="tpu_custom_call" | custom-call | flops 1048576 | bytes 655360 | tf_op jit(solution)/shard_map/pallas_call | solution.py:26
  14.1 0.2 collective-permute-done.6.second
  14.2 0.0 collective-permute-done.5.first
  14.3 0.1 shard_map.107
  14.4 0.0 collective-permute-start.10
  14.4 2.0 %collective-permute-start.9 = (f32[8,32,128]{2,1,0:T(8,128)S(1)}, f32[8,32,128]{2,1,0:T(8,128)S(1)}, u32[]{:S(2)}, u32[]{:S(2)}) collective-permute-start(f32[8,32,128]{2,1,0:T(8,128)S(1)} %get-tuple-element.41.moved_ref), channel_id=1, source_target_pairs={{0,4},{4,8},{8,12},{12,13},{5,1},{9,5},{13,9},{1,0},{2,6},{6,10},{... | collective-permute-start | bytes 393224 | tf_op jit(solution)/shard_map/ppermute | solution.py:127
  16.5 0.0 collective-permute-done.2.refs_1_
  16.5 0.6 %shard_map.103.first_ref = f32[16,128]{1,0:T(8,128)S(1)} custom-call(f32[8,32,128]{2,1,0:T(8,128)S(1)} %get-tuple-element.25.models_ref.refs_0_, f32[8,32,128]{2,1,0:T(8,128)S(1)} %collective-permute-done.2.refs_1_), custom_call_target="tpu_custom_call" | custom-call | flops 1048576 | bytes 262144 | tf_op jit(solution)/shard_map/pallas_call | solution.py:26
  17.1 2.0 %collective-permute-start.3 = (f32[16,128]{1,0:T(8,128)S(1)}, f32[16,128]{1,0:T(8,128)S(1)}, u32[]{:S(2)}, u32[]{:S(2)}) collective-permute-start(f32[16,128]{1,0:T(8,128)S(1)} %shard_map.103.first_ref), channel_id=1, source_target_pairs={{0,4},{4,0},{8,12},{12,8},{1,5},{5,1},{9,13},{13,9},{2,6},{6,2},{1... | collective-permute-start | bytes 24584 | tf_op jit(solution)/shard_map/ppermute | solution.py:140
  19.1 0.6 %shard_map.108.inner_ref = f32[8,32,128]{2,1,0:T(8,128)S(1)} custom-call(f32[160,128]{1,0:T(8,128)S(1)} %get-tuple-element.30.spots_ref, f32[8,32,128]{2,1,0:T(8,128)S(1)} %get-tuple-element.41.moved_ref, f32[8,32,128]{2,1,0:T(8,128)S(1)} %get-tuple-element.42.three_ref, bf16[8,32,128]{2,1,0:T(8,128)(2,1)S(1)} %get-tuple-element.37.near_ref, ...), custom_call_target="tpu_custom_call" | custom-call | flops 1048576 | bytes 802816 | tf_op jit(solution)/shard_map/pallas_call | solution.py:26
  19.7 1.1 %collective-permute-done.10.second = f32[8,32,128]{2,1,0:T(8,128)S(1)} collective-permute-done((f32[8,32,128]{2,1,0:T(8,128)S(1)}, f32[8,32,128]{2,1,0:T(8,128)S(1)}, u32[]{:S(2)}, u32[]{:S(2)}) %collective-permute-start.10) | collective-permute-done | bytes 131104 | tf_op jit(solution)/shard_map/ppermute | solution.py:127
  20.8 0.0 collective-permute-done.9.first
  20.8 0.1 shard_map.109.pull_ref
  20.9 1.6 %collective-permute-start.12 = (f32[8,32,128]{2,1,0:T(8,128)S(1)}, f32[8,32,128]{2,1,0:T(8,128)S(1)}, u32[]{:S(2)}, u32[]{:S(2)}) collective-permute-start(f32[8,32,128]{2,1,0:T(8,128)S(1)} %shard_map.109.pull_ref), channel_id=1, source_target_pairs={{2,0},{0,2},{3,1},{1,3},{6,4},{4,6},{7,5},{5,7},{10,8},{8,10},{11,... | collective-permute-start | bytes 393224 | tf_op jit(solution)/shard_map/ppermute | solution.py:130
  22.4 0.0 collective-permute-done.3.second_ref
  22.4 2.7 %collective-permute-start.4 = (f32[16,128]{1,0:T(8,128)S(1)}, f32[16,128]{1,0:T(8,128)S(1)}, u32[]{:S(2)}, u32[]{:S(2)}) collective-permute-start(f32[16,128]{1,0:T(8,128)S(1)} %shard_map.104.gram_ref), channel_id=1, source_target_pairs={{0,8},{4,12},{8,0},{12,4},{1,9},{5,13},{9,1},{13,5},{2,10},{6,14},... | collective-permute-start | bytes 24584 | tf_op jit(solution)/shard_map/ppermute | solution.py:140
  25.1 0.0 collective-permute-start.11
  25.1 1.1 %collective-permute-done.12.refs_0_ = f32[8,32,128]{2,1,0:T(8,128)S(1)} collective-permute-done((f32[8,32,128]{2,1,0:T(8,128)S(1)}, f32[8,32,128]{2,1,0:T(8,128)S(1)}, u32[]{:S(2)}, u32[]{:S(2)}) %collective-permute-start.12) | collective-permute-done | bytes 131104 | tf_op jit(solution)/shard_map/ppermute | solution.py:130
  26.3 0.0 collective-permute-start.13
  26.3 0.7 %collective-permute-done.4.pair_ref = f32[16,128]{1,0:T(8,128)S(1)} collective-permute-done((f32[16,128]{1,0:T(8,128)S(1)}, f32[16,128]{1,0:T(8,128)S(1)}, u32[]{:S(2)}, u32[]{:S(2)}) %collective-permute-start.4) | collective-permute-done | bytes 8224 | tf_op jit(solution)/shard_map/ppermute | solution.py:140
  27.0 0.5 %shard_map.105.kernel_ref = f32[16,8,8,128]{3,2,1,0:T(8,128)S(1)} custom-call(f32[16,128]{1,0:T(8,128)S(1)} %shard_map.104.gram_ref, f32[16,128]{1,0:T(8,128)S(1)} %collective-permute-done.4.pair_ref), custom_call_target="tpu_custom_call" | custom-call | flops 8589934592 | bytes 16384 | tf_op jit(solution)/shard_map/pallas_call | solution.py:26
  27.5 0.0 collective-permute-done.11.pair_ref
  27.5 0.1 shard_map.110.base_ref
  27.6 0.0 collective-permute-done.13.refs_1_
  27.7 0.8 %shard_map.111 = f32[8,32,128]{2,1,0:T(8,128)} custom-call(f32[16,8,8,128]{3,2,1,0:T(8,128)S(1)} %shard_map.105.kernel_ref, f32[8,32,128]{2,1,0:T(8,128)S(1)} %shard_map.110.base_ref, f32[8,32,128]{2,1,0:T(8,128)S(1)} %collective-permute-done.12.refs_0_, f32[8,32,128]{2,1,0:T(8,128)S(1)} %collective-permute-done.13.refs_1_), custom_call_target="tpu_custom_call" | custom-call | flops 1048576 | bytes 917504 | tf_op jit(solution)/shard_map/pallas_call | solution.py:26
  (2 shorter events, 0.0 us)
Async XLA Ops:
  1.1 6.9 %collective-permute-start.1 = (f32[8,32,128]{2,1,0:T(8,128)S(1)}, f32[8,32,128]{2,1,0:T(8,128)S(1)}, u32[]{:S(2)}, u32[]{:S(2)}) collective-permute-start(f32[8,32,128]{2,1,0:T(8,128)S(1)} %get-tuple-element.29.one_ref), channel_id=1, source_target_pairs={{0,4},{4,8},{8,12},{12,13},{5,1},{9,5},{13,9},{1,0},{2,6},{6,10},{... | collective-permute-start | bytes 393224 | tf_op jit(solution)/shard_map/ppermute | solution.py:127
  4.1 5.0 %collective-permute-start = (f32[8,32,128]{2,1,0:T(8,128)S(1)}, f32[8,32,128]{2,1,0:T(8,128)S(1)}, u32[]{:S(2)}, u32[]{:S(2)}) collective-permute-start(f32[8,32,128]{2,1,0:T(8,128)S(1)} %get-tuple-element.29.one_ref), channel_id=1, source_target_pairs={{4,0},{8,4},{12,8},{13,12},{1,5},{5,9},{9,13},{0,1},{6,2},{10,6},{... | collective-permute-start | bytes 393224 | tf_op jit(solution)/shard_map/ppermute | solution.py:127
  4.2 8.8 %collective-permute-start.8 = (f32[8,32,128]{2,1,0:T(8,128)S(1)}, f32[8,32,128]{2,1,0:T(8,128)S(1)}, u32[]{:S(2)}, u32[]{:S(2)}) collective-permute-start(f32[8,32,128]{2,1,0:T(8,128)S(1)} %get-tuple-element.36.moved_ref), channel_id=1, source_target_pairs={{0,4},{4,8},{8,12},{12,13},{5,1},{9,5},{13,9},{1,0},{2,6},{6,10},{... | collective-permute-start | bytes 393224 | tf_op jit(solution)/shard_map/ppermute | solution.py:127
  6.2 6.8 %collective-permute-start.7 = (f32[8,32,128]{2,1,0:T(8,128)S(1)}, f32[8,32,128]{2,1,0:T(8,128)S(1)}, u32[]{:S(2)}, u32[]{:S(2)}) collective-permute-start(f32[8,32,128]{2,1,0:T(8,128)S(1)} %get-tuple-element.36.moved_ref), channel_id=1, source_target_pairs={{4,0},{8,4},{12,8},{13,12},{1,5},{5,9},{9,13},{0,1},{6,2},{10,6},{... | collective-permute-start | bytes 393224 | tf_op jit(solution)/shard_map/ppermute | solution.py:127
  9.3 5.0 %collective-permute-start.6 = (f32[8,32,128]{2,1,0:T(8,128)S(1)}, f32[8,32,128]{2,1,0:T(8,128)S(1)}, u32[]{:S(2)}, u32[]{:S(2)}) collective-permute-start(f32[8,32,128]{2,1,0:T(8,128)S(1)} %get-tuple-element.35.two_ref), channel_id=1, source_target_pairs={{4,0},{8,4},{12,8},{13,12},{1,5},{5,9},{9,13},{0,1},{6,2},{10,6},{... | collective-permute-start | bytes 393224 | tf_op jit(solution)/shard_map/ppermute | solution.py:127
  9.3 5.0 %collective-permute-start.5 = (f32[8,32,128]{2,1,0:T(8,128)S(1)}, f32[8,32,128]{2,1,0:T(8,128)S(1)}, u32[]{:S(2)}, u32[]{:S(2)}) collective-permute-start(f32[8,32,128]{2,1,0:T(8,128)S(1)} %get-tuple-element.35.two_ref), channel_id=1, source_target_pairs={{0,4},{4,8},{8,12},{12,13},{5,1},{9,5},{13,9},{1,0},{2,6},{6,10},{... | collective-permute-start | bytes 393224 | tf_op jit(solution)/shard_map/ppermute | solution.py:127
  11.3 5.2 %collective-permute-start.2 = (f32[8,32,128]{2,1,0:T(8,128)S(1)}, f32[8,32,128]{2,1,0:T(8,128)S(1)}, u32[]{:S(2)}, u32[]{:S(2)}) collective-permute-start(f32[8,32,128]{2,1,0:T(8,128)S(1)} %get-tuple-element.34), channel_id=1, source_target_pairs={{2,0},{0,2},{3,1},{1,3},{6,4},{4,6},{7,5},{5,7},{10,8},{8,10},{11,... | collective-permute-start | bytes 393224 | tf_op jit(solution)/shard_map/ppermute | solution.py:130
  14.4 6.4 %collective-permute-start.10 = (f32[8,32,128]{2,1,0:T(8,128)S(1)}, f32[8,32,128]{2,1,0:T(8,128)S(1)}, u32[]{:S(2)}, u32[]{:S(2)}) collective-permute-start(f32[8,32,128]{2,1,0:T(8,128)S(1)} %get-tuple-element.41.moved_ref), channel_id=1, source_target_pairs={{4,0},{8,4},{12,8},{13,12},{1,5},{5,9},{9,13},{0,1},{6,2},{10,6},{... | collective-permute-start | bytes 393224 | tf_op jit(solution)/shard_map/ppermute | solution.py:127
  14.4 6.3 %collective-permute-start.9 = (f32[8,32,128]{2,1,0:T(8,128)S(1)}, f32[8,32,128]{2,1,0:T(8,128)S(1)}, u32[]{:S(2)}, u32[]{:S(2)}) collective-permute-start(f32[8,32,128]{2,1,0:T(8,128)S(1)} %get-tuple-element.41.moved_ref), channel_id=1, source_target_pairs={{0,4},{4,8},{8,12},{12,13},{5,1},{9,5},{13,9},{1,0},{2,6},{6,10},{... | collective-permute-start | bytes 393224 | tf_op jit(solution)/shard_map/ppermute | solution.py:127
  17.1 5.4 %collective-permute-start.3 = (f32[16,128]{1,0:T(8,128)S(1)}, f32[16,128]{1,0:T(8,128)S(1)}, u32[]{:S(2)}, u32[]{:S(2)}) collective-permute-start(f32[16,128]{1,0:T(8,128)S(1)} %shard_map.103.first_ref), channel_id=1, source_target_pairs={{0,4},{4,0},{8,12},{12,8},{1,5},{5,1},{9,13},{13,9},{2,6},{6,2},{1... | collective-permute-start | bytes 24584 | tf_op jit(solution)/shard_map/ppermute | solution.py:140
  20.9 5.4 %collective-permute-start.12 = (f32[8,32,128]{2,1,0:T(8,128)S(1)}, f32[8,32,128]{2,1,0:T(8,128)S(1)}, u32[]{:S(2)}, u32[]{:S(2)}) collective-permute-start(f32[8,32,128]{2,1,0:T(8,128)S(1)} %shard_map.109.pull_ref), channel_id=1, source_target_pairs={{2,0},{0,2},{3,1},{1,3},{6,4},{4,6},{7,5},{5,7},{10,8},{8,10},{11,... | collective-permute-start | bytes 393224 | tf_op jit(solution)/shard_map/ppermute | solution.py:130
  22.4 4.6 %collective-permute-start.4 = (f32[16,128]{1,0:T(8,128)S(1)}, f32[16,128]{1,0:T(8,128)S(1)}, u32[]{:S(2)}, u32[]{:S(2)}) collective-permute-start(f32[16,128]{1,0:T(8,128)S(1)} %shard_map.104.gram_ref), channel_id=1, source_target_pairs={{0,8},{4,12},{8,0},{12,4},{1,9},{5,13},{9,1},{13,5},{2,10},{6,14},... | collective-permute-start | bytes 24584 | tf_op jit(solution)/shard_map/ppermute | solution.py:140
  25.1 2.4 %collective-permute-start.11 = (f32[8,32,128]{2,1,0:T(8,128)S(1)}, f32[8,32,128]{2,1,0:T(8,128)S(1)}, u32[]{:S(2)}, u32[]{:S(2)}) collective-permute-start(f32[8,32,128]{2,1,0:T(8,128)S(1)} %shard_map.109.pull_ref), channel_id=1, source_target_pairs={{0,1},{1,0},{2,3},{3,2},{4,5},{5,4},{6,7},{7,6},{8,9},{9,8},{10,11... | collective-permute-start | bytes 393224 | tf_op jit(solution)/shard_map/ppermute | solution.py:133
  26.3 1.4 %collective-permute-start.13 = (f32[8,32,128]{2,1,0:T(8,128)S(1)}, f32[8,32,128]{2,1,0:T(8,128)S(1)}, u32[]{:S(2)}, u32[]{:S(2)}) collective-permute-start(f32[8,32,128]{2,1,0:T(8,128)S(1)} %collective-permute-done.12.refs_0_), channel_id=1, source_target_pairs={{0,1},{1,0},{2,3},{3,2},{4,5},{5,4},{6,7},{7,6},{8,9},{9,8},{10,11... | collective-permute-start | bytes 393224 | tf_op jit(solution)/shard_map/ppermute | solution.py:133

commit v5 on v4

--- a/solution.py
+++ b/solution.py
@@ -363,7 +363,7 @@
         (gram_one,) = call(gram, [(total, wide)], models, *others)
         if not halving:
             gram_one = lax.psum(gram_one, "slab")
-        gram_pair = from_slab(gram_one, 1)
+        gram_pair = from_slab(gram_one, 2)
 
         def third_base(spots_ref, moved_ref, three_ref, near_ref, two_ref, lap_one_ref, lap_two_ref, out_ref):
             weights = plane_weights(rows, columns)
@@ -424,7 +424,7 @@
         step = 2
         while halving and step < slabs:
             (gram_one,) = call(plus, [(total, wide)], gram_one, gram_pair, flops=LONG)
-            gram_pair = from_slab(gram_one, step)
+            gram_pair = from_slab(gram_one, 1 if step == 2 else step)
             step *= 2
 
         def spread(gram_ref, pair_ref, out_ref):
@@ -440,15 +440,14 @@
             kernel = jnp.where(c % rows == 0, jnp.exp(-distance / width), 0.0)
             kernel = kernel / jnp.sum(kernel, axis=1, keepdims=True)
             for j in range(total):
-                for i in range(count):
-                    out_ref[j, i] = jnp.broadcast_to(kernel[i : i + 1, j * rows : j * rows + 1], (rows, columns))
-
-        (spread_kernel,) = call(spread, [(total, count, rows, columns)], gram_one, gram_pair, flops=LONG)
+                out_ref[j] = jnp.broadcast_to(kernel[:count, j * rows : j * rows + 1], (count, columns))
+
+        (spread_kernel,) = call(spread, [(total, count, columns)], gram_one, gram_pair, flops=LONG)
 
         def weigh(kernel_ref, start, pulled, values):
             for j in range(len(values)):
                 for i in range(count):
-                    pulled[i] = pulled[i] + kernel_ref[start + j, i] * values[j]
+                    pulled[i] = pulled[i] + kernel_ref[start + j, i : i + 1] * values[j]
             return pulled
 
         def last_base(kernel_ref, pull_ref, pair_ref, models_ref, out_ref):

time: 28.6 us -> 28.5 us (level)
    ppermute x8, waiting for transfers between devices: 2.77 us -> 1.66 us  [exchange(): return [lax.ppermute(block, ('slab', 'shot'), way) for way in ways]]
    ppermute x2, waiting for transfers between devices: 1.15 us -> 2.07 us  [from_dom(): lax.ppermute(block, 'dom', [((i + distance) % doms, i) for i in range(dom...]
    ppermute x2, waiting for transfers between devices: 0.01 us -> 0.86 us  [other_shot(): return lax.ppermute(block, 'shot', [(0, 1), (1, 0)])]
    ppermute x2, waiting for transfers between devices: 0.74 us -> 0.01 us  [from_slab(): return lax.ppermute(block, 'slab', [(i, i ^ step) for i in range(slabs)])]
  transfers between devices with their start and end apart: 14 -> 14, of which waited for: 6 -> 5; matrix products, arithmetic and copies ran while one was open for 0% -> 0% of each run, Pallas kernels for 14% -> 14%
where the time goes in v5:
time: 28.5 us; the launch traced here: 28.4 us
  starting transfers between devices  17.2 us (60%)
  Pallas kernels  5.8 us (20%)
  waiting for transfers between devices  4.59 us (16%)
  between operations  0.78 us (3%)
    ppermute x8, starting transfers between devices, exchange(): return [lax.ppermute(block, ('slab', 'shot'), way) for way in ways]  9.16 us
    pallas_call x12, Pallas kernels, call(): pl.pallas_call(body, out_shape=outs, in_specs=[pl.BlockSpec(memory_space=...  5.8 us
    ppermute x2, starting transfers between devices, from_slab(): return lax.ppermute(block, 'slab', [(i, i ^ step) for i in range(slabs)])  4.83 us
    ppermute x2, starting transfers between devices, from_dom(): lax.ppermute(block, 'dom', [((i + distance) % doms, i) for i in range(dom...  3.19 us
    ppermute x2, waiting for transfers between devices, from_dom(): lax.ppermute(block, 'dom', [((i + distance) % doms, i) for i in range(dom...  2.07 us
    ppermute x8, waiting for transfers between devices, exchange(): return [lax.ppermute(block, ('slab', 'shot'), way) for way in ways]  1.66 us
    ppermute x2, waiting for transfers between devices, other_shot(): return lax.ppermute(block, 'shot', [(0, 1), (1, 0)])  0.86 us
  transfers between devices with their start and end apart: 14, of which 5 were waited for; matrix products, arithmetic and copies ran while one was open for 0% of the time, Pallas kernels for 14%

profile of v5, /device:TPU:0, one launch (start us, length us, event | category | flops | bytes accessed | tf_op | source)
XLA Modules:
  0.0 28.4 jit_solution(1479798500854290597)
XLA Ops:
  0.0 1.1 %shard_map.100 = (f32[8,32,128]{2,1,0:T(8,128)S(1)}, f32[8,32,128]{2,1,0:T(8,128)S(1)}, f32[8,32,128]{2,1,0:T(8,128)S(1)}, f32[8,32,128]{2,1,0:T(8,128)S(1)}, bf...) custom-call(bf16[8,32,128]{2,1,0:T(8,128)(2,1)} %bitcast.11, ...), custom_call_target="tpu_custom_call" | custom-call | flops 1048576 | bytes 411144 | tf_op jit(solution)/shard_map/pallas_call | solution.py:26
  1.1 3.0 %collective-permute-start.1 = (f32[8,32,128]{2,1,0:T(8,128)S(1)}, f32[8,32,128]{2,1,0:T(8,128)S(1)}, u32[]{:S(2)}, u32[]{:S(2)}) collective-permute-start(f32[8,32,128]{2,1,0:T(8,128)S(1)} %get-tuple-element.29.one_ref), channel_id=1, source_target_pairs={{0,4},{4,8},{8,12},{12,13},{5,1},{9,5},{13,9},{1,0},{2,6},{6,10},{... | collective-permute-start | bytes 393224 | tf_op jit(solution)/shard_map/ppermute | solution.py:127
  4.1 0.0 collective-permute-start
  4.2 2.0 %collective-permute-start.8 = (f32[8,32,128]{2,1,0:T(8,128)S(1)}, f32[8,32,128]{2,1,0:T(8,128)S(1)}, u32[]{:S(2)}, u32[]{:S(2)}) collective-permute-start(f32[8,32,128]{2,1,0:T(8,128)S(1)} %get-tuple-element.36.moved_ref), channel_id=1, source_target_pairs={{0,4},{4,8},{8,12},{12,13},{5,1},{9,5},{13,9},{1,0},{2,6},{6,10},{... | collective-permute-start | bytes 393224 | tf_op jit(solution)/shard_map/ppermute | solution.py:127
  6.2 0.0 collective-permute-start.7
  6.8 0.8 %shard_map.101 = (f32[8,32,128]{2,1,0:T(8,128)S(1)}, f32[160,128]{1,0:T(8,128)S(1)}) custom-call(s32[8,128]{1,0:T(8,128)S(1)} %broadcast_in_dim.9.source_ref, f32[1,2]{1,0:T(1,128)S(1)} %get-tuple-element.26.wavelet_ref, s32[1,128]{1,0:T(1,128)S(1)} %get-tuple-element.27.receiver_ref, f32[2,128]{1,0:T(2,128)S(1)} %get-tuple-element.28.observed_ref, ...), custom_call_target="tpu_custom_call" | custom-call | flops 1048576 | bytes 136712 | tf_op jit(solution)/shard_map/pallas_call | solution.py:26
  7.7 0.4 %collective-permute-done.1.second = f32[8,32,128]{2,1,0:T(8,128)S(1)} collective-permute-done((f32[8,32,128]{2,1,0:T(8,128)S(1)}, f32[8,32,128]{2,1,0:T(8,128)S(1)}, u32[]{:S(2)}, u32[]{:S(2)}) %collective-permute-start.1) | collective-permute-done | bytes 131104 | tf_op jit(solution)/shard_map/ppermute | solution.py:127
  8.0 1.1 %collective-permute-done.first = f32[8,32,128]{2,1,0:T(8,128)S(1)} collective-permute-done((f32[8,32,128]{2,1,0:T(8,128)S(1)}, f32[8,32,128]{2,1,0:T(8,128)S(1)}, u32[]{:S(2)}, u32[]{:S(2)}) %collective-permute-start) | collective-permute-done | bytes 131104 | tf_op jit(solution)/shard_map/ppermute | solution.py:127
  9.1 0.1 shard_map.102
  9.3 0.0 collective-permute-start.6
  9.3 2.0 %collective-permute-start.5 = (f32[8,32,128]{2,1,0:T(8,128)S(1)}, f32[8,32,128]{2,1,0:T(8,128)S(1)}, u32[]{:S(2)}, u32[]{:S(2)}) collective-permute-start(f32[8,32,128]{2,1,0:T(8,128)S(1)} %get-tuple-element.35.two_ref), channel_id=1, source_target_pairs={{0,4},{4,8},{8,12},{12,13},{5,1},{9,5},{13,9},{1,0},{2,6},{6,10},{... | collective-permute-start | bytes 393224 | tf_op jit(solution)/shard_map/ppermute | solution.py:127
  11.3 1.6 %collective-permute-start.2 = (f32[8,32,128]{2,1,0:T(8,128)S(1)}, f32[8,32,128]{2,1,0:T(8,128)S(1)}, u32[]{:S(2)}, u32[]{:S(2)}) collective-permute-start(f32[8,32,128]{2,1,0:T(8,128)S(1)} %get-tuple-element.34), channel_id=1, source_target_pairs={{2,0},{0,2},{3,1},{1,3},{6,4},{4,6},{7,5},{5,7},{10,8},{8,10},{11,... | collective-permute-start | bytes 393224 | tf_op jit(solution)/shard_map/ppermute | solution.py:130
  12.9 0.0 collective-permute-done.8.second
  12.9 0.0 collective-permute-done.7.first
  12.9 1.1 %shard_map.106 = (f32[8,32,128]{2,1,0:T(8,128)S(1)}, f32[8,32,128]{2,1,0:T(8,128)S(1)}) custom-call(f32[8,32,128]{2,1,0:T(8,128)S(1)} %collective-permute-done.7.first, f32[8,32,128]{2,1,0:T(8,128)S(1)} %collective-permute-done.8.second, f32[8,32,128]{2,1,0:T(8,128)S(1)} %get-tuple-element.36.moved_ref, bf16[8,32,128]{2,1,0:T(8,128)(2,1)S(1)} %get-tuple-element.37.near_ref, ...), custom_call_target="tpu_custom_call" | custom-call | flops 1048576 | bytes 655360 | tf_op jit(solution)/shard_map/pallas_call | solution.py:26
  14.1 0.2 collective-permute-done.6.second
  14.2 0.0 collective-permute-done.5.first
  14.3 0.1 shard_map.107
  14.4 0.0 collective-permute-start.10
  14.4 2.0 %collective-permute-start.9 = (f32[8,32,128]{2,1,0:T(8,128)S(1)}, f32[8,32,128]{2,1,0:T(8,128)S(1)}, u32[]{:S(2)}, u32[]{:S(2)}) collective-permute-start(f32[8,32,128]{2,1,0:T(8,128)S(1)} %get-tuple-element.41.moved_ref), channel_id=1, source_target_pairs={{0,4},{4,8},{8,12},{12,13},{5,1},{9,5},{13,9},{1,0},{2,6},{6,10},{... | collective-permute-start | bytes 393224 | tf_op jit(solution)/shard_map/ppermute | solution.py:127
  16.5 0.0 collective-permute-done.2.refs_1_
  16.5 0.6 %shard_map.103.first_ref = f32[16,128]{1,0:T(8,128)S(1)} custom-call(f32[8,32,128]{2,1,0:T(8,128)S(1)} %get-tuple-element.25.models_ref.refs_0_, f32[8,32,128]{2,1,0:T(8,128)S(1)} %collective-permute-done.2.refs_1_), custom_call_target="tpu_custom_call" | custom-call | flops 1048576 | bytes 262144 | tf_op jit(solution)/shard_map/pallas_call | solution.py:26
  17.1 3.2 %collective-permute-start.3 = (f32[16,128]{1,0:T(8,128)S(1)}, f32[16,128]{1,0:T(8,128)S(1)}, u32[]{:S(2)}, u32[]{:S(2)}) collective-permute-start(f32[16,128]{1,0:T(8,128)S(1)} %shard_map.103.first_ref), channel_id=1, source_target_pairs={{0,8},{4,12},{8,0},{12,4},{1,9},{5,13},{9,1},{13,5},{2,10},{6,14},... | collective-permute-start | bytes 24584 | tf_op jit(solution)/shard_map/ppermute | solution.py:140
  20.2 0.6 %shard_map.108.inner_ref = f32[8,32,128]{2,1,0:T(8,128)S(1)} custom-call(f32[160,128]{1,0:T(8,128)S(1)} %get-tuple-element.30.spots_ref, f32[8,32,128]{2,1,0:T(8,128)S(1)} %get-tuple-element.41.moved_ref, f32[8,32,128]{2,1,0:T(8,128)S(1)} %get-tuple-element.42.three_ref, bf16[8,32,128]{2,1,0:T(8,128)(2,1)S(1)} %get-tuple-element.37.near_ref, ...), custom_call_target="tpu_custom_call" | custom-call | flops 1048576 | bytes 802816 | tf_op jit(solution)/shard_map/pallas_call | solution.py:26
  20.8 0.0 collective-permute-done.10.second
  20.8 0.0 collective-permute-done.9.first
  20.8 0.1 shard_map.109.pull_ref
  20.9 1.6 %collective-permute-start.12 = (f32[8,32,128]{2,1,0:T(8,128)S(1)}, f32[8,32,128]{2,1,0:T(8,128)S(1)}, u32[]{:S(2)}, u32[]{:S(2)}) collective-permute-start(f32[8,32,128]{2,1,0:T(8,128)S(1)} %shard_map.109.pull_ref), channel_id=1, source_target_pairs={{2,0},{0,2},{3,1},{1,3},{6,4},{4,6},{7,5},{5,7},{10,8},{8,10},{11,... | collective-permute-start | bytes 393224 | tf_op jit(solution)/shard_map/ppermute | solution.py:130
  22.5 0.0 collective-permute-done.3.second_ref
  22.5 1.7 %collective-permute-start.4 = (f32[16,128]{1,0:T(8,128)S(1)}, f32[16,128]{1,0:T(8,128)S(1)}, u32[]{:S(2)}, u32[]{:S(2)}) collective-permute-start(f32[16,128]{1,0:T(8,128)S(1)} %shard_map.104.gram_ref), channel_id=1, source_target_pairs={{0,4},{4,0},{8,12},{12,8},{1,5},{5,1},{9,13},{13,9},{2,6},{6,2},{1... | collective-permute-start | bytes 24584 | tf_op jit(solution)/shard_map/ppermute | solution.py:140
  24.2 0.0 collective-permute-start.11
  24.2 2.1 %collective-permute-done.12.refs_0_ = f32[8,32,128]{2,1,0:T(8,128)S(1)} collective-permute-done((f32[8,32,128]{2,1,0:T(8,128)S(1)}, f32[8,32,128]{2,1,0:T(8,128)S(1)}, u32[]{:S(2)}, u32[]{:S(2)}) %collective-permute-start.12) | collective-permute-done | bytes 131104 | tf_op jit(solution)/shard_map/ppermute | solution.py:130
  26.3 0.0 collective-permute-start.13
  26.3 0.0 collective-permute-done.4.pair_ref
  26.3 0.4 %shard_map.105.kernel_ref = f32[16,8,128]{2,1,0:T(8,128)S(1)} custom-call(f32[16,128]{1,0:T(8,128)S(1)} %shard_map.104.gram_ref, f32[16,128]{1,0:T(8,128)S(1)} %collective-permute-done.4.pair_ref), custom_call_target="tpu_custom_call" | custom-call | flops 8589934592 | bytes 16384 | tf_op jit(solution)/shard_map/pallas_call | solution.py:26
  26.6 0.0 collective-permute-done.11.pair_ref
  26.6 0.1 shard_map.110.base_ref
  26.7 0.9 %collective-permute-done.13.refs_1_ = f32[8,32,128]{2,1,0:T(8,128)S(1)} collective-permute-done((f32[8,32,128]{2,1,0:T(8,128)S(1)}, f32[8,32,128]{2,1,0:T(8,128)S(1)}, u32[]{:S(2)}, u32[]{:S(2)}) %collective-permute-start.13) | collective-permute-done | bytes 131104 | tf_op jit(solution)/shard_map/ppermute | solution.py:133
  27.6 0.7 %shard_map.111 = f32[8,32,128]{2,1,0:T(8,128)} custom-call(f32[16,8,128]{2,1,0:T(8,128)S(1)} %shard_map.105.kernel_ref, f32[8,32,128]{2,1,0:T(8,128)S(1)} %shard_map.110.base_ref, f32[8,32,128]{2,1,0:T(8,128)S(1)} %collective-permute-done.12.refs_0_, f32[8,32,128]{2,1,0:T(8,128)S(1)} %collective-permute-done.13.refs_1_), custom_call_target="tpu_custom_call" | custom-call | flops 1048576 | bytes 458752 | tf_op jit(solution)/shard_map/pallas_call | solution.py:26
  (2 shorter events, 0.0 us)
Async XLA Ops:
  1.1 6.9 %collective-permute-start.1 = (f32[8,32,128]{2,1,0:T(8,128)S(1)}, f32[8,32,128]{2,1,0:T(8,128)S(1)}, u32[]{:S(2)}, u32[]{:S(2)}) collective-permute-start(f32[8,32,128]{2,1,0:T(8,128)S(1)} %get-tuple-element.29.one_ref), channel_id=1, source_target_pairs={{0,4},{4,8},{8,12},{12,13},{5,1},{9,5},{13,9},{1,0},{2,6},{6,10},{... | collective-permute-start | bytes 393224 | tf_op jit(solution)/shard_map/ppermute | solution.py:127
  4.1 5.0 %collective-permute-start = (f32[8,32,128]{2,1,0:T(8,128)S(1)}, f32[8,32,128]{2,1,0:T(8,128)S(1)}, u32[]{:S(2)}, u32[]{:S(2)}) collective-permute-start(f32[8,32,128]{2,1,0:T(8,128)S(1)} %get-tuple-element.29.one_ref), channel_id=1, source_target_pairs={{4,0},{8,4},{12,8},{13,12},{1,5},{5,9},{9,13},{0,1},{6,2},{10,6},{... | collective-permute-start | bytes 393224 | tf_op jit(solution)/shard_map/ppermute | solution.py:127
  4.2 8.8 %collective-permute-start.8 = (f32[8,32,128]{2,1,0:T(8,128)S(1)}, f32[8,32,128]{2,1,0:T(8,128)S(1)}, u32[]{:S(2)}, u32[]{:S(2)}) collective-permute-start(f32[8,32,128]{2,1,0:T(8,128)S(1)} %get-tuple-element.36.moved_ref), channel_id=1, source_target_pairs={{0,4},{4,8},{8,12},{12,13},{5,1},{9,5},{13,9},{1,0},{2,6},{6,10},{... | collective-permute-start | bytes 393224 | tf_op jit(solution)/shard_map/ppermute | solution.py:127
  6.2 6.8 %collective-permute-start.7 = (f32[8,32,128]{2,1,0:T(8,128)S(1)}, f32[8,32,128]{2,1,0:T(8,128)S(1)}, u32[]{:S(2)}, u32[]{:S(2)}) collective-permute-start(f32[8,32,128]{2,1,0:T(8,128)S(1)} %get-tuple-element.36.moved_ref), channel_id=1, source_target_pairs={{4,0},{8,4},{12,8},{13,12},{1,5},{5,9},{9,13},{0,1},{6,2},{10,6},{... | collective-permute-start | bytes 393224 | tf_op jit(solution)/shard_map/ppermute | solution.py:127
  9.3 5.0 %collective-permute-start.6 = (f32[8,32,128]{2,1,0:T(8,128)S(1)}, f32[8,32,128]{2,1,0:T(8,128)S(1)}, u32[]{:S(2)}, u32[]{:S(2)}) collective-permute-start(f32[8,32,128]{2,1,0:T(8,128)S(1)} %get-tuple-element.35.two_ref), channel_id=1, source_target_pairs={{4,0},{8,4},{12,8},{13,12},{1,5},{5,9},{9,13},{0,1},{6,2},{10,6},{... | collective-permute-start | bytes 393224 | tf_op jit(solution)/shard_map/ppermute | solution.py:127
  9.3 5.0 %collective-permute-start.5 = (f32[8,32,128]{2,1,0:T(8,128)S(1)}, f32[8,32,128]{2,1,0:T(8,128)S(1)}, u32[]{:S(2)}, u32[]{:S(2)}) collective-permute-start(f32[8,32,128]{2,1,0:T(8,128)S(1)} %get-tuple-element.35.two_ref), channel_id=1, source_target_pairs={{0,4},{4,8},{8,12},{12,13},{5,1},{9,5},{13,9},{1,0},{2,6},{6,10},{... | collective-permute-start | bytes 393224 | tf_op jit(solution)/shard_map/ppermute | solution.py:127
  11.3 5.2 %collective-permute-start.2 = (f32[8,32,128]{2,1,0:T(8,128)S(1)}, f32[8,32,128]{2,1,0:T(8,128)S(1)}, u32[]{:S(2)}, u32[]{:S(2)}) collective-permute-start(f32[8,32,128]{2,1,0:T(8,128)S(1)} %get-tuple-element.34), channel_id=1, source_target_pairs={{2,0},{0,2},{3,1},{1,3},{6,4},{4,6},{7,5},{5,7},{10,8},{8,10},{11,... | collective-permute-start | bytes 393224 | tf_op jit(solution)/shard_map/ppermute | solution.py:130
  14.4 6.4 %collective-permute-start.10 = (f32[8,32,128]{2,1,0:T(8,128)S(1)}, f32[8,32,128]{2,1,0:T(8,128)S(1)}, u32[]{:S(2)}, u32[]{:S(2)}) collective-permute-start(f32[8,32,128]{2,1,0:T(8,128)S(1)} %get-tuple-element.41.moved_ref), channel_id=1, source_target_pairs={{4,0},{8,4},{12,8},{13,12},{1,5},{5,9},{9,13},{0,1},{6,2},{10,6},{... | collective-permute-start | bytes 393224 | tf_op jit(solution)/shard_map/ppermute | solution.py:127
  14.4 6.4 %collective-permute-start.9 = (f32[8,32,128]{2,1,0:T(8,128)S(1)}, f32[8,32,128]{2,1,0:T(8,128)S(1)}, u32[]{:S(2)}, u32[]{:S(2)}) collective-permute-start(f32[8,32,128]{2,1,0:T(8,128)S(1)} %get-tuple-element.41.moved_ref), channel_id=1, source_target_pairs={{0,4},{4,8},{8,12},{12,13},{5,1},{9,5},{13,9},{1,0},{2,6},{6,10},{... | collective-permute-start | bytes 393224 | tf_op jit(solution)/shard_map/ppermute | solution.py:127
  17.1 5.5 %collective-permute-start.3 = (f32[16,128]{1,0:T(8,128)S(1)}, f32[16,128]{1,0:T(8,128)S(1)}, u32[]{:S(2)}, u32[]{:S(2)}) collective-permute-start(f32[16,128]{1,0:T(8,128)S(1)} %shard_map.103.first_ref), channel_id=1, source_target_pairs={{0,8},{4,12},{8,0},{12,4},{1,9},{5,13},{9,1},{13,5},{2,10},{6,14},... | collective-permute-start | bytes 24584 | tf_op jit(solution)/shard_map/ppermute | solution.py:140
  20.9 5.3 %collective-permute-start.12 = (f32[8,32,128]{2,1,0:T(8,128)S(1)}, f32[8,32,128]{2,1,0:T(8,128)S(1)}, u32[]{:S(2)}, u32[]{:S(2)}) collective-permute-start(f32[8,32,128]{2,1,0:T(8,128)S(1)} %shard_map.109.pull_ref), channel_id=1, source_target_pairs={{2,0},{0,2},{3,1},{1,3},{6,4},{4,6},{7,5},{5,7},{10,8},{8,10},{11,... | collective-permute-start | bytes 393224 | tf_op jit(solution)/shard_map/ppermute | solution.py:130
  22.5 3.8 %collective-permute-start.4 = (f32[16,128]{1,0:T(8,128)S(1)}, f32[16,128]{1,0:T(8,128)S(1)}, u32[]{:S(2)}, u32[]{:S(2)}) collective-permute-start(f32[16,128]{1,0:T(8,128)S(1)} %shard_map.104.gram_ref), channel_id=1, source_target_pairs={{0,4},{4,0},{8,12},{12,8},{1,5},{5,1},{9,13},{13,9},{2,6},{6,2},{1... | collective-permute-start | bytes 24584 | tf_op jit(solution)/shard_map/ppermute | solution.py:140
  24.2 2.4 %collective-permute-start.11 = (f32[8,32,128]{2,1,0:T(8,128)S(1)}, f32[8,32,128]{2,1,0:T(8,128)S(1)}, u32[]{:S(2)}, u32[]{:S(2)}) collective-permute-start(f32[8,32,128]{2,1,0:T(8,128)S(1)} %shard_map.109.pull_ref), channel_id=1, source_target_pairs={{0,1},{1,0},{2,3},{3,2},{4,5},{5,4},{6,7},{7,6},{8,9},{9,8},{10,11... | collective-permute-start | bytes 393224 | tf_op jit(solution)/shard_map/ppermute | solution.py:133
  26.3 1.3 %collective-permute-start.13 = (f32[8,32,128]{2,1,0:T(8,128)S(1)}, f32[8,32,128]{2,1,0:T(8,128)S(1)}, u32[]{:S(2)}, u32[]{:S(2)}) collective-permute-start(f32[8,32,128]{2,1,0:T(8,128)S(1)} %collective-permute-done.12.refs_0_), channel_id=1, source_target_pairs={{0,1},{1,0},{2,3},{3,2},{4,5},{5,4},{6,7},{7,6},{8,9},{9,8},{10,11... | collective-permute-start | bytes 393224 | tf_op jit(solution)/shard_map/ppermute | solution.py:133

commit v6 on v5

--- a/solution.py
+++ b/solution.py
@@ -104,7 +104,7 @@
     return below, above
 
 
-def loop(count, body, together=2):
+def loop(count, body, together=8):
     if count % together:
         together = 1
 
@@ -205,7 +205,7 @@
             ],
         )
         one_first, one_second = exchange(wave_one, flip=True)
-        near_first, near_second = exchange(near_moved, flip=True)
+        near_first, near_second = exchange(near_moved)
 
         def first_base(source_ref, wavelet_ref, receiver_ref, observed_ref, one_ref, inner_out, spots_out):
             weights = plane_weights(rows, columns)
@@ -249,9 +249,8 @@
             return spots_ref[kind * depth + z * rows : kind * depth + (z + 1) * rows]
 
         def first(
-            spots_ref, first, second, inner_ref, one_ref, zero_ref, squared_ref, models_ref, lap_out, wave_out, models_out
+            spots_ref, first, second, inner_ref, one_ref, zero_ref, squared_ref, lap_out, wave_out
         ):
-            models_out[...] = models_ref[...]
             masks = side_masks(rows, columns, flip=True)
 
             def particle(p):
@@ -265,15 +264,15 @@
 
             loop(count, particle)
 
-        lap_one, wave_two, models_sent = call(
-            first, [stack] * 3, spots, one_first, one_second, one_inner, wave_one, zero, squared, models
+        lap_one, wave_two = call(
+            first, [stack] * 2, spots, one_first, one_second, one_inner, wave_one, zero, squared
         )
         two_first, two_second = exchange(wave_two)
-        others = [from_dom(models_sent, k) for k in range(1, doms)]
+        others = [from_dom(models, k) for k in range(1, doms)]
 
         def second_base(first, second, moved_ref, near_ref, far_ref, two_ref, base_out, inner_out):
             weights = plane_weights(rows, columns)
-            masks = side_masks(rows, columns, flip=True)
+            masks = side_masks(rows, columns)
 
             def waves(p):
                 for at, plane in zip(at_plane, inner_laplace(planes_of(two_ref[p], rows), weights)):
@@ -360,10 +359,10 @@
             first_of = lax.broadcasted_iota(jnp.int32, (total, wide), 1) % rows == 0
             out_ref[...] = jnp.where(first_of, same, 0.0)
 
-        (gram_one,) = call(gram, [(total, wide)], models, *others)
+        (gram_one,) = call(gram, [(total, wide)], models, *others, flops=LONG)
         if not halving:
             gram_one = lax.psum(gram_one, "slab")
-        gram_pair = from_slab(gram_one, 2)
+        gram_pair = from_slab(gram_one, 1)
 
         def third_base(spots_ref, moved_ref, three_ref, near_ref, two_ref, lap_one_ref, lap_two_ref, out_ref):
             weights = plane_weights(rows, columns)
@@ -424,11 +423,12 @@
         step = 2
         while halving and step < slabs:
             (gram_one,) = call(plus, [(total, wide)], gram_one, gram_pair, flops=LONG)
-            gram_pair = from_slab(gram_one, 1 if step == 2 else step)
+            gram_pair = from_slab(gram_one, step)
             step *= 2
-
-        def spread(gram_ref, pair_ref, out_ref):
-            value = gram_ref[...] + pair_ref[...]
+        (gram_one,) = call(plus, [(total, wide)], gram_one, gram_pair, flops=LONG)
+
+        def spread(gram_ref, out_ref):
+            value = gram_ref[...]
             r = lax.broadcasted_iota(jnp.int32, (total, wide), 0)
             c = lax.broadcasted_iota(jnp.int32, (total, wide), 1)
             diagonal = jnp.where(r * rows == c, value, 0.0)
@@ -442,7 +442,7 @@
             for j in range(total):
                 out_ref[j] = jnp.broadcast_to(kernel[:count, j * rows : j * rows + 1], (count, columns))
 
-        (spread_kernel,) = call(spread, [(total, count, columns)], gram_one, gram_pair, flops=LONG)
+        (spread_kernel,) = call(spread, [(total, count, columns)], gram_one, flops=LONG)
 
         def weigh(kernel_ref, start, pulled, values):
             for j in range(len(values)):

time: 28.5 us -> 28.4 us (level)
  waiting for transfers between devices: 4.59 us -> 7 us
  starting transfers between devices: 17.2 us -> 15.9 us
  Pallas kernels: 5.8 us -> 4.52 us
    ppermute x2, waiting for transfers between devices: 2.07 us -> 3.35 us  [from_dom(): lax.ppermute(block, 'dom', [((i + distance) % doms, i) for i in range(dom...]
    pallas_call x12 -> x13, Pallas kernels: 5.8 us -> 4.52 us  [call(): pl.pallas_call(body, out_shape=outs, in_specs=[pl.BlockSpec(memory_space=...]
    ppermute x2, starting transfers between devices: 4.83 us -> 3.63 us  [from_slab(): return lax.ppermute(block, 'slab', [(i, i ^ step) for i in range(slabs)])]
    ppermute x8, waiting for transfers between devices: 1.66 us -> 2.78 us  [exchange(): return [lax.ppermute(block, ('slab', 'shot'), way) for way in ways]]
    ppermute x8, starting transfers between devices: 9.16 us -> 8.72 us  [exchange(): return [lax.ppermute(block, ('slab', 'shot'), way) for way in ways]]
    ppermute x2, starting transfers between devices: 3.19 us -> 3.58 us  [from_dom(): lax.ppermute(block, 'dom', [((i + distance) % doms, i) for i in range(dom...]
  transfers between devices with their start and end apart: 14 -> 14, of which waited for: 5 -> 5; matrix products, arithmetic and copies ran while one was open for 0% -> 0% of each run, Pallas kernels for 14% -> 9%
where the time goes in v6:
time: 28.4 us; the launch traced here: 28.2 us
  starting transfers between devices  15.9 us (56%)
  waiting for transfers between devices  7 us (25%)
  Pallas kernels  4.52 us (16%)
  between operations  0.78 us (3%)
    ppermute x8, starting transfers between devices, exchange(): return [lax.ppermute(block, ('slab', 'shot'), way) for way in ways]  8.72 us
    pallas_call x13, Pallas kernels, call(): pl.pallas_call(body, out_shape=outs, in_specs=[pl.BlockSpec(memory_space=...  4.52 us
    ppermute x2, starting transfers between devices, from_slab(): return lax.ppermute(block, 'slab', [(i, i ^ step) for i in range(slabs)])  3.63 us
    ppermute x2, starting transfers between devices, from_dom(): lax.ppermute(block, 'dom', [((i + distance) % doms, i) for i in range(dom...  3.58 us
    ppermute x2, waiting for transfers between devices, from_dom(): lax.ppermute(block, 'dom', [((i + distance) % doms, i) for i in range(dom...  3.35 us
    ppermute x8, waiting for transfers between devices, exchange(): return [lax.ppermute(block, ('slab', 'shot'), way) for way in ways]  2.78 us
    ppermute x2, waiting for transfers between devices, other_shot(): return lax.ppermute(block, 'shot', [(0, 1), (1, 0)])  0.86 us
  transfers between devices with their start and end apart: 14, of which 5 were waited for; matrix products, arithmetic and copies ran while one was open for 0% of the time, Pallas kernels for 9%

profile of v6, /device:TPU:0, one launch (start us, length us, event | category | flops | bytes accessed | tf_op | source)
XLA Modules:
  0.0 28.2 jit_solution(12474137078168284162)
XLA Ops:
  0.0 1.1 %shard_map.100 = (f32[8,32,128]{2,1,0:T(8,128)S(1)}, f32[8,32,128]{2,1,0:T(8,128)S(1)}, f32[8,32,128]{2,1,0:T(8,128)S(1)}, f32[8,32,128]{2,1,0:T(8,128)S(1)}, bf...) custom-call(bf16[8,32,128]{2,1,0:T(8,128)(2,1)} %bitcast.11, ...), custom_call_target="tpu_custom_call" | custom-call | flops 1048576 | bytes 411144 | tf_op jit(solution)/shard_map/pallas_call | solution.py:26
  1.1 0.5 %collective-permute-start.3 = (f32[8,32,128]{2,1,0:T(8,128)S(1)}, f32[8,32,128]{2,1,0:T(8,128)S(1)}, u32[]{:S(2)}, u32[]{:S(2)}) collective-permute-start(f32[8,32,128]{2,1,0:T(8,128)S(1)} %get-tuple-element.28.one_ref), channel_id=1, source_target_pairs={{4,0},{8,4},{12,8},{13,12},{1,5},{5,9},{9,13},{0,1},{6,2},{10,6},{... | collective-permute-start | bytes 393224 | tf_op jit(solution)/shard_map/ppermute | solution.py:127
  1.6 2.6 %collective-permute-start.4 = (f32[8,32,128]{2,1,0:T(8,128)S(1)}, f32[8,32,128]{2,1,0:T(8,128)S(1)}, u32[]{:S(2)}, u32[]{:S(2)}) collective-permute-start(f32[8,32,128]{2,1,0:T(8,128)S(1)} %get-tuple-element.28.one_ref), channel_id=1, source_target_pairs={{0,4},{4,8},{8,12},{12,13},{5,1},{9,5},{13,9},{1,0},{2,6},{6,10},{... | collective-permute-start | bytes 393224 | tf_op jit(solution)/shard_map/ppermute | solution.py:127
  4.2 1.9 %collective-permute-start = (f32[8,32,128]{2,1,0:T(8,128)S(1)}, f32[8,32,128]{2,1,0:T(8,128)S(1)}, u32[]{:S(2)}, u32[]{:S(2)}) collective-permute-start(f32[8,32,128]{2,1,0:T(8,128)S(1)} %get-tuple-element.24.refs_0_.models_ref), channel_id=1, source_target_pairs={{2,0},{0,2},{3,1},{1,3},{6,4},{4,6},{7,5},{5,7},{10,8},{8,10},{11,... | collective-permute-start | bytes 393224 | tf_op jit(solution)/shard_map/ppermute | solution.py:130
  6.1 1.6 %collective-permute-start.7 = (f32[8,32,128]{2,1,0:T(8,128)S(1)}, f32[8,32,128]{2,1,0:T(8,128)S(1)}, u32[]{:S(2)}, u32[]{:S(2)}) collective-permute-start(f32[8,32,128]{2,1,0:T(8,128)S(1)} %get-tuple-element.34.moved_ref), channel_id=1, source_target_pairs={{0,4},{4,8},{8,12},{12,13},{5,1},{9,5},{13,9},{1,0},{2,6},{6,10},{... | collective-permute-start | bytes 393224 | tf_op jit(solution)/shard_map/ppermute | solution.py:127
  7.7 0.0 collective-permute-start.8
  8.3 0.4 %shard_map.105 = (f32[8,32,128]{2,1,0:T(8,128)S(1)}, f32[160,128]{1,0:T(8,128)S(1)}) custom-call(s32[8,128]{1,0:T(8,128)S(1)} %broadcast_in_dim.9.source_ref, f32[1,2]{1,0:T(1,128)S(1)} %get-tuple-element.25.wavelet_ref, s32[1,128]{1,0:T(1,128)S(1)} %get-tuple-element.26.receiver_ref, f32[2,128]{1,0:T(2,128)S(1)} %get-tuple-element.27.observed_ref, ...), custom_call_target="tpu_custom_call" | custom-call | flops 1048576 | bytes 136712 | tf_op jit(solution)/shard_map/pallas_call | solution.py:26
  8.7 0.0 collective-permute-done.3.first
  8.7 0.0 collective-permute-done.4.second
  8.7 0.1 shard_map.106
  8.8 2.0 %collective-permute-start.5 = (f32[8,32,128]{2,1,0:T(8,128)S(1)}, f32[8,32,128]{2,1,0:T(8,128)S(1)}, u32[]{:S(2)}, u32[]{:S(2)}) collective-permute-start(f32[8,32,128]{2,1,0:T(8,128)S(1)} %get-tuple-element.33.two_ref), channel_id=1, source_target_pairs={{0,4},{4,8},{8,12},{12,13},{5,1},{9,5},{13,9},{1,0},{2,6},{6,10},{... | collective-permute-start | bytes 393224 | tf_op jit(solution)/shard_map/ppermute | solution.py:127
  10.9 0.0 collective-permute-start.6
  10.9 0.0 collective-permute-done.refs_1_
  10.9 0.6 %shard_map.101.first_ref = f32[16,128]{1,0:T(8,128)S(1)} custom-call(f32[8,32,128]{2,1,0:T(8,128)S(1)} %get-tuple-element.24.refs_0_.models_ref, f32[8,32,128]{2,1,0:T(8,128)S(1)} %collective-permute-done.refs_1_), custom_call_target="tpu_custom_call" | custom-call | flops 8589934592 | bytes 262144 | tf_op jit(solution)/shard_map/pallas_call | solution.py:26
  11.5 2.0 %collective-permute-start.1 = (f32[16,128]{1,0:T(8,128)S(1)}, f32[16,128]{1,0:T(8,128)S(1)}, u32[]{:S(2)}, u32[]{:S(2)}) collective-permute-start(f32[16,128]{1,0:T(8,128)S(1)} %shard_map.101.first_ref), channel_id=1, source_target_pairs={{0,4},{4,0},{8,12},{12,8},{1,5},{5,1},{9,13},{13,9},{2,6},{6,2},{1... | collective-permute-start | bytes 24584 | tf_op jit(solution)/shard_map/ppermute | solution.py:140
  13.5 0.0 collective-permute-done.7.first
  13.5 0.3 collective-permute-done.8.second
  13.7 0.6 %shard_map.107 = (f32[8,32,128]{2,1,0:T(8,128)S(1)}, f32[8,32,128]{2,1,0:T(8,128)S(1)}) custom-call(f32[8,32,128]{2,1,0:T(8,128)S(1)} %collective-permute-done.7.first, f32[8,32,128]{2,1,0:T(8,128)S(1)} %collective-permute-done.8.second, f32[8,32,128]{2,1,0:T(8,128)S(1)} %get-tuple-element.34.moved_ref, bf16[8,32,128]{2,1,0:T(8,128)(2,1)S(1)} %get-tuple-element.35.near_ref, ...), custom_call_target="tpu_custom_call" | custom-call | flops 1048576 | bytes 655360 | tf_op jit(solution)/shard_map/pallas_call | solution.py:26
  14.4 0.0 collective-permute-done.5.first
  14.4 1.5 %collective-permute-done.6.second = f32[8,32,128]{2,1,0:T(8,128)S(1)} collective-permute-done((f32[8,32,128]{2,1,0:T(8,128)S(1)}, f32[8,32,128]{2,1,0:T(8,128)S(1)}, u32[]{:S(2)}, u32[]{:S(2)}) %collective-permute-start.6) | collective-permute-done | bytes 131104 | tf_op jit(solution)/shard_map/ppermute | solution.py:127
  15.8 0.1 shard_map.108
  16.0 0.0 collective-permute-start.10
  16.0 2.0 %collective-permute-start.9 = (f32[8,32,128]{2,1,0:T(8,128)S(1)}, f32[8,32,128]{2,1,0:T(8,128)S(1)}, u32[]{:S(2)}, u32[]{:S(2)}) collective-permute-start(f32[8,32,128]{2,1,0:T(8,128)S(1)} %get-tuple-element.39.moved_ref), channel_id=1, source_target_pairs={{0,4},{4,8},{8,12},{12,13},{5,1},{9,5},{13,9},{1,0},{2,6},{6,10},{... | collective-permute-start | bytes 393224 | tf_op jit(solution)/shard_map/ppermute | solution.py:127
  18.0 0.0 collective-permute-done.1.second_ref
  18.0 1.6 %collective-permute-start.2 = (f32[16,128]{1,0:T(8,128)S(1)}, f32[16,128]{1,0:T(8,128)S(1)}, u32[]{:S(2)}, u32[]{:S(2)}) collective-permute-start(f32[16,128]{1,0:T(8,128)S(1)} %shard_map.102.first_ref), channel_id=1, source_target_pairs={{0,8},{4,12},{8,0},{12,4},{1,9},{5,13},{9,1},{13,5},{2,10},{6,14},... | collective-permute-start | bytes 24584 | tf_op jit(solution)/shard_map/ppermute | solution.py:140
  19.6 0.3 %shard_map.109.inner_ref = f32[8,32,128]{2,1,0:T(8,128)S(1)} custom-call(f32[160,128]{1,0:T(8,128)S(1)} %get-tuple-element.29.spots_ref, f32[8,32,128]{2,1,0:T(8,128)S(1)} %get-tuple-element.39.moved_ref, f32[8,32,128]{2,1,0:T(8,128)S(1)} %get-tuple-element.40.three_ref, bf16[8,32,128]{2,1,0:T(8,128)(2,1)S(1)} %get-tuple-element.35.near_ref, ...), custom_call_target="tpu_custom_call" | custom-call | flops 1048576 | bytes 802816 | tf_op jit(solution)/shard_map/pallas_call | solution.py:26
  20.0 1.0 %collective-permute-done.10.second = f32[8,32,128]{2,1,0:T(8,128)S(1)} collective-permute-done((f32[8,32,128]{2,1,0:T(8,128)S(1)}, f32[8,32,128]{2,1,0:T(8,128)S(1)}, u32[]{:S(2)}, u32[]{:S(2)}) %collective-permute-start.10) | collective-permute-done | bytes 131104 | tf_op jit(solution)/shard_map/ppermute | solution.py:127
  21.0 0.0 collective-permute-done.9.first
  21.0 0.1 shard_map.110.pull_ref
  21.1 1.7 %collective-permute-start.12 = (f32[8,32,128]{2,1,0:T(8,128)S(1)}, f32[8,32,128]{2,1,0:T(8,128)S(1)}, u32[]{:S(2)}, u32[]{:S(2)}) collective-permute-start(f32[8,32,128]{2,1,0:T(8,128)S(1)} %shard_map.110.pull_ref), channel_id=1, source_target_pairs={{2,0},{0,2},{3,1},{1,3},{6,4},{4,6},{7,5},{5,7},{10,8},{8,10},{11,... | collective-permute-start | bytes 393224 | tf_op jit(solution)/shard_map/ppermute | solution.py:130
  22.8 0.0 collective-permute-done.2.second_ref
  22.8 0.0 collective-permute-start.11
  22.8 3.4 %collective-permute-done.12.refs_0_ = f32[8,32,128]{2,1,0:T(8,128)S(1)} collective-permute-done((f32[8,32,128]{2,1,0:T(8,128)S(1)}, f32[8,32,128]{2,1,0:T(8,128)S(1)}, u32[]{:S(2)}, u32[]{:S(2)}) %collective-permute-start.12) | collective-permute-done | bytes 131104 | tf_op jit(solution)/shard_map/ppermute | solution.py:130
  26.1 0.0 collective-permute-start.13
  26.1 0.4 %shard_map.104.kernel_ref = f32[16,8,128]{2,1,0:T(8,128)S(1)} custom-call(f32[16,128]{1,0:T(8,128)S(1)} %shard_map.103.gram_ref), custom_call_target="tpu_custom_call" | custom-call | flops 8589934592 | bytes 8192 | tf_op jit(solution)/shard_map/pallas_call | solution.py:26
  26.5 0.0 collective-permute-done.11.pair_ref
  26.5 0.1 shard_map.111.base_ref
  26.6 0.9 %collective-permute-done.13.refs_1_ = f32[8,32,128]{2,1,0:T(8,128)S(1)} collective-permute-done((f32[8,32,128]{2,1,0:T(8,128)S(1)}, f32[8,32,128]{2,1,0:T(8,128)S(1)}, u32[]{:S(2)}, u32[]{:S(2)}) %collective-permute-start.13) | collective-permute-done | bytes 131104 | tf_op jit(solution)/shard_map/ppermute | solution.py:133
  27.5 0.7 %shard_map.112 = f32[8,32,128]{2,1,0:T(8,128)} custom-call(f32[16,8,128]{2,1,0:T(8,128)S(1)} %shard_map.104.kernel_ref, f32[8,32,128]{2,1,0:T(8,128)S(1)} %shard_map.111.base_ref, f32[8,32,128]{2,1,0:T(8,128)S(1)} %collective-permute-done.12.refs_0_, f32[8,32,128]{2,1,0:T(8,128)S(1)} %collective-permute-done.13.refs_1_), custom_call_target="tpu_custom_call" | custom-call | flops 1048576 | bytes 458752 | tf_op jit(solution)/shard_map/pallas_call | solution.py:26
  (3 shorter events, 0.0 us)
Async XLA Ops:
  1.1 7.6 %collective-permute-start.3 = (f32[8,32,128]{2,1,0:T(8,128)S(1)}, f32[8,32,128]{2,1,0:T(8,128)S(1)}, u32[]{:S(2)}, u32[]{:S(2)}) collective-permute-start(f32[8,32,128]{2,1,0:T(8,128)S(1)} %get-tuple-element.28.one_ref), channel_id=1, source_target_pairs={{4,0},{8,4},{12,8},{13,12},{1,5},{5,9},{9,13},{0,1},{6,2},{10,6},{... | collective-permute-start | bytes 393224 | tf_op jit(solution)/shard_map/ppermute | solution.py:127
  1.6 7.1 %collective-permute-start.4 = (f32[8,32,128]{2,1,0:T(8,128)S(1)}, f32[8,32,128]{2,1,0:T(8,128)S(1)}, u32[]{:S(2)}, u32[]{:S(2)}) collective-permute-start(f32[8,32,128]{2,1,0:T(8,128)S(1)} %get-tuple-element.28.one_ref), channel_id=1, source_target_pairs={{0,4},{4,8},{8,12},{12,13},{5,1},{9,5},{13,9},{1,0},{2,6},{6,10},{... | collective-permute-start | bytes 393224 | tf_op jit(solution)/shard_map/ppermute | solution.py:127
  4.2 6.7 %collective-permute-start = (f32[8,32,128]{2,1,0:T(8,128)S(1)}, f32[8,32,128]{2,1,0:T(8,128)S(1)}, u32[]{:S(2)}, u32[]{:S(2)}) collective-permute-start(f32[8,32,128]{2,1,0:T(8,128)S(1)} %get-tuple-element.24.refs_0_.models_ref), channel_id=1, source_target_pairs={{2,0},{0,2},{3,1},{1,3},{6,4},{4,6},{7,5},{5,7},{10,8},{8,10},{11,... | collective-permute-start | bytes 393224 | tf_op jit(solution)/shard_map/ppermute | solution.py:130
  6.1 7.4 %collective-permute-start.7 = (f32[8,32,128]{2,1,0:T(8,128)S(1)}, f32[8,32,128]{2,1,0:T(8,128)S(1)}, u32[]{:S(2)}, u32[]{:S(2)}) collective-permute-start(f32[8,32,128]{2,1,0:T(8,128)S(1)} %get-tuple-element.34.moved_ref), channel_id=1, source_target_pairs={{0,4},{4,8},{8,12},{12,13},{5,1},{9,5},{13,9},{1,0},{2,6},{6,10},{... | collective-permute-start | bytes 393224 | tf_op jit(solution)/shard_map/ppermute | solution.py:127
  7.7 6.1 %collective-permute-start.8 = (f32[8,32,128]{2,1,0:T(8,128)S(1)}, f32[8,32,128]{2,1,0:T(8,128)S(1)}, u32[]{:S(2)}, u32[]{:S(2)}) collective-permute-start(f32[8,32,128]{2,1,0:T(8,128)S(1)} %get-tuple-element.34.moved_ref), channel_id=1, source_target_pairs={{4,0},{8,4},{12,8},{13,12},{1,5},{5,9},{9,13},{0,1},{6,2},{10,6},{... | collective-permute-start | bytes 393224 | tf_op jit(solution)/shard_map/ppermute | solution.py:127
  8.8 5.5 %collective-permute-start.5 = (f32[8,32,128]{2,1,0:T(8,128)S(1)}, f32[8,32,128]{2,1,0:T(8,128)S(1)}, u32[]{:S(2)}, u32[]{:S(2)}) collective-permute-start(f32[8,32,128]{2,1,0:T(8,128)S(1)} %get-tuple-element.33.two_ref), channel_id=1, source_target_pairs={{0,4},{4,8},{8,12},{12,13},{5,1},{9,5},{13,9},{1,0},{2,6},{6,10},{... | collective-permute-start | bytes 393224 | tf_op jit(solution)/shard_map/ppermute | solution.py:127
  10.9 5.0 %collective-permute-start.6 = (f32[8,32,128]{2,1,0:T(8,128)S(1)}, f32[8,32,128]{2,1,0:T(8,128)S(1)}, u32[]{:S(2)}, u32[]{:S(2)}) collective-permute-start(f32[8,32,128]{2,1,0:T(8,128)S(1)} %get-tuple-element.33.two_ref), channel_id=1, source_target_pairs={{4,0},{8,4},{12,8},{13,12},{1,5},{5,9},{9,13},{0,1},{6,2},{10,6},{... | collective-permute-start | bytes 393224 | tf_op jit(solution)/shard_map/ppermute | solution.py:127
  11.5 6.5 %collective-permute-start.1 = (f32[16,128]{1,0:T(8,128)S(1)}, f32[16,128]{1,0:T(8,128)S(1)}, u32[]{:S(2)}, u32[]{:S(2)}) collective-permute-start(f32[16,128]{1,0:T(8,128)S(1)} %shard_map.101.first_ref), channel_id=1, source_target_pairs={{0,4},{4,0},{8,12},{12,8},{1,5},{5,1},{9,13},{13,9},{2,6},{6,2},{1... | collective-permute-start | bytes 24584 | tf_op jit(solution)/shard_map/ppermute | solution.py:140
  16.0 5.0 %collective-permute-start.10 = (f32[8,32,128]{2,1,0:T(8,128)S(1)}, f32[8,32,128]{2,1,0:T(8,128)S(1)}, u32[]{:S(2)}, u32[]{:S(2)}) collective-permute-start(f32[8,32,128]{2,1,0:T(8,128)S(1)} %get-tuple-element.39.moved_ref), channel_id=1, source_target_pairs={{4,0},{8,4},{12,8},{13,12},{1,5},{5,9},{9,13},{0,1},{6,2},{10,6},{... | collective-permute-start | bytes 393224 | tf_op jit(solution)/shard_map/ppermute | solution.py:127
  16.0 5.0 %collective-permute-start.9 = (f32[8,32,128]{2,1,0:T(8,128)S(1)}, f32[8,32,128]{2,1,0:T(8,128)S(1)}, u32[]{:S(2)}, u32[]{:S(2)}) collective-permute-start(f32[8,32,128]{2,1,0:T(8,128)S(1)} %get-tuple-element.39.moved_ref), channel_id=1, source_target_pairs={{0,4},{4,8},{8,12},{12,13},{5,1},{9,5},{13,9},{1,0},{2,6},{6,10},{... | collective-permute-start | bytes 393224 | tf_op jit(solution)/shard_map/ppermute | solution.py:127
  18.0 4.8 %collective-permute-start.2 = (f32[16,128]{1,0:T(8,128)S(1)}, f32[16,128]{1,0:T(8,128)S(1)}, u32[]{:S(2)}, u32[]{:S(2)}) collective-permute-start(f32[16,128]{1,0:T(8,128)S(1)} %shard_map.102.first_ref), channel_id=1, source_target_pairs={{0,8},{4,12},{8,0},{12,4},{1,9},{5,13},{9,1},{13,5},{2,10},{6,14},... | collective-permute-start | bytes 24584 | tf_op jit(solution)/shard_map/ppermute | solution.py:140
  21.1 5.0 %collective-permute-start.12 = (f32[8,32,128]{2,1,0:T(8,128)S(1)}, f32[8,32,128]{2,1,0:T(8,128)S(1)}, u32[]{:S(2)}, u32[]{:S(2)}) collective-permute-start(f32[8,32,128]{2,1,0:T(8,128)S(1)} %shard_map.110.pull_ref), channel_id=1, source_target_pairs={{2,0},{0,2},{3,1},{1,3},{6,4},{4,6},{7,5},{5,7},{10,8},{8,10},{11,... | collective-permute-start | bytes 393224 | tf_op jit(solution)/shard_map/ppermute | solution.py:130
  22.8 3.7 %collective-permute-start.11 = (f32[8,32,128]{2,1,0:T(8,128)S(1)}, f32[8,32,128]{2,1,0:T(8,128)S(1)}, u32[]{:S(2)}, u32[]{:S(2)}) collective-permute-start(f32[8,32,128]{2,1,0:T(8,128)S(1)} %shard_map.110.pull_ref), channel_id=1, source_target_pairs={{0,1},{1,0},{2,3},{3,2},{4,5},{5,4},{6,7},{7,6},{8,9},{9,8},{10,11... | collective-permute-start | bytes 393224 | tf_op jit(solution)/shard_map/ppermute | solution.py:133
  26.1 1.3 %collective-permute-start.13 = (f32[8,32,128]{2,1,0:T(8,128)S(1)}, f32[8,32,128]{2,1,0:T(8,128)S(1)}, u32[]{:S(2)}, u32[]{:S(2)}) collective-permute-start(f32[8,32,128]{2,1,0:T(8,128)S(1)} %collective-permute-done.12.refs_0_), channel_id=1, source_target_pairs={{0,1},{1,0},{2,3},{3,2},{4,5},{5,4},{6,7},{7,6},{8,9},{9,8},{10,11... | collective-permute-start | bytes 393224 | tf_op jit(solution)/shard_map/ppermute | solution.py:133
